TPU v7x, 32 devices: a whole 2x2x4 slice. The times are simulated.
32 devices in a mesh: ctx: 4 (over y, x), fsdp: 8 (over z, core).
Axes of the slice: x: 2, y: 2, z: 4, core: 2. Of those that a mesh axis runs over, the one named last changes fastest.
Arguments:
- tokens: bfloat16 [8, 768, 2048], P('fsdp', 'ctx'), may hold values from -16 to 16
- cotangent: bfloat16 [8, 768, 2048], P('fsdp', 'ctx'), may hold values from -6 to 6
- norm_attn: bfloat16 [2048], P('fsdp'), may hold values from 0.25 to 1.75
- w_qkv: bfloat16 [2048, 4096], P('fsdp'), may hold values from -0.1875 to 0.1875
- w_out: bfloat16 [2048, 2048], P('fsdp'), may hold values from -0.5 to 0.5
- norm_ffn: bfloat16 [2048], P('fsdp'), may hold values from 0.25 to 1.75
- w_gate: bfloat16 [8192, 2048], P('fsdp'), may hold values from -0.125 to 0.125
- w_up: bfloat16 [8192, 2048], P('fsdp'), may hold values from -0.125 to 0.125
- w_down: bfloat16 [8192, 2048], P('fsdp'), may hold values from -0.0625 to 0.0625
- seq_len: int32 [8], P('fsdp'), may hold values from 577 to 768, as said below
- window: int32 [8], P('fsdp'), may hold values from 256 to 512, as said below
- global_pos: int32 [8, 64], P('fsdp'), may hold values from 0 to 576, as said below
Outputs:
- layer_out: bfloat16 [8, 768, 2048], P('fsdp', 'ctx')
- d_tokens: float32 [8, 768, 2048], P('fsdp', 'ctx')
- d_norm_attn: float32 [2048], P('fsdp')
- d_w_qkv: float32 [2048, 4096], P('fsdp')
- d_w_out: float32 [2048, 2048], P('fsdp')
- d_norm_ffn: float32 [2048], P('fsdp')
- d_w_gate: float32 [8192, 2048], P('fsdp')
- d_w_up: float32 [8192, 2048], P('fsdp')
- d_w_down: float32 [8192, 2048], P('fsdp')
Inputs may be any that keep to these rules, and one draw needn't show every extreme that they name: `seq_len`: one entry is 768 and another 768 - 191. `window`: one entry is 512 and another half of 512, rounded down. `global_pos`: each row rises strictly, starts with 0 and ends with 576.
All inputs are finite; a program needn't handle non-finite values.
Results may differ from a plain program's by a relative error of at most 0.022.
Values may be sent and summed in bfloat16 or wider, within the bound.
No kernel may reach another device: no remote copies, remote signals or barrier semaphores. Data moves between devices by JAX's collectives and lax.ppermute only.
A program may use at most 832 MiB of HBM per device.

v0:
```python
import jax
import jax.numpy as jnp
from jax import lax
from jax.sharding import PartitionSpec as P

QUERY_HEADS = 16
KEY_VALUE_HEADS = 8
HEAD_WIDTH = 128


NORM_EPS = 1e-05
NEGATIVE_FILLER = -1e30
ROPE_BASE = 1000000.0


def passed_along(x, axis, by):
    devices = lax.axis_size(axis)
    pairs = [(i, i + by) for i in range(devices) if 0 <= i + by < devices]
    return lax.ppermute(x, axis, pairs)


def from_behind(x, axis, by):
    devices = lax.axis_size(axis)
    return lax.ppermute(x, axis, [(i, (i + by) % devices) for i in range(devices)])


def rope_tables(positions):
    half_width = HEAD_WIDTH // 2
    frequency = ROPE_BASE ** (-(2.0 * jnp.arange(half_width, dtype=jnp.float32)) / HEAD_WIDTH)
    angle_table = positions.astype(jnp.float32)[:, None] * frequency[None, :]
    return (jnp.cos(angle_table)[:, None, :], jnp.sin(angle_table)[:, None, :])


def apply_rotation(heads, cosine_lookup, sine_lookup):
    half_width = heads.shape[-1] // 2
    first_half = heads[..., :half_width]
    second_half = heads[..., half_width:]
    return jnp.concatenate(
        [
            first_half * cosine_lookup - second_half * sine_lookup,
            second_half * cosine_lookup + first_half * sine_lookup,
        ],
        axis=-1,
    )


def norm_back(d_normed, normed, inv_rms, gain):
    scaled = d_normed * gain[None, :]
    gain_grad = jnp.sum(d_normed * normed, axis=0)
    return (
        inv_rms * (scaled - normed * jnp.mean(scaled * normed, axis=-1, keepdims=True)),
        gain_grad,
    )


def silu_grads(d_hidden, gate, up_values):
    sigmoid_gate = jax.nn.sigmoid(gate)
    d_gate = d_hidden * up_values * sigmoid_gate * (1.0 + gate * (1.0 - sigmoid_gate))
    d_up = d_hidden * (gate * sigmoid_gate)
    return (d_gate.astype(jnp.bfloat16), d_up.astype(jnp.bfloat16))


def local(
    tokens,
    cotangent,
    norm_attn,
    w_qkv,
    w_out,
    norm_ffn,
    w_gate,
    w_up,
    w_down,
    seq_len,
    window,
    global_pos,
):
    context_length = lax.axis_size("ctx")
    context_place = lax.axis_index("ctx")
    count_of_rows = tokens.shape[1]
    group_count = QUERY_HEADS // KEY_VALUE_HEADS
    score_scale = HEAD_WIDTH ** (-0.5)
    length = seq_len[0]
    window_now = window[0]
    global_here = global_pos[0]
    inputs = tokens[0].astype(jnp.float32)
    cot_low = cotangent[0]
    cot_full = cot_low.astype(jnp.float32)
    gain_attn, gain_ffn, qkv_full, out_full = (
        lax.all_gather(norm_attn, "fsdp", axis=0, tiled=True),
        lax.all_gather(norm_ffn, "fsdp", axis=0, tiled=True),
        lax.all_gather(w_qkv, "fsdp", axis=0, tiled=True),
        lax.all_gather(w_out, "fsdp", axis=0, tiled=True),
    )
    gain_attn = gain_attn.astype(jnp.float32)
    gain_ffn = gain_ffn.astype(jnp.float32)
    inv_attn = lax.rsqrt(jnp.mean(inputs * inputs, axis=-1, keepdims=True) + NORM_EPS)
    normed_attn = inputs * inv_attn
    normed_low = (normed_attn * gain_attn[None, :]).astype(jnp.bfloat16)
    packed_projection = jnp.dot(normed_low, qkv_full, preferred_element_type=jnp.float32)
    positions = context_place * count_of_rows + jnp.arange(count_of_rows, dtype=jnp.int32)
    cosine_lookup, sine_lookup = rope_tables(positions)
    query_head_rows = apply_rotation(
        packed_projection[:, : QUERY_HEADS * HEAD_WIDTH].reshape(
            count_of_rows, QUERY_HEADS, HEAD_WIDTH
        ),
        cosine_lookup,
        sine_lookup,
    ).astype(jnp.bfloat16)
    key_head_rows = apply_rotation(
        packed_projection[
            :, QUERY_HEADS * HEAD_WIDTH : (QUERY_HEADS + KEY_VALUE_HEADS) * HEAD_WIDTH
        ].reshape(count_of_rows, KEY_VALUE_HEADS, HEAD_WIDTH),
        cosine_lookup,
        sine_lookup,
    ).astype(jnp.bfloat16)
    value_head_rows = (
        packed_projection[:, (QUERY_HEADS + KEY_VALUE_HEADS) * HEAD_WIDTH :]
        .reshape(count_of_rows, KEY_VALUE_HEADS, HEAD_WIDTH)
        .astype(jnp.bfloat16)
    )
    query_head_group = query_head_rows.reshape(
        count_of_rows, KEY_VALUE_HEADS, group_count, HEAD_WIDTH
    )
    row_global = jnp.any(positions[:, None] == global_here[None, :], axis=1)

    def allowed_for(source):
        key_pos = source * count_of_rows + jnp.arange(count_of_rows, dtype=jnp.int32)
        key_global = jnp.any(key_pos[:, None] == global_here[None, :], axis=1)
        in_window = positions[:, None] - key_pos[None, :] < window_now
        return (
            (key_pos[None, :] <= positions[:, None])
            & (key_pos[None, :] < length)
            & (in_window | row_global[:, None] | key_global[None, :])
        )

    def scores_for(key_block, allowed):
        raw_scores = (
            jnp.einsum(
                "igkd,jgd->gkij", query_head_group, key_block, preferred_element_type=jnp.float32
            )
            * score_scale
        )
        return jnp.where(allowed[None, None], raw_scores, NEGATIVE_FILLER)

    def absorb(
        step_index, key_block, value_block, kept_keys, kept_values, running_top, running_sum
    ):
        source = (context_place - step_index) % context_length
        allowed = allowed_for(source)
        scores = scores_for(key_block, allowed)
        new_top = jnp.maximum(running_top, jnp.max(scores, axis=-1))
        block_sum = jnp.sum(
            jnp.where(allowed[None, None], jnp.exp(scores - new_top[..., None]), 0.0), axis=-1
        )
        running_sum = running_sum * jnp.exp(running_top - new_top) + block_sum
        kept_keys = lax.dynamic_update_index_in_dim(kept_keys, key_block, source, 0)
        kept_values = lax.dynamic_update_index_in_dim(kept_values, value_block, source, 0)
        return (kept_keys, kept_values, new_top, running_sum)

    def forward_turn(step_index, turn_state):
        key_block, value_block, kept_keys, kept_values, running_top, running_sum = turn_state
        kept_keys, kept_values, running_top, running_sum = absorb(
            step_index, key_block, value_block, kept_keys, kept_values, running_top, running_sum
        )
        key_block, value_block = passed_along((key_block, value_block), "ctx", 1)
        return (key_block, value_block, kept_keys, kept_values, running_top, running_sum)

    blank_blocks = jnp.zeros(
        (context_length, count_of_rows, KEY_VALUE_HEADS, HEAD_WIDTH), jnp.bfloat16
    )
    initial_maximum = jnp.full(
        (KEY_VALUE_HEADS, group_count, count_of_rows), NEGATIVE_FILLER, jnp.float32
    )
    initial_sum = jnp.zeros((KEY_VALUE_HEADS, group_count, count_of_rows), jnp.float32)
    turn_state = lax.fori_loop(
        0,
        context_length - 1,
        forward_turn,
        (key_head_rows, value_head_rows, blank_blocks, blank_blocks, initial_maximum, initial_sum),
    )
    kept_keys, kept_values, running_top, running_sum = absorb(
        context_length - 1,
        turn_state[0],
        turn_state[1],
        turn_state[2],
        turn_state[3],
        turn_state[4],
        turn_state[5],
    )
    log_total = running_top + jnp.log(running_sum)

    def weight_one_block(source, attended_sum):
        key_block = lax.dynamic_index_in_dim(kept_keys, source, 0, keepdims=False)
        value_block = lax.dynamic_index_in_dim(kept_values, source, 0, keepdims=False)
        allowed = allowed_for(source)
        scores = scores_for(key_block, allowed)
        probs_low = jnp.where(
            allowed[None, None], jnp.exp(scores - log_total[..., None]), 0.0
        ).astype(jnp.bfloat16)
        return attended_sum + jnp.einsum(
            "gkij,jgd->igkd", probs_low, value_block, preferred_element_type=jnp.float32
        )

    attended_output = lax.fori_loop(
        0,
        context_length,
        weight_one_block,
        jnp.zeros((count_of_rows, KEY_VALUE_HEADS, group_count, HEAD_WIDTH), jnp.float32),
    )
    attended_output = attended_output.reshape(count_of_rows, QUERY_HEADS * HEAD_WIDTH)
    attended_low = attended_output.astype(jnp.bfloat16)
    branch = jnp.dot(attended_low, out_full, preferred_element_type=jnp.float32)
    middle = inputs + branch
    inv_ffn = lax.rsqrt(jnp.mean(middle * middle, axis=-1, keepdims=True) + NORM_EPS)
    normed_ffn = middle * inv_ffn
    ffn_low = (normed_ffn * gain_ffn[None, :]).astype(jnp.bfloat16)
    gate_stack = jnp.stack([w_gate, w_up])
    gate_and_up = jnp.einsum(
        "td,sfd->stf",
        ffn_low,
        lax.all_gather(gate_stack, "fsdp", axis=1, tiled=True),
        preferred_element_type=jnp.float32,
    )
    gate = gate_and_up[0]
    up_values = gate_and_up[1]
    hidden = (gate * jax.nn.sigmoid(gate) * up_values).astype(jnp.bfloat16)
    hidden_part = hidden
    ffn_out = jnp.dot(
        hidden_part,
        lax.all_gather(w_down, "fsdp", axis=0, tiled=True),
        preferred_element_type=jnp.float32,
    )
    layer_value = middle + ffn_out
    d_hidden = jnp.einsum(
        "td,fd->tf",
        cot_low,
        lax.all_gather(w_down, "fsdp", axis=0, tiled=True),
        preferred_element_type=jnp.float32,
    )
    d_gate, d_up = silu_grads(d_hidden, gate, up_values)
    gate_part = d_gate
    up_part = d_up
    partial_sum = jnp.dot(
        gate_part,
        lax.all_gather(w_gate, "fsdp", axis=0, tiled=True),
        preferred_element_type=jnp.float32,
    )
    d_ffn_low = partial_sum + jnp.dot(
        up_part,
        lax.all_gather(w_up, "fsdp", axis=0, tiled=True),
        preferred_element_type=jnp.float32,
    )
    gate_part = d_gate
    up_part = d_up
    hidden_part = hidden
    ffn_shards = lax.psum_scatter(
        jnp.stack(
            [
                jnp.einsum("tf,td->fd", gate_part, ffn_low, preferred_element_type=jnp.float32),
                jnp.einsum("tf,td->fd", up_part, ffn_low, preferred_element_type=jnp.float32),
                jnp.einsum("tf,td->fd", hidden_part, cot_low, preferred_element_type=jnp.float32),
            ],
            axis=1,
        ).astype(jnp.bfloat16),
        "fsdp",
        scatter_dimension=0,
        tiled=True,
    ).astype(jnp.float32)
    grad_gate = ffn_shards[:, 0]
    grad_up = ffn_shards[:, 1]
    grad_down = ffn_shards[:, 2]
    d_normed_ffn, grad_gain_ffn = norm_back(d_ffn_low, normed_ffn, inv_ffn, gain_ffn)
    d_middle = cot_full + d_normed_ffn
    d_branch = d_middle.astype(jnp.bfloat16)
    attended_gradient = jnp.einsum(
        "te,fe->tf", d_branch, out_full, preferred_element_type=jnp.float32
    ).astype(jnp.bfloat16)
    grouped_attention_grad = attended_gradient.reshape(
        count_of_rows, KEY_VALUE_HEADS, group_count, HEAD_WIDTH
    )
    row_delta = jnp.sum(
        grouped_attention_grad.astype(jnp.float32)
        * attended_output.reshape(count_of_rows, KEY_VALUE_HEADS, group_count, HEAD_WIDTH),
        axis=-1,
    )
    row_delta = jnp.transpose(row_delta, (1, 2, 0))

    def backward_turn(step_index, back_state):
        d_queries, key_grad, value_gradient = back_state
        source = (context_place - step_index) % context_length
        key_block = lax.dynamic_index_in_dim(kept_keys, source, 0, keepdims=False)
        value_block = lax.dynamic_index_in_dim(kept_values, source, 0, keepdims=False)
        allowed = allowed_for(source)
        scores = scores_for(key_block, allowed)
        probs = jnp.where(allowed[None, None], jnp.exp(scores - log_total[..., None]), 0.0)
        probs_low = probs.astype(jnp.bfloat16)
        d_probs = jnp.einsum(
            "igkd,jgd->gkij",
            grouped_attention_grad,
            value_block,
            preferred_element_type=jnp.float32,
        )
        d_scores = (probs * (d_probs - row_delta[..., None])).astype(jnp.bfloat16)
        d_queries = d_queries + score_scale * jnp.einsum(
            "gkij,jgd->igkd", d_scores, key_block, preferred_element_type=jnp.float32
        )
        key_grad = key_grad + score_scale * jnp.einsum(
            "gkij,igkd->jgd", d_scores, query_head_group, preferred_element_type=jnp.float32
        )
        value_gradient = value_gradient + jnp.einsum(
            "gkij,igkd->jgd", probs_low, grouped_attention_grad, preferred_element_type=jnp.float32
        )
        key_grad, value_gradient = (
            from_behind(key_grad.astype(jnp.bfloat16), "ctx", 1).astype(key_grad.dtype),
            from_behind(value_gradient.astype(jnp.bfloat16), "ctx", 1).astype(value_gradient.dtype),
        )
        return (d_queries, key_grad, value_gradient)

    zeroed_heads = jnp.zeros((count_of_rows, KEY_VALUE_HEADS, HEAD_WIDTH), jnp.float32)
    d_queries, key_grad, value_gradient = lax.fori_loop(
        0,
        context_length,
        backward_turn,
        (
            jnp.zeros((count_of_rows, KEY_VALUE_HEADS, group_count, HEAD_WIDTH), jnp.float32),
            zeroed_heads,
            zeroed_heads,
        ),
    )
    d_query_turned = apply_rotation(
        d_queries.reshape(count_of_rows, QUERY_HEADS, HEAD_WIDTH), cosine_lookup, -sine_lookup
    )
    rotated_key_gradient = apply_rotation(key_grad, cosine_lookup, -sine_lookup)
    d_packed = jnp.concatenate(
        [
            d_query_turned.reshape(count_of_rows, QUERY_HEADS * HEAD_WIDTH),
            rotated_key_gradient.reshape(count_of_rows, KEY_VALUE_HEADS * HEAD_WIDTH),
            value_gradient.reshape(count_of_rows, KEY_VALUE_HEADS * HEAD_WIDTH),
        ],
        axis=-1,
    ).astype(jnp.bfloat16)
    d_attn_low = jnp.einsum("tc,dc->td", d_packed, qkv_full, preferred_element_type=jnp.float32)
    d_normed_attn, grad_gain_attn = norm_back(d_attn_low, normed_attn, inv_attn, gain_attn)
    d_inputs = d_middle + d_normed_attn
    grad_qkv = jnp.einsum("td,tc->dc", normed_low, d_packed, preferred_element_type=jnp.float32)
    grad_out = jnp.einsum("tf,te->fe", attended_low, d_branch, preferred_element_type=jnp.float32)
    shard_gain_attn, shard_gain_ffn, shard_qkv, shard_out = (
        lax.psum_scatter(
            grad_gain_attn.astype(jnp.bfloat16), "fsdp", scatter_dimension=0, tiled=True
        ).astype(jnp.float32),
        lax.psum_scatter(
            grad_gain_ffn.astype(jnp.bfloat16), "fsdp", scatter_dimension=0, tiled=True
        ).astype(jnp.float32),
        lax.psum_scatter(
            grad_qkv.astype(jnp.bfloat16), "fsdp", scatter_dimension=0, tiled=True
        ).astype(jnp.float32),
        lax.psum_scatter(
            grad_out.astype(jnp.bfloat16), "fsdp", scatter_dimension=0, tiled=True
        ).astype(jnp.float32),
    )
    summed = (
        lax.psum(shard_gain_attn.astype(jnp.bfloat16), "ctx").astype(jnp.float32),
        lax.psum(shard_qkv.astype(jnp.bfloat16), "ctx").astype(jnp.float32),
        lax.psum(shard_out.astype(jnp.bfloat16), "ctx").astype(jnp.float32),
        lax.psum(shard_gain_ffn.astype(jnp.bfloat16), "ctx").astype(jnp.float32),
        lax.psum(grad_gate.astype(jnp.bfloat16), "ctx").astype(jnp.float32),
        lax.psum(grad_up.astype(jnp.bfloat16), "ctx").astype(jnp.float32),
        lax.psum(grad_down.astype(jnp.bfloat16), "ctx").astype(jnp.float32),
    )
    return (
        layer_value.astype(jnp.bfloat16)[None],
        d_inputs[None],
        summed[0],
        summed[1],
        summed[2],
        summed[3],
        summed[4],
        summed[5],
        summed[6],
    )


def solution(mesh):
    return jax.shard_map(
        local,
        mesh=mesh,
        in_specs=(
            P("fsdp", "ctx", None),
            P("fsdp", "ctx", None),
            P("fsdp"),
            P("fsdp", None),
            P("fsdp", None),
            P("fsdp"),
            P("fsdp", None),
            P("fsdp", None),
            P("fsdp", None),
            P("fsdp"),
            P("fsdp"),
            P("fsdp", None),
        ),
        out_specs=(
            P("fsdp", "ctx", None),
            P("fsdp", "ctx", None),
            P("fsdp"),
            P("fsdp", None),
            P("fsdp", None),
            P("fsdp"),
            P("fsdp", None),
            P("fsdp", None),
            P("fsdp", None),
        ),
        check_vma=False,
    )
```

profile of v0, /device:TPU:0, one launch (start us, length us, event | category | flops | bytes accessed | tf_op | source)
XLA Modules:
  0.0 3214.4 jit_solution(1502499297186942144)
XLA Ops:
  8.7 7.6 pad_maximum_fusion.1
  18.3 13.6 all-gather
  33.2 8.8 all-gather.1
  43.7 119.8 %all-gather.9.cloned.1.call-done = bf16[2048,4096]{1,0:T(8,128)(2,1)} async-done(((bf16[256,4096]{1,0:T(8,128)(2,1)}), bf16[2048,4096]{1,0:T(8,128)(2,1)}) %all-gather.9.cloned.1.call-update) | async-done | bytes 16777232 | tf_op jit(solution)/shard_map/all_gather | solution.py:91
  163.5 7.6 fusion.113
  177.3 61.6 %while.60 = (s32[]{:T(128)}, bf16[192,8,128]{2,0,1:T(8,128)(2,1)S(1)}, bf16[192,8,128]{2,1,0:T(8,128)(2,1)S(1)}, bf16[4,192,8,128]{3,1,2,0:T(8,128)(2,1)}, bf16[...) while((s32[]{:T(128)}, ...), condition=%wide.region_6.7_spmd.clone, body=%wide.region_2.6_spmd.clone.sunk | while | flops 156012112 | bytes 12465543 | solution.py:175
  190.2 7.8 collective-permute-done.1
  242.7 24.4 while.61
  278.6 531.6 %all-gather.13.cloned.1.call-done = bf16[2,8192,2048]{2,1,0:T(8,128)(2,1)} async-done(((bf16[2,1024,2048]{2,1,0:T(8,128)(2,1)}), bf16[2,8192,2048]{2,1,0:T(8,128)(2,1)}) %all-gather.13.cloned.1.call-update) | async-done | bytes 67108880 | tf_op jit(solution)/shard_map/all_gather | solution.py:221
  810.2 36.8 %convolution_bitcast_fusion.1 = f32[2,192,8192]{2,1,0:T(8,128)} fusion(bf16[2,8192,2048]{2,1,0:T(8,128)(2,1)} %all-gather.13.cloned.1.call-done, bf16[192,2048]{1,0:T(8,128)(2,1)S(1)} %multiply_convert_fusion.3), kind=kOutput, calls=%fused_computation.89 | convolution fusion | flops 12884901888 | bytes 80478208 | tf_op jit(solution)/shard_map/td,sfd->stf/dot_general | solution.py:218
  847.0 251.5 %all-gather.15.cloned.1.call-done = bf16[8192,2048]{1,0:T(8,128)(2,1)} async-done(((bf16[1024,2048]{1,0:T(8,128)(2,1)}), bf16[8192,2048]{1,0:T(8,128)(2,1)}) %all-gather.15.cloned.1.call-update) | async-done | bytes 33554448 | tf_op jit(solution)/shard_map/all_gather | solution.py:230
  1098.5 26.2 multiply_convert_fusion.1
  1124.7 16.7 convert_bitcast_fusion.1
  1141.4 14.0 convert_bitcast_fusion.2
  1155.4 18.8 convert_bitcast_fusion
  1174.3 68.1 %pad_maximum_fusion = bf16[8192,3,2048]{2,0,1:T(8,128)(2,1)} fusion(bf16[8192,1,2048]{2,0,1:T(8,128)(2,1)} %convert_bitcast_fusion, bf16[8192,1,2048]{2,0,1:T(8,128)(2,1)} %convert_bitcast_fusion.1, bf16[8192,1,2048]{2,0,1:T(8,128)(2,1)} %convert_bitcast_fusion.2), kind=kLoop, calls=%fused_computation.84 | loop fusion | flops 100663296 | bytes 201326592 | tf_op jit(solution)/shard_map/stack | solution.py:257
  1242.5 144.3 %all-gather.17.cloned.1.call-done = bf16[8192,2048]{1,0:T(8,128)(2,1)} async-done(((bf16[1024,2048]{1,0:T(8,128)(2,1)}), bf16[8192,2048]{1,0:T(8,128)(2,1)}) %all-gather.17.cloned.1.call-update) | async-done | bytes 33554448 | tf_op jit(solution)/shard_map/all_gather | solution.py:245
  1386.8 19.2 fusion.124
  1406.0 269.1 %all-gather.19.cloned.1.call-done = bf16[8192,2048]{1,0:T(8,128)(2,1)} async-done(((bf16[1024,2048]{1,0:T(8,128)(2,1)}), bf16[8192,2048]{1,0:T(8,128)(2,1)}) %all-gather.19.cloned.1.call-update) | async-done | bytes 33554448 | tf_op jit(solution)/shard_map/all_gather | solution.py:250
  1675.1 16.7 multiply_reduce_fusion
  1709.7 113.1 %while.62 = (s32[]{:T(128)}, f32[192,8,2,128]{3,0,2,1:T(8,128)}, f32[192,8,128]{2,0,1:T(8,128)S(1)}, f32[192,8,128]{2,0,1:T(8,128)}, s32[]{:T(128)}, /*index=5*/...) while((s32[]{:T(128)}, f32[192,8,2,128]{3,0,2,1:T(8,128)}, ...), condition=%wide.region_18.19_spmd.clone, body=%wide.region_16.18_spmd.clone.sunk | while | flops 765284928 | bytes 32404952 | solution.py:320
  1729.9 7.7 collective-permute-done.3
  1829.1 8.3 convolution_convert_fusion
  1837.4 793.3 %reduce-scatter.8.cloned.1.call-done = bf16[1024,3,2048]{2,0,1:T(8,128)(2,1)} async-done(((bf16[8192,3,2048]{2,0,1:T(8,128)(2,1)}), bf16[1024,3,2048]{2,0,1:T(8,128)(2,1)}) %reduce-scatter.8.cloned.1.call-update) | async-done | bytes 12582928 | tf_op jit(solution)/shard_map/reduce_scatter | solution.py:256
  2630.7 9.2 slice_bitcast_fusion
  2639.9 81.8 %reduce-scatter.6.cloned.1.call-done = bf16[256,2048]{1,0:T(8,128)(2,1)} async-done(((bf16[2048,2048]{1,0:T(8,128)(2,1)}), bf16[256,2048]{1,0:T(8,128)(2,1)}) %reduce-scatter.6.cloned.1.call-update) | async-done | bytes 1048592 | tf_op jit(solution)/shard_map/reduce_scatter | solution.py:357
  2721.7 169.1 %reduce-scatter.4.cloned.1.call-done = bf16[256,4096]{1,0:T(8,128)(2,1)} async-done(((bf16[2048,4096]{1,0:T(8,128)(2,1)}), bf16[256,4096]{1,0:T(8,128)(2,1)}) %reduce-scatter.4.cloned.1.call-update) | async-done | bytes 2097168 | tf_op jit(solution)/shard_map/reduce_scatter | solution.py:354
  2892.7 13.2 fusion.101
  2905.9 13.9 all-reduce.2
  2920.0 10.2 all-reduce.3
  2934.3 23.8 fusion.88
  2958.1 230.2 %all-reduce.7.cloned.1.call-done = (bf16[256,4096]{1,0:T(8,128)(2,1)}, bf16[256,2048]{1,0:T(8,128)(2,1)}, bf16[1024,2048]{1,0:T(8,128)(2,1)}, bf16[1024,2048]{1,0:T(8,128)(2,1)}, bf16[1024,2048]{1,0:T(8,128)(2,1)}) async-done(((bf16[256,4096]{1,0:T(8,128)(2,1)}, bf16[256,2048]{1,0:T(8,128)(2,1)}, bf16[1024,2048]{1,0:T(8,128)(2,1)}, bf16[1024,2048]{1,0:T(8,128)(2,1)}, bf16[1024,2048]{1,0:T(8,128)(2,1)}), ...) | async-done | bytes 15728656 | tf_op jit(solution)/shard_map/psum | solution.py:363
  (314 shorter events, 257.2 us)
Async XLA Ops:
  7.2 156.4 %all-gather.9.cloned.1.call-start = ((), (), s32[]{:S(2)}) async-start(), calls=%async_computation.3 | async-start | bytes 18874368 | tf_op jit(solution)/shard_map/all_gather | solution.py:91
  7.9 262.9 %all-gather.11.cloned.1.call-start = ((), (), s32[]{:S(2)}) async-start(), calls=%async_computation.4 | async-start | bytes 9437184 | tf_op jit(solution)/shard_map/all_gather | solution.py:92
  8.7 801.5 %all-gather.13.cloned.1.call-start = ((), (), s32[]{:S(2)}) async-start(), calls=%async_computation.5 | async-start | bytes 75497472 | tf_op jit(solution)/shard_map/all_gather | solution.py:221
  16.4 1082.1 %all-gather.15.cloned.1.call-start = ((), (), s32[]{:S(2)}) async-start(), calls=%async_computation.6 | async-start | bytes 37748736 | tf_op jit(solution)/shard_map/all_gather | solution.py:230
  16.9 1369.9 %all-gather.17.cloned.1.call-start = ((), (), s32[]{:S(2)}) async-start(), calls=%async_computation.7 | async-start | bytes 37748736 | tf_op jit(solution)/shard_map/all_gather | solution.py:245
  17.6 1657.5 %all-gather.19.cloned.1.call-start = ((), (), s32[]{:S(2)}) async-start(), calls=%async_computation.8 | async-start | bytes 37748736 | tf_op jit(solution)/shard_map/all_gather | solution.py:250
  18.2 2612.5 %reduce-scatter.8.cloned.1.call-start = ((), (), s32[]{:S(2)}) async-start(), calls=%async_computation.11 | async-start | bytes 113246208 | tf_op jit(solution)/shard_map/reduce_scatter | solution.py:256
  31.9 139.3 %copy-start.26 = (f32[8,1,256]{2,1,0:T(1,128)}, f32[8,1,256]{2,1,0:T(1,128)S(1)}, u32[]{:S(2)}) copy-start(f32[8,1,256]{2,1,0:T(1,128)S(1)} %convert_element_type.225) | copy-start | bytes 24580
  42.0 235.2 %copy-start.31 = (f32[8,1,256]{2,1,0:T(1,128)}, f32[8,1,256]{2,1,0:T(1,128)S(1)}, u32[]{:S(2)}) copy-start(f32[8,1,256]{2,1,0:T(1,128)S(1)} %convert_element_type.226) | copy-start | bytes 24580
  42.5 128.7 %copy-start.33 = (f32[192]{0:T(256)}, f32[192]{0:T(256)S(1)}, u32[]{:S(2)}) copy-start(f32[192]{0:T(256)S(1)} %add_rsqrt_fusion.1) | copy-start | bytes 2308
  43.7 129.6 %copy-start.16 = (f32[192,64]{1,0:T(8,128)}, f32[192,64]{1,0:T(8,128)S(1)}, u32[]{:S(2)}) copy-start(f32[192,64]{1,0:T(8,128)S(1)} %get-tuple-element.1323) | copy-start | bytes 147460
  177.4 12.8 collective-permute-start
  180.8 17.1 collective-permute-start.1
  198.0 13.9 collective-permute-start
  202.4 16.4 collective-permute-start.1
  218.9 13.9 collective-permute-start
  223.4 15.6 collective-permute-start.1
  278.6 819.9 %copy-start.20 = (bf16[1,192,2048]{2,1,0:T(8,128)(2,1)S(1)}, bf16[1,192,2048]{2,1,0:T(8,128)(2,1)}, u32[]{:S(2)}) copy-start(bf16[1,192,2048]{2,1,0:T(8,128)(2,1)} %param.19) | copy-start | bytes 2359300
  1242.4 432.7 %copy-start.7 = (f32[192,2048]{1,0:T(8,128)S(1)}, f32[192,2048]{1,0:T(8,128)}, u32[]{:S(2)}) copy-start(f32[192,2048]{1,0:T(8,128)} %copy-done.6) | copy-start | bytes 4718596
  1242.4 432.7 %copy-start.32 = (f32[8,1,256]{2,1,0:T(1,128)S(1)}, f32[8,1,256]{2,1,0:T(1,128)}, u32[]{:S(2)}) copy-start(f32[8,1,256]{2,1,0:T(1,128)} %copy-done.31) | copy-start | bytes 24580
  1242.4 432.7 %copy-start.36 = (f32[192]{0:T(256)S(1)}, f32[192]{0:T(256)}, u32[]{:S(2)}) copy-start(f32[192]{0:T(256)} %copy-done.35) | copy-start | bytes 2308
  1242.4 1479.2 %reduce-scatter.6.cloned.1.call-start = ((), (), s32[]{:S(2)}) async-start(), calls=%async_computation.10 | async-start | bytes 9437184 | tf_op jit(solution)/shard_map/reduce_scatter | solution.py:357
  1698.8 1192.0 %reduce-scatter.4.cloned.1.call-start = ((), (), s32[]{:S(2)}) async-start(), calls=%async_computation.9 | async-start | bytes 18874368 | tf_op jit(solution)/shard_map/reduce_scatter | solution.py:354
  1716.8 13.1 collective-permute-start.2
  1720.8 16.8 collective-permute-start.3
  1746.2 13.2 collective-permute-start.2
  1749.4 16.8 collective-permute-start.3
  1774.9 13.2 collective-permute-start.2
  1777.5 16.5 collective-permute-start.3
  1802.6 13.2 collective-permute-start.2
  1805.2 15.6 collective-permute-start.3
  1837.4 1350.9 %all-reduce.7.cloned.1.call-start = ((), (), s32[]{:S(2)}) async-start(), calls=%async_computation.12 | async-start | bytes 31457280 | tf_op jit(solution)/shard_map/psum | solution.py:363
  (38 other events, 252.3 us)
Sparse Core Ops, SparseCore 0:
  9.6 153.8 all-gather.8
  165.1 80.2 all-gather.10
  247.6 562.5 all-gather.12
  811.6 286.8 all-gather.14
  1099.9 286.8 all-gather.16
  1388.2 286.8 all-gather.18
  1677.5 953.1 reduce-scatter.7
  2633.7 87.9 reduce-scatter.5
  2724.2 166.6 reduce-scatter.3
  2896.1 292.0 all-reduce.6
where the time goes:
time: 3230 us; the launch traced here: 3210 us
  waiting for transfers between devices  2660 us (82%)
  matrix products  284 us (9%)
  other arithmetic  140 us (4%)
  blocking collectives  46.5 us (1%)
  starting transfers between devices  37.3 us (1%)
    reduce_scatter x1, waiting for transfers between devices, local(): lax.psum_scatter(jnp.stack([jnp.einsum('tf,td->fd', gate_part, ffn_low, p...  793 us
    all_gather x1, waiting for transfers between devices, local(): lax.all_gather(gate_stack, 'fsdp', axis=1, tiled=True)  532 us
    all_gather x1, waiting for transfers between devices, local(): lax.all_gather(w_up, 'fsdp', axis=0, tiled=True)  269 us
    all_gather x1, waiting for transfers between devices, local(): lax.all_gather(w_down, 'fsdp', axis=0, tiled=True)  252 us
    psum x1, waiting for transfers between devices, local(): lax.psum(shard_qkv.astype(jnp.bfloat16), 'ctx').astype(jnp.float32)  230 us
    reduce_scatter x1, waiting for transfers between devices, local(): lax.psum_scatter(grad_qkv.astype(jnp.bfloat16), 'fsdp', scatter_dimension...  169 us
    all_gather x1, waiting for transfers between devices, local(): lax.all_gather(w_gate, 'fsdp', axis=0, tiled=True)  144 us
    all_gather x1, waiting for transfers between devices, local(): lax.all_gather(w_qkv, 'fsdp', axis=0, tiled=True)  120 us
  transfers between devices with their start and end apart: 24, of which 23 were waited for; matrix products, arithmetic and copies ran while one was open for 13% of the time, Pallas kernels for 0%

commit v1 on v0

v1 whole, which is shorter than its diff:
```python
import jax
import jax.numpy as jnp
from jax import lax
from jax.sharding import PartitionSpec as P

QUERY_HEADS = 16
KEY_VALUE_HEADS = 8
HEAD_WIDTH = 128
GROUP = QUERY_HEADS // KEY_VALUE_HEADS

NORM_EPS = 1e-05
NEGATIVE_FILLER = -1e30
ROPE_BASE = 1000000.0
BF16 = jnp.bfloat16
F32 = jnp.float32


def rope_tables(positions):
    half_width = HEAD_WIDTH // 2
    frequency = ROPE_BASE ** (-(2.0 * jnp.arange(half_width, dtype=F32)) / HEAD_WIDTH)
    angle_table = positions.astype(F32)[:, None] * frequency[None, :]
    return (jnp.cos(angle_table)[:, None, :], jnp.sin(angle_table)[:, None, :])


def apply_rotation(heads, cosine_lookup, sine_lookup):
    half_width = heads.shape[-1] // 2
    first_half = heads[..., :half_width]
    second_half = heads[..., half_width:]
    return jnp.concatenate(
        [
            first_half * cosine_lookup - second_half * sine_lookup,
            second_half * cosine_lookup + first_half * sine_lookup,
        ],
        axis=-1,
    )


def square():
    return lax.axis_size("ctx") == 4


def swap(x, bit):
    return lax.ppermute(x, "ctx", [(i, i ^ bit) for i in range(4)])


def block_order():
    if square():
        return lax.axis_index("ctx") ^ jnp.arange(4, dtype=jnp.int32)
    return jnp.arange(lax.axis_size("ctx"), dtype=jnp.int32)


def gather_ctx(x):
    if not square():
        return lax.all_gather(x, "ctx", axis=0)
    half = x.shape[-1] // 2
    first, second = x[..., :half], x[..., half:]
    first_1 = swap(first, 1)
    second_2 = swap(second, 2)
    first_23 = swap(jnp.stack([first, first_1]), 2)
    second_13 = swap(jnp.stack([second, second_2]), 1)
    return jnp.stack(
        [
            x,
            jnp.concatenate([first_1, second_13[0]], axis=-1),
            jnp.concatenate([first_23[0], second_2], axis=-1),
            jnp.concatenate([first_23[1], second_13[1]], axis=-1),
        ]
    )


def scatter_sum_ctx(x):
    if not square():
        return lax.psum_scatter(x, "ctx", scatter_dimension=0, tiled=False).astype(F32)
    half = x.shape[-1] // 2
    first, second = x[..., :half], x[..., half:]
    got_first = swap(jnp.stack([first[1], first[3]]), 1)
    got_second = swap(second[2:4], 2)
    first_2 = (first[2].astype(F32) + got_first[1].astype(F32)).astype(BF16)
    second_1 = (second[1].astype(F32) + got_second[1].astype(F32)).astype(BF16)
    last_first = swap(first_2, 2)
    last_second = swap(second_1, 1)
    return jnp.concatenate(
        [
            first[0].astype(F32) + got_first[0].astype(F32) + last_first.astype(F32),
            second[0].astype(F32) + got_second[0].astype(F32) + last_second.astype(F32),
        ],
        axis=-1,
    )


def absolute_order(blocks):
    if not square():
        return [blocks[i] for i in range(lax.axis_size("ctx"))]
    place = lax.axis_index("ctx")
    low, high = (place & 1) == 1, (place & 2) == 2
    a = [jnp.where(low, blocks[r ^ 1], blocks[r]) for r in range(4)]
    return [jnp.where(high, a[r ^ 2], a[r]) for r in range(4)]


def own_row_order(blocks):
    if not square():
        return blocks
    return [jnp.stack([blocks[s][r ^ s] for r in range(4)]) for s in range(4)]


def exchange_ctx(x):
    if not square():
        got = lax.all_to_all(x, "ctx", 0, 0, tiled=False)
        return [got[i] for i in range(lax.axis_size("ctx"))]
    order = block_order()
    parts = [lax.dynamic_index_in_dim(x, order[r], 0, keepdims=False) for r in range(4)]
    got = [parts[0]] + [swap(parts[r], r) for r in range(1, 4)]
    return absolute_order(got)


def local(
    tokens,
    cotangent,
    norm_attn,
    w_qkv,
    w_out,
    norm_ffn,
    w_gate,
    w_up,
    w_down,
    seq_len,
    window,
    global_pos,
):
    places = lax.axis_size("ctx")
    place = lax.axis_index("ctx")
    shards = lax.axis_size("fsdp")
    rows = tokens.shape[1]
    width = tokens.shape[2]
    count = places * rows
    kv_heads = KEY_VALUE_HEADS // places
    q_heads = kv_heads * GROUP
    q_cols = q_heads * HEAD_WIDTH
    kv_cols = kv_heads * HEAD_WIDTH
    q_all = QUERY_HEADS * HEAD_WIDTH
    kv_all = KEY_VALUE_HEADS * HEAD_WIDTH
    out_cols = width // places
    score_scale = HEAD_WIDTH ** (-0.5)
    length = seq_len[0]
    window_now = window[0]
    global_here = global_pos[0]
    x_own = tokens[0]
    cot_own = cotangent[0]

    qkv_mine = jnp.concatenate(
        [
            lax.dynamic_slice_in_dim(w_qkv, place * q_cols, q_cols, 1),
            lax.dynamic_slice_in_dim(w_qkv, q_all + place * kv_cols, kv_cols, 1),
            lax.dynamic_slice_in_dim(w_qkv, q_all + kv_all + place * kv_cols, kv_cols, 1),
        ],
        axis=1,
    )
    w_heads = lax.all_gather(qkv_mine, "fsdp", axis=0, tiled=True)
    gains = lax.all_gather(jnp.stack([norm_attn, norm_ffn]), "fsdp", axis=1, tiled=True)
    gain_attn = gains[0].astype(F32)
    gain_ffn = gains[1].astype(F32)
    x_seq = gather_ctx(x_own).reshape(count, width).astype(F32)
    out_mine = lax.dynamic_slice_in_dim(w_out, place * out_cols, out_cols, 1)
    out_gathered = lax.all_gather(out_mine, "fsdp", axis=0, tiled=True)
    w_rows = jnp.concatenate(
        exchange_ctx(out_gathered.reshape(places, q_cols, out_cols)), axis=1
    )
    cot_all = lax.all_gather(cot_own, "fsdp", axis=0, tiled=True)

    inv_attn = lax.rsqrt(jnp.mean(x_seq * x_seq, axis=-1, keepdims=True) + NORM_EPS)
    normed_low = (x_seq * inv_attn * gain_attn[None, :]).astype(BF16)
    packed = jnp.dot(normed_low, w_heads, preferred_element_type=F32)
    order = block_order()
    positions = (order[:, None] * rows + jnp.arange(rows, dtype=jnp.int32)[None, :]).reshape(count)
    cosine, sine = rope_tables(positions)
    queries = apply_rotation(
        packed[:, :q_cols].reshape(count, q_heads, HEAD_WIDTH), cosine, sine
    ).astype(BF16)
    queries = queries.reshape(count, kv_heads, GROUP, HEAD_WIDTH)
    keys = apply_rotation(
        packed[:, q_cols : q_cols + kv_cols].reshape(count, kv_heads, HEAD_WIDTH), cosine, sine
    ).astype(BF16)
    values = packed[:, q_cols + kv_cols :].reshape(count, kv_heads, HEAD_WIDTH).astype(BF16)
    is_global = jnp.any(positions[:, None] == global_here[None, :], axis=1)
    allowed = (
        (positions[None, :] <= positions[:, None])
        & (positions[None, :] < length)
        & (
            (positions[:, None] - positions[None, :] < window_now)
            | is_global[:, None]
            | is_global[None, :]
        )
    )
    scores = (
        jnp.einsum("igkd,jgd->gkij", queries, keys, preferred_element_type=F32) * score_scale
    )
    scores = jnp.where(allowed[None, None], scores, NEGATIVE_FILLER)
    top = jnp.max(scores, axis=-1, keepdims=True)
    weights = jnp.where(allowed[None, None], jnp.exp(scores - top), 0.0)
    probs = weights / jnp.sum(weights, axis=-1, keepdims=True)
    probs_low = probs.astype(BF16)
    attended = jnp.einsum(
        "gkij,jgd->igkd", probs_low, values, preferred_element_type=F32
    ).reshape(count, q_cols)
    attended_low = attended.astype(BF16)
    branch_part = jnp.dot(attended_low, w_rows, preferred_element_type=F32).astype(BF16)
    branch = scatter_sum_ctx(branch_part.reshape(places, rows, width))

    x_full = x_own.astype(F32)
    middle = x_full + branch
    inv_ffn = lax.rsqrt(jnp.mean(middle * middle, axis=-1, keepdims=True) + NORM_EPS)
    normed_ffn = middle * inv_ffn
    ffn_low = (normed_ffn * gain_ffn[None, :]).astype(BF16)
    ffn_all = lax.all_gather(ffn_low, "fsdp", axis=0, tiled=True)
    attended_all = jnp.concatenate(
        absolute_order(own_row_order(gather_ctx(attended_low.reshape(places, rows, q_cols)))), axis=-1
    ).reshape(count, q_all)
    gate = jnp.einsum("td,fd->tf", ffn_all, w_gate, preferred_element_type=F32)
    up = jnp.einsum("td,fd->tf", ffn_all, w_up, preferred_element_type=F32)
    d_hidden = jnp.einsum("td,fd->tf", cot_all, w_down, preferred_element_type=F32)
    sigmoid = jax.nn.sigmoid(gate)
    silu = gate * sigmoid
    hidden = (silu * up).astype(BF16)
    d_gate = (d_hidden * up * sigmoid * (1.0 + gate * (1.0 - sigmoid))).astype(BF16)
    d_up = (d_hidden * silu).astype(BF16)
    d_ffn_part = jnp.dot(d_gate, w_gate, preferred_element_type=F32) + jnp.dot(
        d_up, w_up, preferred_element_type=F32
    )
    d_ffn = lax.psum_scatter(
        d_ffn_part.astype(BF16), "fsdp", scatter_dimension=0, tiled=True
    ).astype(F32)
    ffn_part = jnp.dot(hidden, w_down, preferred_element_type=F32).astype(BF16)
    layer_out = middle + lax.psum_scatter(
        ffn_part, "fsdp", scatter_dimension=0, tiled=True
    ).astype(F32)
    grads_ffn = [
        lax.psum(
            jnp.einsum("tf,td->fd", a, b, preferred_element_type=F32).astype(BF16), "ctx"
        ).astype(F32)
        for a, b in ((hidden, cot_all), (d_gate, ffn_all), (d_up, ffn_all))
    ]

    scaled = d_ffn * gain_ffn[None, :]
    d_gain_ffn = jnp.sum(d_ffn * normed_ffn, axis=0)
    d_middle = cot_own.astype(F32) + inv_ffn * (
        scaled - normed_ffn * jnp.mean(scaled * normed_ffn, axis=-1, keepdims=True)
    )
    d_branch_own = d_middle.astype(BF16)
    d_branch = gather_ctx(d_branch_own).reshape(count, width)
    d_attended = jnp.einsum("te,fe->tf", d_branch, w_rows, preferred_element_type=F32).astype(BF16)
    d_att_heads = d_attended.reshape(count, kv_heads, GROUP, HEAD_WIDTH)
    delta = jnp.sum(
        d_attended.astype(F32).reshape(count, q_heads, HEAD_WIDTH)
        * attended.reshape(count, q_heads, HEAD_WIDTH),
        axis=-1,
    )
    delta = jnp.transpose(delta.reshape(count, kv_heads, GROUP), (1, 2, 0))
    d_probs = jnp.einsum("igkd,jgd->gkij", d_att_heads, values, preferred_element_type=F32)
    d_scores = (probs * (d_probs - delta[..., None])).astype(BF16)
    d_queries = score_scale * jnp.einsum(
        "gkij,jgd->igkd", d_scores, keys, preferred_element_type=F32
    )
    d_keys = score_scale * jnp.einsum(
        "gkij,igkd->jgd", d_scores, queries, preferred_element_type=F32
    )
    d_values = jnp.einsum("gkij,igkd->jgd", probs_low, d_att_heads, preferred_element_type=F32)
    d_packed = jnp.concatenate(
        [
            apply_rotation(
                d_queries.reshape(count, q_heads, HEAD_WIDTH), cosine, -sine
            ).reshape(count, q_cols),
            apply_rotation(d_keys, cosine, -sine).reshape(count, kv_cols),
            d_values.reshape(count, kv_cols),
        ],
        axis=-1,
    ).astype(BF16)
    d_attn_part = jnp.einsum("tc,dc->td", d_packed, w_heads, preferred_element_type=F32)
    d_attn = scatter_sum_ctx(d_attn_part.astype(BF16).reshape(places, rows, width))
    inv_own = lax.rsqrt(jnp.mean(x_full * x_full, axis=-1, keepdims=True) + NORM_EPS)
    normed_attn = x_full * inv_own
    scaled_attn = d_attn * gain_attn[None, :]
    d_tokens = d_middle + inv_own * (
        scaled_attn - normed_attn * jnp.mean(scaled_attn * normed_attn, axis=-1, keepdims=True)
    )

    d_out_cols = jnp.einsum(
        "tf,te->fe",
        attended_all,
        lax.dynamic_slice_in_dim(d_branch, place * out_cols, out_cols, 1),
        preferred_element_type=F32,
    ).astype(BF16)
    gain_cols = jnp.broadcast_to(d_gain_ffn.astype(BF16)[:, None], (width, 128))
    out_scattered = lax.psum_scatter(
        jnp.concatenate([d_out_cols, gain_cols], axis=1), "fsdp", scatter_dimension=0, tiled=True
    )
    out_blocks = absolute_order(gather_ctx(out_scattered))
    grad_out = jnp.concatenate([b[:, :out_cols] for b in out_blocks], axis=1).astype(F32)
    grad_gain_ffn = sum(b[:, out_cols].astype(F32) for b in out_blocks)
    d_heads = jnp.einsum("td,tc->dc", normed_low, d_packed, preferred_element_type=F32)
    heads_scattered = lax.psum_scatter(
        d_heads.astype(BF16), "fsdp", scatter_dimension=0, tiled=True
    )
    head_blocks = absolute_order(gather_ctx(heads_scattered))
    grad_qkv = jnp.concatenate(
        [b[:, :q_cols] for b in head_blocks]
        + [b[:, q_cols : q_cols + kv_cols] for b in head_blocks]
        + [b[:, q_cols + kv_cols :] for b in head_blocks],
        axis=1,
    ).astype(F32)
    grad_gain_attn = jnp.sum(grad_qkv * w_qkv.astype(F32), axis=1) / norm_attn.astype(F32)
    return (
        layer_out.astype(BF16)[None],
        d_tokens[None],
        grad_gain_attn,
        grad_qkv,
        grad_out,
        grad_gain_ffn,
        grads_ffn[1],
        grads_ffn[2],
        grads_ffn[0],
    )


def solution(mesh):
    return jax.shard_map(
        local,
        mesh=mesh,
        in_specs=(
            P("fsdp", "ctx", None),
            P("fsdp", "ctx", None),
            P("fsdp"),
            P("fsdp", None),
            P("fsdp", None),
            P("fsdp"),
            P("fsdp", None),
            P("fsdp", None),
            P("fsdp", None),
            P("fsdp"),
            P("fsdp"),
            P("fsdp", None),
        ),
        out_specs=(
            P("fsdp", "ctx", None),
            P("fsdp", "ctx", None),
            P("fsdp"),
            P("fsdp", None),
            P("fsdp", None),
            P("fsdp"),
            P("fsdp", None),
            P("fsdp", None),
            P("fsdp", None),
        ),
        check_vma=False,
    )
```

time: 3230 us -> 904 us (0.28)
  waiting for transfers between devices: 2660 us -> 510 us
  matrix products: 284 us -> 152 us
  other arithmetic: 140 us -> 84.5 us
  local copies, waits for them, and re-layouts: 27.7 us -> 72.5 us
  blocking collectives: 46.5 us -> 12 us
    all_gather x6 -> x4, waiting for transfers between devices: 1320 us -> 107 us  [the longest x1 62.5 us: local(): ffn_all = lax.all_gather(ffn_low, 'fsdp', axis=0, tiled=True)]
    reduce_scatter x3 -> x4, waiting for transfers between devices: 1040 us -> 127 us  [the longest x1 60.2 us: local(): lax.psum_scatter(ffn_part, 'fsdp', scatter_dimension=0, tiled=True)]
    dot_general x42 -> x21, matrix products: 284 us -> 152 us  [the longest x3 31.5 us: local(): jnp.einsum('tf,td->fd', a, b, preferred_element_type=F32).astype(BF16)]
    psum x1, waiting for transfers between devices: 230 us -> 120 us  [local(): lax.psum(jnp.einsum('tf,td->fd', a, b, preferred_element_type=F32).astype...]
    ppermute x14 -> x31, waiting for transfers between devices: 66.3 us -> 156 us  [swap(): return lax.ppermute(x, 'ctx', [(i, i ^ bit) for i in range(4)])]
    another operation x6 -> x24, other arithmetic: 79.2 us -> 13.8 us  [the longest x1 68.1 us: local(): jnp.stack([jnp.einsum('tf,td->fd', gate_part, ffn_low, preferred_element_...]
  transfers between devices with their start and end apart: 24 -> 40, of which waited for: 23 -> 28; matrix products, arithmetic and copies ran while one was open for 13% -> 22% of each run, Pallas kernels for 0% -> 0%
where the time goes in v1:
time: 904 us; the launch traced here: 896 us
  waiting for transfers between devices  510 us (56%)
  matrix products  152 us (17%)
  other arithmetic  84.5 us (9%)
  local copies, waits for them, and re-layouts  72.5 us (8%)
  starting transfers between devices  41.1 us (5%)
  between operations  24.8 us (3%)
  blocking collectives  12 us (1%)
    ppermute x31, waiting for transfers between devices, swap(): return lax.ppermute(x, 'ctx', [(i, i ^ bit) for i in range(4)])  156 us
    psum x1, waiting for transfers between devices, local(): lax.psum(jnp.einsum('tf,td->fd', a, b, preferred_element_type=F32).astype...  120 us
    all_gather x1, waiting for transfers between devices, local(): ffn_all = lax.all_gather(ffn_low, 'fsdp', axis=0, tiled=True)  62.5 us
    reduce_scatter x1, waiting for transfers between devices, local(): lax.psum_scatter(ffn_part, 'fsdp', scatter_dimension=0, tiled=True)  60.2 us
    reduce_scatter x1, waiting for transfers between devices, local(): lax.psum_scatter(d_heads.astype(BF16), 'fsdp', scatter_dimension=0, tiled...  45.8 us
    all_gather x1, waiting for transfers between devices, local(): cot_all = lax.all_gather(cot_own, 'fsdp', axis=0, tiled=True)  44.3 us
    ppermute x31, starting transfers between devices, swap(): return lax.ppermute(x, 'ctx', [(i, i ^ bit) for i in range(4)])  40.6 us
    dot_general x3, matrix products, local(): jnp.einsum('tf,td->fd', a, b, preferred_element_type=F32).astype(BF16)  31.5 us
  transfers between devices with their start and end apart: 40, of which 28 were waited for; matrix products, arithmetic and copies ran while one was open for 22% of the time, Pallas kernels for 0%

profile of v1, /device:TPU:0, one launch (start us, length us, event | category | flops | bytes accessed | tf_op | source)
XLA Modules:
  0.0 896.4 jit_solution(14603575492479198908)
XLA Ops:
  38.6 12.0 %all_gather.15 = bf16[2,2048]{1,0:T(2,128)(2,1)S(1)} all-gather(bf16[2,256]{1,0:T(2,128)(2,1)S(1)} %pad_maximum_fusion.35), channel_id=1, replica_groups=mesh['ctx'=4,'fsdp'=8] {'fsdp'}, dimensions={1}, use_global_device_ids=true | all-gather | bytes 9216 | tf_op jit(solution)/shard_map/all_gather | solution.py:159
  72.4 7.2 collective-permute-done.4
  79.5 8.0 collective-permute-done.5
  90.9 6.1 fusion.97
  114.1 5.1 fusion.73
  119.3 11.4 %fusion.96 = (f32[2,2,768]{2,1,0:T(2,128)S(1)}, f32[2,2,768,768]{2,3,1,0:T(8,128)S(1)}) fusion(f32[2,768,768,2]{2,1,3,0:T(8,128)} %fusion.73, pred[768,768]{0,1:T(8,128)(4,1)S(1)} %copy-done.63), kind=kOutput, calls=%fused_computation.298 | output fusion | flops 16515839 | bytes 19476480 | tf_op jit(solution)/shard_map/sub | solution.py:199
  142.4 16.7 %collective-permute-done.7 = bf16[2,192,1024]{2,1,0:T(8,128)(2,1)S(1)} collective-permute-done((bf16[2,192,1024]{2,1,0:T(8,128)(2,1)S(1)}, bf16[2,192,1024]{2,1,0:T(8,128)(2,1)S(1)}, u32[]{:S(2)}, u32[]{:S(2)}) %collective-permute-start.7) | collective-permute-done | bytes 786464 | tf_op jit(solution)/shard_map/ppermute | solution.py:43
  163.1 8.1 collective-permute-done.8
  175.5 62.5 %all-gather.10.cloned.1.call-done = bf16[1536,2048]{1,0:T(8,128)(2,1)} async-done(((bf16[192,2048]{1,0:T(8,128)(2,1)}), bf16[1536,2048]{1,0:T(8,128)(2,1)}) %all-gather.10.cloned.1.call-update) | async-done | bytes 6291472 | tf_op jit(solution)/shard_map/all_gather | solution.py:214
  238.0 11.8 %fusion.98 = f32[1536,1024]{1,0:T(8,128)} fusion(bf16[1536,2048]{1,0:T(8,128)(2,1)} %all-gather.10.cloned.1.call-done, bf16[1024,2048]{1,0:T(8,128)(2,1)} %param.18), kind=kOutput, calls=%fused_computation.300 | convolution fusion | flops 6442450944 | bytes 16777216 | tf_op jit(solution)/shard_map/td,fd->tf/dot_general | solution.py:218
  249.9 8.8 fusion.99
  258.7 44.3 %all-gather.12.cloned.1.call-done = bf16[1,1536,2048]{2,1,0:T(8,128)(2,1)} async-done(((bf16[1,192,2048]{2,1,0:T(8,128)(2,1)}), bf16[1,1536,2048]{2,1,0:T(8,128)(2,1)}) %all-gather.12.cloned.1.call-update) | async-done | bytes 6291472 | tf_op jit(solution)/shard_map/all_gather | solution.py:168
  303.0 18.2 %multiply_convert_fusion = (bf16[1536,1024]{1,0:T(8,128)(2,1)}, bf16[1536,1024]{1,0:T(8,128)(2,1)}, bf16[1536,1024]{1,0:T(8,128)(2,1)}) fusion(f32[1536,1024]{1,0:T(8,128)} %fusion.98, f32[1536,1024]{1,0:T(8,128)} %fusion.99, bf16[1024,2048]{1,0:T(8,128)(2,1)} %param.20, bf16[1,1536,2048]{2,1,0:T(8,128)(2,1)} %all-gather.12.cloned.1.call-done), kind=kOutput, calls=%fused_computation.16 | convolution fusion | flops 6466043904 | bytes 32505856 | tf_op jit(solution)/shard_map/td,fd->tf/dot_general | solution.py:220
  321.1 11.9 %fusion.100 = f32[1536,2048]{1,0:T(8,128)} fusion(bf16[1536,1024]{1,0:T(8,128)(2,1)} %get-tuple-element.48, bf16[1024,2048]{1,0:T(8,128)(2,1)S(1)} %copy-done.81), kind=kOutput, calls=%fused_computation.302 | convolution fusion | flops 6442450944 | bytes 19922944 | tf_op jit(solution)/shard_map/dot_general | solution.py:226
  333.0 11.5 %add_convert_fusion = bf16[1536,2048]{1,0:T(8,128)(2,1)} fusion(f32[1536,2048]{1,0:T(8,128)} %fusion.100, bf16[1536,1024]{1,0:T(8,128)(2,1)S(1)} %copy-done.86, bf16[1024,2048]{1,0:T(8,128)(2,1)S(1)} %copy-done.83), kind=kOutput, calls=%fused_computation.1 | convolution fusion | flops 6448742400 | bytes 26214400 | tf_op jit(solution)/shard_map/dot_general | solution.py:226
  344.6 11.3 %convolution_convert_fusion.2 = bf16[1024,2048]{1,0:T(8,128)(2,1)} fusion(bf16[1536,1024]{1,0:T(8,128)(2,1)} %get-tuple-element.48, bf16[1536,2048]{1,0:T(8,128)(2,1)} %all-gather.10.cloned.1.call-done), kind=kOutput, calls=%fused_computation.29 | convolution fusion | flops 6444548096 | bytes 13631488 | tf_op jit(solution)/shard_map/tf,td->fd/dot_general | solution.py:238
  355.9 11.5 %convolution_convert_fusion.1 = bf16[1024,2048]{1,0:T(8,128)(2,1)} fusion(bf16[1536,1024]{1,0:T(8,128)(2,1)S(1)} %copy-done.87, bf16[1536,2048]{1,0:T(8,128)(2,1)} %all-gather.10.cloned.1.call-done), kind=kOutput, calls=%fused_computation.28 | convolution fusion | flops 6444548096 | bytes 13631488 | tf_op jit(solution)/shard_map/tf,td->fd/dot_general | solution.py:238
  367.5 8.6 fusion.15
  386.8 8.3 collective-permute-done.23
  407.6 7.8 collective-permute-done.24
  426.8 16.6 %collective-permute-done.12 = bf16[192,1024]{1,0:T(8,128)(2,1)S(1)} collective-permute-done((bf16[192,1024]{1,0:T(8,128)(2,1)S(1)}, bf16[192,1024]{1,0:T(8,128)(2,1)S(1)}, u32[]{:S(2)}, u32[]{:S(2)}) %collective-permute-start.12) | collective-permute-done | bytes 393248 | tf_op jit(solution)/shard_map/ppermute | solution.py:43
  447.0 32.6 %collective-permute-done.13 = bf16[2,192,1024]{2,1,0:T(8,128)(2,1)S(1)} collective-permute-done((bf16[2,192,1024]{2,1,0:T(8,128)(2,1)S(1)}, bf16[2,192,1024]{2,1,0:T(8,128)(2,1)S(1)}, u32[]{:S(2)}, u32[]{:S(2)}) %collective-permute-start.13) | collective-permute-done | bytes 786464 | tf_op jit(solution)/shard_map/ppermute | solution.py:43
  487.2 11.6 %convolution_convert_fusion = bf16[1536,2048]{1,0:T(8,128)(2,1)} fusion(bf16[1536,1024]{1,0:T(8,128)(2,1)} %get-tuple-element.49, bf16[1024,2048]{1,0:T(8,128)(2,1)} %param.20), kind=kOutput, calls=%fused_computation.7 | convolution fusion | flops 6445596672 | bytes 13631488 | tf_op jit(solution)/shard_map/dot_general | solution.py:232
  535.8 5.2 convolution_convert_fusion.3
  541.0 6.1 convolution_convert_fusion.5
  548.7 27.5 %collective-permute-done.15 = bf16[2,192,1024]{2,1,0:T(8,128)(2,1)S(1)} collective-permute-done((bf16[2,192,1024]{2,1,0:T(8,128)(2,1)S(1)}, bf16[2,192,1024]{2,1,0:T(8,128)(2,1)S(1)}, u32[]{:S(2)}, u32[]{:S(2)}) %collective-permute-start.15) | collective-permute-done | bytes 786464 | tf_op jit(solution)/shard_map/ppermute | solution.py:43
  579.4 119.7 %all-reduce.3.cloned.1.call-done = (bf16[1024,2048]{1,0:T(8,128)(2,1)}, bf16[1024,2048]{1,0:T(8,128)(2,1)}, bf16[1024,2048]{1,0:T(8,128)(2,1)}) async-done(((bf16[1024,2048]{1,0:T(8,128)(2,1)}, bf16[1024,2048]{1,0:T(8,128)(2,1)}, bf16[1024,2048]{1,0:T(8,128)(2,1)}), (bf16[1024,2048]{1,0:T(8,128)(2,1)}, bf16[1024,2048]{1,0:T(8,128)(2,1)}, bf16[1024,2048]{1,0:T(8,128)(2,1)})) %all-reduce.3.cloned.1.call-update) | async-done | bytes 12582928 | tf_op jit(solution)/shard_map/psum | solution.py:237
  699.1 6.8 convert_element_type.318
  718.3 20.7 %reduce-scatter.11.cloned.1.call-done = bf16[256,640]{0,1:T(8,128)(2,1)} async-done(((bf16[2048,640]{0,1:T(8,128)(2,1)}), bf16[256,640]{0,1:T(8,128)(2,1)}) %reduce-scatter.11.cloned.1.call-update) | async-done | bytes 327696 | tf_op jit(solution)/shard_map/reduce_scatter | solution.py:293
  749.8 60.2 %reduce-scatter.5.cloned.1.call-done = bf16[192,2048]{1,0:T(8,128)(2,1)} async-done(((bf16[1536,2048]{1,0:T(8,128)(2,1)}), bf16[192,2048]{1,0:T(8,128)(2,1)}) %reduce-scatter.5.cloned.1.call-update) | async-done | bytes 786448 | tf_op jit(solution)/shard_map/reduce_scatter | solution.py:233
  815.5 45.8 %reduce-scatter.9.cloned.1.call-done = bf16[256,1024]{1,0:T(8,128)(2,1)} async-done(((bf16[2048,1024]{1,0:T(8,128)(2,1)}), bf16[256,1024]{1,0:T(8,128)(2,1)}) %reduce-scatter.9.cloned.1.call-update) | async-done | bytes 524304 | tf_op jit(solution)/shard_map/reduce_scatter | solution.py:300
  876.8 5.3 collective-permute-done.22
  (411 shorter events, 222.3 us)
Async XLA Ops:
  7.2 55.0 %all-gather.8.cloned.1.call-start = ((), (), s32[]{:S(2)}) async-start(), calls=%async_computation.5 | async-start | bytes 2359296 | tf_op jit(solution)/shard_map/all_gather | solution.py:164
  9.2 81.7 %all-gather.6.cloned.1.call-start = ((), (), s32[]{:S(2)}) async-start(), calls=%async_computation.4 | async-start | bytes 4718592 | tf_op jit(solution)/shard_map/all_gather | solution.py:158
  12.1 225.9 %all-gather.10.cloned.1.call-start = ((), (), s32[]{:S(2)}) async-start(), calls=%async_computation.6 | async-start | bytes 7077888 | tf_op jit(solution)/shard_map/all_gather | solution.py:214
  13.2 12.3 %collective-permute-start.1 = (bf16[192,1024]{1,0:T(8,128)(2,1)}, bf16[192,1024]{1,0:T(8,128)(2,1)S(1)}, u32[]{:S(2)}, u32[]{:S(2)}) collective-permute-start(bf16[192,1024]{1,0:T(8,128)(2,1)} %get-tuple-element.127), channel_id=1, source_target_pairs={{0,16},{8,24},{16,0},{24,8},{1,17},{9,25},{17,1},{25,9},{2,18},{10... | collective-permute-start | bytes 1179656 | tf_op jit(solution)/shard_map/ppermute | solution.py:43
  16.2 20.7 %collective-permute-start = (bf16[192,1024]{1,0:T(8,128)(2,1)}, bf16[192,1024]{1,0:T(8,128)(2,1)S(1)}, u32[]{:S(2)}, u32[]{:S(2)}) collective-permute-start(bf16[192,1024]{1,0:T(8,128)(2,1)} %get-tuple-element.126), channel_id=1, source_target_pairs={{0,8},{8,0},{16,24},{24,16},{1,9},{9,1},{17,25},{25,17},{2,10},{10... | collective-permute-start | bytes 1179656 | tf_op jit(solution)/shard_map/ppermute | solution.py:43
  26.5 24.1 %collective-permute-start.2 = (bf16[2,192,1024]{2,1,0:T(8,128)(2,1)}, bf16[2,192,1024]{2,1,0:T(8,128)(2,1)}, u32[]{:S(2)}, u32[]{:S(2)}) collective-permute-start(bf16[2,192,1024]{2,1,0:T(8,128)(2,1)} %pad_maximum_fusion.6), channel_id=1, source_target_pairs={{0,8},{8,0},{16,24},{24,16},{1,9},{9,1},{17,25},{25,17},{2,10},{10... | collective-permute-start | bytes 2359304 | tf_op jit(solution)/shard_map/ppermute | solution.py:43
  37.0 18.3 %collective-permute-start.3 = (bf16[2,192,1024]{2,1,0:T(8,128)(2,1)S(1)}, bf16[2,192,1024]{2,1,0:T(8,128)(2,1)S(1)}, u32[]{:S(2)}, u32[]{:S(2)}) collective-permute-start(bf16[2,192,1024]{2,1,0:T(8,128)(2,1)S(1)} %pad_maximum_fusion.7), channel_id=1, source_target_pairs={{0,16},{8,24},{16,0},{24,8},{1,17},{9,25},{17,1},{25,9},{2,18},{10... | collective-permute-start | bytes 2359304 | tf_op jit(solution)/shard_map/ppermute | solution.py:43
  63.7 15.8 %collective-permute-start.4 = (bf16[512,512]{1,0:T(8,128)(2,1)S(1)}, bf16[512,512]{1,0:T(8,128)(2,1)S(1)}, u32[]{:S(2)}, u32[]{:S(2)}) collective-permute-start(bf16[512,512]{1,0:T(8,128)(2,1)S(1)} %get-tuple-element.78), channel_id=1, source_target_pairs={{0,24},{8,16},{16,8},{24,0},{1,25},{9,17},{17,9},{25,1},{2,26},{10... | collective-permute-start | bytes 1572872 | tf_op jit(solution)/shard_map/ppermute | solution.py:43
  65.2 22.3 %collective-permute-start.5 = (bf16[512,512]{1,0:T(8,128)(2,1)S(1)}, bf16[512,512]{1,0:T(8,128)(2,1)S(1)}, u32[]{:S(2)}, u32[]{:S(2)}) collective-permute-start(bf16[512,512]{1,0:T(8,128)(2,1)S(1)} %get-tuple-element.77), channel_id=1, source_target_pairs={{0,16},{8,24},{16,0},{24,8},{1,17},{9,25},{17,1},{25,9},{2,18},{10... | collective-permute-start | bytes 1572872 | tf_op jit(solution)/shard_map/ppermute | solution.py:43
  65.8 21.9 %collective-permute-start.6 = (bf16[512,512]{1,0:T(8,128)(2,1)S(1)}, bf16[512,512]{1,0:T(8,128)(2,1)S(1)}, u32[]{:S(2)}, u32[]{:S(2)}) collective-permute-start(bf16[512,512]{1,0:T(8,128)(2,1)S(1)} %get-tuple-element.76), channel_id=1, source_target_pairs={{0,8},{8,0},{16,24},{24,16},{1,9},{9,1},{17,25},{25,17},{2,10},{10... | collective-permute-start | bytes 1572872 | tf_op jit(solution)/shard_map/ppermute | solution.py:43
  139.4 19.8 %collective-permute-start.7 = (bf16[2,192,1024]{2,1,0:T(8,128)(2,1)S(1)}, bf16[2,192,1024]{2,1,0:T(8,128)(2,1)S(1)}, u32[]{:S(2)}, u32[]{:S(2)}) collective-permute-start(bf16[2,192,1024]{2,1,0:T(8,128)(2,1)S(1)} %pad_maximum_fusion.9), channel_id=1, source_target_pairs={{0,8},{8,0},{16,24},{24,16},{1,9},{9,1},{17,25},{25,17},{2,10},{10... | collective-permute-start | bytes 2359304 | tf_op jit(solution)/shard_map/ppermute | solution.py:43
  140.9 19.4 %collective-permute-start.9 = (bf16[2,192,1024]{2,1,0:T(8,128)(2,1)S(1)}, bf16[2,192,1024]{2,1,0:T(8,128)(2,1)S(1)}, u32[]{:S(2)}, u32[]{:S(2)}) collective-permute-start(bf16[2,192,1024]{2,1,0:T(8,128)(2,1)S(1)} %slice.476), channel_id=1, source_target_pairs={{0,16},{8,24},{16,0},{24,8},{1,17},{9,25},{17,1},{25,9},{2,18},{10... | collective-permute-start | bytes 2359304 | tf_op jit(solution)/shard_map/ppermute | solution.py:43
  174.9 128.0 %all-gather.12.cloned.1.call-start = ((), (), s32[]{:S(2)}) async-start(), calls=%async_computation.11 | async-start | bytes 7077888 | tf_op jit(solution)/shard_map/all_gather | solution.py:168
  175.5 245.6 %reduce-scatter.7.cloned.1.call-start = ((), (), s32[]{:S(2)}) async-start(), calls=%async_computation.8 | async-start | bytes 7077888 | tf_op jit(solution)/shard_map/reduce_scatter | solution.py:229
  344.5 354.6 %all-reduce.3.cloned.1.call-start = ((), (), s32[]{:S(2)}) async-start(), calls=%async_computation.12 | async-start | bytes 25165824 | tf_op jit(solution)/shard_map/psum | solution.py:237
  376.1 362.8 %reduce-scatter.11.cloned.1.call-start = ((), (), s32[]{:S(2)}) async-start(), calls=%async_computation.10 | async-start | bytes 2949120 | tf_op jit(solution)/shard_map/reduce_scatter | solution.py:293
  385.4 12.2 %collective-permute-start.25 = (bf16[4,192,256]{2,1,0:T(8,128)(2,1)S(1)}, bf16[4,192,256]{2,1,0:T(8,128)(2,1)S(1)}, u32[]{:S(2)}, u32[]{:S(2)}) collective-permute-start(bf16[4,192,256]{2,1,0:T(8,128)(2,1)S(1)} %get-tuple-element.103), channel_id=1, source_target_pairs={{0,16},{8,24},{16,0},{24,8},{1,17},{9,25},{17,1},{25,9},{2,18},{10... | collective-permute-start | bytes 1179656 | tf_op jit(solution)/shard_map/ppermute | solution.py:43
  396.1 19.3 %collective-permute-start.24 = (bf16[2,4,192,256]{3,2,1,0:T(8,128)(2,1)}, bf16[2,4,192,256]{3,2,1,0:T(8,128)(2,1)}, u32[]{:S(2)}, u32[]{:S(2)}) collective-permute-start(bf16[2,4,192,256]{3,2,1,0:T(8,128)(2,1)} %pad_maximum_fusion.14), channel_id=1, source_target_pairs={{0,16},{8,24},{16,0},{24,8},{1,17},{9,25},{17,1},{25,9},{2,18},{10... | collective-permute-start | bytes 2359304 | tf_op jit(solution)/shard_map/ppermute | solution.py:43
  398.5 19.0 %collective-permute-start.26 = (bf16[2,4,192,256]{3,2,1,0:T(8,128)(2,1)}, bf16[2,4,192,256]{3,2,1,0:T(8,128)(2,1)}, u32[]{:S(2)}, u32[]{:S(2)}) collective-permute-start(bf16[2,4,192,256]{3,2,1,0:T(8,128)(2,1)} %pad_maximum_fusion.15), channel_id=1, source_target_pairs={{0,8},{8,0},{16,24},{24,16},{1,9},{9,1},{17,25},{25,17},{2,10},{10... | collective-permute-start | bytes 2359304 | tf_op jit(solution)/shard_map/ppermute | solution.py:43
  423.9 19.4 %collective-permute-start.12 = (bf16[192,1024]{1,0:T(8,128)(2,1)S(1)}, bf16[192,1024]{1,0:T(8,128)(2,1)S(1)}, u32[]{:S(2)}, u32[]{:S(2)}) collective-permute-start(bf16[192,1024]{1,0:T(8,128)(2,1)S(1)} %get-tuple-element.116), channel_id=1, source_target_pairs={{0,16},{8,24},{16,0},{24,8},{1,17},{9,25},{17,1},{25,9},{2,18},{10... | collective-permute-start | bytes 1179656 | tf_op jit(solution)/shard_map/ppermute | solution.py:43
  424.8 20.4 %collective-permute-start.11 = (bf16[192,1024]{1,0:T(8,128)(2,1)S(1)}, bf16[192,1024]{1,0:T(8,128)(2,1)S(1)}, u32[]{:S(2)}, u32[]{:S(2)}) collective-permute-start(bf16[192,1024]{1,0:T(8,128)(2,1)S(1)} %get-tuple-element.117), channel_id=1, source_target_pairs={{0,8},{8,0},{16,24},{24,16},{1,9},{9,1},{17,25},{25,17},{2,10},{10... | collective-permute-start | bytes 1179656 | tf_op jit(solution)/shard_map/ppermute | solution.py:43
  443.5 36.1 %collective-permute-start.13 = (bf16[2,192,1024]{2,1,0:T(8,128)(2,1)S(1)}, bf16[2,192,1024]{2,1,0:T(8,128)(2,1)S(1)}, u32[]{:S(2)}, u32[]{:S(2)}) collective-permute-start(bf16[2,192,1024]{2,1,0:T(8,128)(2,1)S(1)} %pad_maximum_fusion.10), channel_id=1, source_target_pairs={{0,8},{8,0},{16,24},{24,16},{1,9},{9,1},{17,25},{25,17},{2,10},{10... | collective-permute-start | bytes 2359304 | tf_op jit(solution)/shard_map/ppermute | solution.py:43
  445.3 35.9 %collective-permute-start.14 = (bf16[2,192,1024]{2,1,0:T(8,128)(2,1)S(1)}, bf16[2,192,1024]{2,1,0:T(8,128)(2,1)S(1)}, u32[]{:S(2)}, u32[]{:S(2)}) collective-permute-start(bf16[2,192,1024]{2,1,0:T(8,128)(2,1)S(1)} %pad_maximum_fusion.11), channel_id=1, source_target_pairs={{0,16},{8,24},{16,0},{24,8},{1,17},{9,25},{17,1},{25,9},{2,18},{10... | collective-permute-start | bytes 2359304 | tf_op jit(solution)/shard_map/ppermute | solution.py:43
  487.1 323.0 %reduce-scatter.5.cloned.1.call-start = ((), (), s32[]{:S(2)}) async-start(), calls=%async_computation.7 | async-start | bytes 7077888 | tf_op jit(solution)/shard_map/reduce_scatter | solution.py:233
  498.8 362.5 %reduce-scatter.9.cloned.1.call-start = ((), (), s32[]{:S(2)}) async-start(), calls=%async_computation.9 | async-start | bytes 4718592 | tf_op jit(solution)/shard_map/reduce_scatter | solution.py:300
  547.4 28.8 %collective-permute-start.15 = (bf16[2,192,1024]{2,1,0:T(8,128)(2,1)S(1)}, bf16[2,192,1024]{2,1,0:T(8,128)(2,1)S(1)}, u32[]{:S(2)}, u32[]{:S(2)}) collective-permute-start(bf16[2,192,1024]{2,1,0:T(8,128)(2,1)S(1)} %pad_maximum_fusion.13), channel_id=1, source_target_pairs={{0,8},{8,0},{16,24},{24,16},{1,9},{9,1},{17,25},{25,17},{2,10},{10... | collective-permute-start | bytes 2359304 | tf_op jit(solution)/shard_map/ppermute | solution.py:43
  547.7 28.5 %collective-permute-start.17 = (bf16[2,192,1024]{2,1,0:T(8,128)(2,1)S(1)}, bf16[2,192,1024]{2,1,0:T(8,128)(2,1)S(1)}, u32[]{:S(2)}, u32[]{:S(2)}) collective-permute-start(bf16[2,192,1024]{2,1,0:T(8,128)(2,1)S(1)} %slice.498), channel_id=1, source_target_pairs={{0,16},{8,24},{16,0},{24,8},{1,17},{9,25},{17,1},{25,9},{2,18},{10... | collective-permute-start | bytes 2359304 | tf_op jit(solution)/shard_map/ppermute | solution.py:43
  577.4 137.5 %collective-permute-start.16 = (bf16[192,1024]{1,0:T(8,128)(2,1)S(1)}, bf16[192,1024]{1,0:T(8,128)(2,1)}, u32[]{:S(2)}, u32[]{:S(2)}) collective-permute-start(bf16[192,1024]{1,0:T(8,128)(2,1)S(1)} %get-tuple-element.58), channel_id=1, source_target_pairs={{0,16},{8,24},{16,0},{24,8},{1,17},{9,25},{17,1},{25,9},{2,18},{10... | collective-permute-start | bytes 1179656 | tf_op jit(solution)/shard_map/ppermute | solution.py:43
  578.8 136.0 %collective-permute-start.18 = (bf16[192,1024]{1,0:T(8,128)(2,1)S(1)}, bf16[192,1024]{1,0:T(8,128)(2,1)}, u32[]{:S(2)}, u32[]{:S(2)}) collective-permute-start(bf16[192,1024]{1,0:T(8,128)(2,1)S(1)} %get-tuple-element.59), channel_id=1, source_target_pairs={{0,8},{8,0},{16,24},{24,16},{1,9},{9,1},{17,25},{25,17},{2,10},{10... | collective-permute-start | bytes 1179656 | tf_op jit(solution)/shard_map/ppermute | solution.py:43
  746.1 68.3 %collective-permute-start.30 = (bf16[2,256,320]{1,2,0:T(8,128)(2,1)}, bf16[2,256,320]{1,2,0:T(8,128)(2,1)S(1)}, u32[]{:S(2)}, u32[]{:S(2)}) collective-permute-start(bf16[2,256,320]{1,2,0:T(8,128)(2,1)} %pad_maximum_fusion.29), channel_id=1, source_target_pairs={{0,8},{8,0},{16,24},{24,16},{1,9},{9,1},{17,25},{25,17},{2,10},{10... | collective-permute-start | bytes 983048 | tf_op jit(solution)/shard_map/ppermute | solution.py:43
  749.3 65.2 %collective-permute-start.28 = (bf16[2,256,320]{1,2,0:T(8,128)(2,1)}, bf16[2,256,320]{1,2,0:T(8,128)(2,1)}, u32[]{:S(2)}, u32[]{:S(2)}) collective-permute-start(bf16[2,256,320]{1,2,0:T(8,128)(2,1)} %pad_maximum_fusion.28), channel_id=1, source_target_pairs={{0,16},{8,24},{16,0},{24,8},{1,17},{9,25},{17,1},{25,9},{2,18},{10... | collective-permute-start | bytes 983048 | tf_op jit(solution)/shard_map/ppermute | solution.py:43
  869.7 12.3 %collective-permute-start.22 = (bf16[2,256,512]{2,1,0:T(8,128)(2,1)}, bf16[2,256,512]{2,1,0:T(8,128)(2,1)}, u32[]{:S(2)}, u32[]{:S(2)}) collective-permute-start(bf16[2,256,512]{2,1,0:T(8,128)(2,1)} %pad_maximum_fusion.21), channel_id=1, source_target_pairs={{0,8},{8,0},{16,24},{24,16},{1,9},{9,1},{17,25},{25,17},{2,10},{10... | collective-permute-start | bytes 1572872 | tf_op jit(solution)/shard_map/ppermute | solution.py:43
  (100 other events, 730.5 us)
Sparse Core Ops, SparseCore 0:
  10.2 31.7 all-gather.7
  44.2 46.6 all-gather.5
  175.0 62.9 all-gather.9
  239.5 63.3 all-gather.11
  344.6 68.4 reduce-scatter.6
  417.5 281.5 all-reduce.2
  701.4 37.5 reduce-scatter.10
  741.2 68.7 reduce-scatter.4
  813.0 48.3 reduce-scatter.8

commit v2 on v1

v2 whole, which is shorter than its diff:
```python
import functools

import jax
import jax.numpy as jnp
from jax import lax
from jax.experimental import pallas as pl
from jax.experimental.pallas import tpu as pltpu
from jax.sharding import PartitionSpec as P

QUERY_HEADS = 16
KEY_VALUE_HEADS = 8
HEAD_WIDTH = 128
GROUP = QUERY_HEADS // KEY_VALUE_HEADS

NORM_EPS = 1e-05
NEGATIVE_FILLER = -1e30
ROPE_BASE = 1000000.0
LOG2_E = 1.4426950408889634
BF16 = jnp.bfloat16
F32 = jnp.float32


def rope_tables(positions):
    half_width = HEAD_WIDTH // 2
    frequency = ROPE_BASE ** (-(2.0 * jnp.arange(half_width, dtype=F32)) / HEAD_WIDTH)
    angle_table = positions.astype(F32)[:, None] * frequency[None, :]
    cosine, sine = jnp.cos(angle_table), jnp.sin(angle_table)
    return (
        jnp.concatenate([cosine, cosine], axis=1),
        jnp.concatenate([-sine, sine], axis=1),
    )


NT = (((1,), (1,)), ((), ()))
NN = (((1,), (0,)), ((), ()))
TN = (((0,), (0,)), ((), ()))
VMEM_LIMIT = 56 * 2**20


def product(a, b, dims):
    return lax.dot_general(a, b, dims, preferred_element_type=F32)


def pieces(length, most):
    size = most if length % most == 0 else length
    return [pl.ds(start, size) for start in range(0, length, size)]


def resident(shape):
    return pl.BlockSpec(shape, lambda i: (0,) * len(shape), pipeline_mode=pl.Buffered(1))


def kernel_params():
    return pltpu.CompilerParams(vmem_limit_bytes=VMEM_LIMIT)


def cost(us=0.3):
    return pl.CostEstimate(flops=int(us * 1e9), bytes_accessed=int(us * 3.69e6), transcendentals=0)


def anywhere(values):
    return [pl.BlockSpec(memory_space=pl.ANY)] * len(values)


def norm_project_kernel(blocks, count_in, *refs):
    parts, (gain_ref, weight_ref, normed_ref, out_ref) = refs[:count_in], refs[count_in:]

    @pl.when(pl.program_id(0) == 0)
    def _():
        gain = gain_ref[...]
        first_row = 0
        for block in blocks:
            pieces_of = []
            for i, lead in block:
                ref = parts[i]
                pieces_of.append((ref[...] if lead is None else ref[lead]).astype(F32))
            squares = sum(jnp.sum(p * p, axis=1, keepdims=True) for p in pieces_of)
            width = sum(p.shape[1] for p in pieces_of)
            inverse = lax.rsqrt(squares / width + NORM_EPS)
            column = 0
            for p in pieces_of:
                columns = pl.ds(column, p.shape[1])
                normed_ref[pl.ds(first_row, p.shape[0]), columns] = (
                    p * inverse * gain[:, column : column + p.shape[1]]
                ).astype(BF16)
                column += p.shape[1]
            first_row += pieces_of[0].shape[0]

    out_ref[...] = product(normed_ref[...], weight_ref[...], NN)


def norm_project(parts, blocks, gain, weights, columns):
    count = sum(parts[block[0][0]].shape[-2] for block in blocks)
    width = gain.shape[1]
    step = 256
    return pl.pallas_call(
        functools.partial(norm_project_kernel, blocks, len(parts)),
        out_shape=[
            jax.ShapeDtypeStruct((count, width), BF16),
            jax.ShapeDtypeStruct((count, columns), F32),
        ],
        grid=(columns // step,),
        in_specs=[resident(p.shape) for p in parts]
        + [resident((1, width)), pl.BlockSpec((width, step), lambda n: (0, n))],
        out_specs=[
            pl.BlockSpec((count, width), lambda n: (0, 0)),
            pl.BlockSpec((count, step), lambda n: (0, n)),
        ],
        compiler_params=kernel_params(),
        cost_estimate=cost(),
    )(*parts, gain, weights)


def hidden_kernel(x_ref, cot_ref, gate_up_ref, down_ref, *refs):
    hidden_ref, both_ref, hidden_t_ref, d_gate_t_ref, d_up_t_ref = refs[-5:]
    units = down_ref.shape[0]
    gate_up = product(x_ref[...], gate_up_ref[...], NT)
    d_hidden = product(cot_ref[...], down_ref[...], NT)
    gate, up = gate_up[:, :units], gate_up[:, units:]
    sigmoid = 1.0 / (1.0 + jnp.exp(-gate))
    silu = gate * sigmoid
    hidden = (silu * up).astype(BF16)
    d_gate = (d_hidden * up * (sigmoid + silu * (1.0 - sigmoid))).astype(BF16)
    d_up = (d_hidden * silu).astype(BF16)
    hidden_ref[...] = hidden
    both_ref[:, :units] = d_gate
    both_ref[:, units:] = d_up
    hidden_t_ref[...] = hidden.T
    d_gate_t_ref[...] = d_gate.T
    d_up_t_ref[...] = d_up.T


def hidden_grads(x, cot, gate_up, down, part, before=(), waits=()):
    count, width = x.shape
    units = down.shape[0] // 2
    block = 256
    rows_in = pl.BlockSpec((block, width), lambda i: (i, 0))
    once = pl.Buffered(1)
    transposed = pl.BlockSpec((units, block), lambda i: (0, i))
    return pl.pallas_call(
        hidden_kernel,
        out_shape=[
            jax.ShapeDtypeStruct((count, 2 * units), BF16),
            jax.ShapeDtypeStruct((count, 4 * units), BF16),
        ]
        + [jax.ShapeDtypeStruct((units, count), BF16)] * 3,
        grid=(count // block,),
        in_specs=[
            rows_in,
            rows_in,
            pl.BlockSpec((2 * units, width), lambda i: (part, 0), pipeline_mode=once),
            pl.BlockSpec((units, width), lambda i: (part, 0), pipeline_mode=once),
        ]
        + anywhere((*before, *waits)),
        out_specs=[
            pl.BlockSpec((block, units), lambda i: (i, part)),
            pl.BlockSpec((block, 2 * units), lambda i: (i, part)),
        ]
        + [transposed] * 3,
        input_output_aliases={4 + i: i for i in range(len(before))},
        compiler_params=kernel_params(),
        cost_estimate=cost(),
    )(x, cot, gate_up, down, *before, *waits)


def rows_product_kernel(a_ref, w_ref, *refs):
    out_ref = refs[-1]
    for rows in pieces(out_ref.shape[0], 512):
        out_ref[rows, :] = product(a_ref[rows, :], w_ref[...], NN).astype(BF16)


def rows_product(a, w, waits=(), us=0.3):
    count, depth = a.shape
    width = w.shape[1]
    block = 512
    return pl.pallas_call(
        rows_product_kernel,
        out_shape=jax.ShapeDtypeStruct((count, width), BF16),
        grid=(width // block,),
        in_specs=[resident((count, depth)), pl.BlockSpec((depth, block), lambda n: (0, n))]
        + anywhere(waits),
        out_specs=pl.BlockSpec((count, block), lambda n: (0, n)),
        compiler_params=kernel_params(),
        cost_estimate=cost(us),
    )(a, w, *waits)


def weight_grad_kernel(a_ref, b_ref, *refs):
    first_ref, upper_ref, lower_ref = refs[-3:]
    n = pl.program_id(0)
    height = upper_ref.shape[0]
    result = product(a_ref[...], b_ref[...], NN).astype(BF16)

    @pl.when(n < 2)
    def _():
        first_ref[0] = result[:height]
        first_ref[1] = result[height:]

    @pl.when(n >= 2)
    def _():
        upper_ref[...] = result[:height]
        lower_ref[...] = result[height:]


def weight_grad(a, b, waits=(), us=0.3):
    units, count = a.shape
    width = b.shape[1]
    height, half, block = units // 2, width // 2, width // 4
    lone = pl.BlockSpec((height, block), lambda n: (0, jnp.maximum(n - 2, 0)))
    return pl.pallas_call(
        weight_grad_kernel,
        out_shape=[
            jax.ShapeDtypeStruct((2, height, half), BF16),
            jax.ShapeDtypeStruct((height, half), BF16),
            jax.ShapeDtypeStruct((height, half), BF16),
        ],
        grid=(4,),
        in_specs=[
            resident((units, count)),
            pl.BlockSpec((count, block), lambda n: (0, n)),
        ]
        + anywhere(waits),
        out_specs=[
            pl.BlockSpec((2, height, block), lambda n: (0, 0, jnp.minimum(n, 1))),
            lone,
            lone,
        ],
        compiler_params=kernel_params(),
        cost_estimate=cost(us),
    )(a, b, *waits)


def parts_kernel(dims, lhs_ref, rhs_ref, first_sent, first_kept, second_sent, second_kept):
    n = pl.program_id(0)
    rows = first_sent.shape[1]
    result = product(lhs_ref[...], rhs_ref[...], dims).astype(BF16)
    blocks = [result[r * rows : (r + 1) * rows] for r in range(4)]

    @pl.when(n < 2)
    def _():
        first_kept[0], first_sent[0], first_kept[1], first_sent[1] = blocks

    @pl.when(n >= 2)
    def _():
        second_kept[0], second_kept[1], second_sent[0], second_sent[1] = blocks


def product_in_parts(lhs, rhs, dims, width):
    count, depth = lhs.shape
    if not square():
        if dims == NT:
            rhs = rhs[:, :depth]
        return product(lhs, rhs, dims).astype(BF16).reshape(lax.axis_size("ctx"), -1, width)
    block = width // 4
    if dims == NT:
        rhs_spec = pl.BlockSpec((block, depth), lambda n: (n, 0))
    else:
        rhs_spec = pl.BlockSpec((depth, block), lambda n: (0, n))
    shape = (2, count // 4, width // 2)
    first = pl.BlockSpec((*shape[:2], block), lambda n: (0, 0, jnp.minimum(n, 1)))
    second = pl.BlockSpec((*shape[:2], block), lambda n: (0, 0, jnp.maximum(n - 2, 0)))
    return pl.pallas_call(
        functools.partial(parts_kernel, dims),
        out_shape=[jax.ShapeDtypeStruct(shape, BF16)] * 4,
        grid=(4,),
        in_specs=[resident((count, depth)), rhs_spec],
        out_specs=[first, first, second, second],
        compiler_params=kernel_params(),
        cost_estimate=cost(),
    )(lhs, rhs)


def rows_grad_kernel(terms, *refs):
    out_ref = refs[-1]
    column = 0
    for i in range(terms):
        columns = pl.ds(column, refs[terms + i].shape[1])
        out_ref[:, columns] = product(refs[i][...], refs[terms + i][...], TN).astype(BF16)
        column += refs[terms + i].shape[1]
    out_ref[:, column:] = refs[2 * terms][...]


def rows_grad(terms, beside, waits=()):
    count, width = terms[0][0].shape
    block = 512
    total = sum(b.shape[1] for _, b in terms) + beside.shape[1]
    return pl.pallas_call(
        functools.partial(rows_grad_kernel, len(terms)),
        out_shape=jax.ShapeDtypeStruct((width, total), BF16),
        grid=(width // block,),
        in_specs=[pl.BlockSpec((count, block), lambda m: (0, m))] * len(terms)
        + [resident(b.shape) for _, b in terms]
        + [pl.BlockSpec((block, beside.shape[1]), lambda m: (m, 0))]
        + anywhere(waits),
        out_specs=pl.BlockSpec((block, total), lambda m: (m, 0)),
        compiler_params=kernel_params(),
        cost_estimate=cost(),
    )(*[a for a, _ in terms], *[b for _, b in terms], beside, *waits)


def turned(x, cosine, sine):
    return x * cosine + pltpu.roll(x, HEAD_WIDTH // 2, 1) * sine


def attend_kernel(
    query_in, key_in, value_in, cos_ref, sin_ref, bias_ref, query_ref, key_ref, value_ref, probs_ref, out_ref
):
    scale = HEAD_WIDTH ** (-0.5) * LOG2_E
    key = turned(key_in[...], cos_ref[...], sin_ref[...]).astype(BF16)
    value = value_in[...].astype(BF16)
    key_ref[...] = key
    value_ref[...] = value
    for h in range(GROUP):
        head = pl.ds(h * HEAD_WIDTH, HEAD_WIDTH)
        for rows in pieces(query_in.shape[0], 256):
            query = turned(query_in[rows, head], cos_ref[rows, :], sin_ref[rows, :]).astype(BF16)
            query_ref[rows, head] = query
            scores = product(query, key, NT) * scale + bias_ref[rows, :]
            weights = jnp.exp2(scores - jnp.max(scores, axis=1, keepdims=True))
            probs = (weights * (1.0 / jnp.sum(weights, axis=1, keepdims=True))).astype(BF16)
            probs_ref[h, rows, :] = probs
            out_ref[rows, head] = product(probs, value, NN).astype(BF16)


def attend(packed, cosine, sine, bias, kv_heads):
    count = packed.shape[0]
    wide, narrow = GROUP * HEAD_WIDTH, HEAD_WIDTH
    q_heads = kv_heads * GROUP

    def column(width, first):
        return pl.BlockSpec((count, width), lambda g: (0, first + g))

    def sized(*shape):
        return jax.ShapeDtypeStruct(shape, BF16)

    return pl.pallas_call(
        attend_kernel,
        out_shape=[
            sized(count, kv_heads * wide),
            sized(count, kv_heads * narrow),
            sized(count, kv_heads * narrow),
            sized(q_heads, count, count),
            sized(count, kv_heads * wide),
        ],
        grid=(kv_heads,),
        in_specs=[
            column(wide, 0),
            column(narrow, q_heads),
            column(narrow, q_heads + kv_heads),
            resident((count, HEAD_WIDTH)),
            resident((count, HEAD_WIDTH)),
            resident((count, count)),
        ],
        out_specs=[
            column(wide, 0),
            column(narrow, 0),
            column(narrow, 0),
            pl.BlockSpec((GROUP, count, count), lambda g: (g, 0, 0)),
            column(wide, 0),
        ],
        compiler_params=kernel_params(),
        cost_estimate=cost(),
    )(packed, packed, packed, cosine, sine, bias)


def attend_back_kernel(
    query_ref, key_ref, value_ref, probs_ref, d_out_ref, out_ref, cos_ref, sin_ref, *refs
):
    packed_ref = refs[-1]
    g = pl.program_id(0)
    kv_heads = pl.num_programs(0)
    scale = HEAD_WIDTH ** (-0.5)
    key, value = key_ref[...], value_ref[...]
    d_key = d_value = None
    for h in range(GROUP):
        head = pl.ds(h * HEAD_WIDTH, HEAD_WIDTH)
        for rows in pieces(query_ref.shape[0], 256):
            d_out = d_out_ref[rows, head]
            delta = jnp.sum(
                d_out.astype(F32) * out_ref[rows, head].astype(F32), axis=1, keepdims=True
            )
            probs = probs_ref[h, rows, :]
            d_scores = (probs.astype(F32) * (product(d_out, value, NT) - delta)).astype(BF16)
            d_query = turned(
                product(d_scores, key, NN) * scale, cos_ref[rows, :], -sin_ref[rows, :]
            )
            place = pl.multiple_of((g * GROUP + h) * HEAD_WIDTH, HEAD_WIDTH)
            packed_ref[rows, pl.ds(place, HEAD_WIDTH)] = d_query.astype(BF16)
            d_key_here = product(d_scores, query_ref[rows, head], TN)
            d_value_here = product(probs, d_out, TN)
            d_key = d_key_here if d_key is None else d_key + d_key_here
            d_value = d_value_here if d_value is None else d_value + d_value_here
    place = pl.multiple_of((kv_heads * GROUP + g) * HEAD_WIDTH, HEAD_WIDTH)
    packed_ref[:, pl.ds(place, HEAD_WIDTH)] = turned(
        d_key * scale, cos_ref[...], -sin_ref[...]
    ).astype(BF16)
    place = pl.multiple_of((kv_heads * (GROUP + 1) + g) * HEAD_WIDTH, HEAD_WIDTH)
    packed_ref[:, pl.ds(place, HEAD_WIDTH)] = d_value.astype(BF16)


def attend_back(queries, keys, values, probs, d_out, out, cosine, sine, waits=()):
    count = queries.shape[0]
    kv_heads = keys.shape[1] // HEAD_WIDTH
    wide, narrow = GROUP * HEAD_WIDTH, HEAD_WIDTH

    def column(width):
        return pl.BlockSpec((count, width), lambda g: (0, g))

    packed_shape = (count, kv_heads * (GROUP + 2) * HEAD_WIDTH)
    return pl.pallas_call(
        attend_back_kernel,
        out_shape=jax.ShapeDtypeStruct(packed_shape, BF16),
        grid=(kv_heads,),
        in_specs=[
            column(wide),
            column(narrow),
            column(narrow),
            pl.BlockSpec((GROUP, count, count), lambda g: (g, 0, 0)),
            column(wide),
            column(wide),
            resident((count, HEAD_WIDTH)),
            resident((count, HEAD_WIDTH)),
        ]
        + anywhere(waits),
        out_specs=pl.BlockSpec(packed_shape, lambda g: (0, 0)),
        compiler_params=kernel_params(),
        cost_estimate=cost(),
    )(queries, keys, values, probs, d_out, out, cosine, sine, *waits)


def square():
    return lax.axis_size("ctx") == 4


def swap(x, bit):
    return lax.ppermute(x, "ctx", [(i, i ^ bit) for i in range(4)])


def block_order():
    if square():
        return lax.axis_index("ctx") ^ jnp.arange(4, dtype=jnp.int32)
    return jnp.arange(lax.axis_size("ctx"), dtype=jnp.int32)


def gather_parts(x, *others):
    if not square():
        return [lax.all_gather(x, "ctx", axis=0, tiled=True)], [[(0, None)]]
    half = -(-x.shape[-1] // 256) * 128
    first, second = x[..., :half], x[..., half:]
    first_1 = swap(first, 1)
    second_2 = swap(second, 2)
    first_01, second_02 = jnp.stack([first, first_1]), jnp.stack([second, second_2])
    if others:
        first_01, second_02 = after(first_01, *others), after(second_02, *others)
    first_23 = swap(first_01, 2)
    second_13 = swap(second_02, 1)
    blocks = [[(0, None)], [(1, None), (4, 0)], [(3, 0), (2, None)], [(3, 1), (4, 1)]]
    return [x, first_1, second_2, first_23, second_13], blocks


def gather_ctx(x):
    if not square():
        return lax.all_gather(x, "ctx", axis=0)
    parts, blocks = gather_parts(x)
    return jnp.stack(
        [
            jnp.concatenate([parts[i] if lead is None else parts[i][lead] for i, lead in block], axis=-1)
            for block in blocks
        ]
    )


def scatter_sum_ctx(parts):
    if not square():
        return lax.psum_scatter(parts, "ctx", scatter_dimension=0, tiled=False).astype(F32)
    first_sent, first_kept, second_sent, second_kept = parts
    got_first = swap(first_sent, 1)
    got_second = swap(second_sent, 2)
    last_first = swap(sum_low(first_kept[1], got_first[1]), 2)
    last_second = swap(sum_low(second_kept[1], got_second[1]), 1)
    return jnp.concatenate(
        [
            first_kept[0].astype(F32) + got_first[0].astype(F32) + last_first.astype(F32),
            second_kept[0].astype(F32) + got_second[0].astype(F32) + last_second.astype(F32),
        ],
        axis=-1,
    )


def absolute_order(blocks):
    if not square():
        return [blocks[i] for i in range(lax.axis_size("ctx"))]
    place = lax.axis_index("ctx")
    low, high = (place & 1) == 1, (place & 2) == 2
    a = [jnp.where(low, blocks[r ^ 1], blocks[r]) for r in range(4)]
    return [jnp.where(high, a[r ^ 2], a[r]) for r in range(4)]


def own_row_order(blocks):
    if not square():
        return blocks
    return [jnp.stack([blocks[s][r ^ s] for r in range(4)]) for s in range(4)]


def exchange_ctx(x):
    if not square():
        got = lax.all_to_all(x, "ctx", 0, 0, tiled=False)
        return [got[i] for i in range(lax.axis_size("ctx"))]
    order = block_order()
    parts = [lax.dynamic_index_in_dim(x, order[r], 0, keepdims=False) for r in range(4)]
    got = [parts[0]] + [swap(parts[r], r) for r in range(1, 4)]
    return absolute_order(got)


def nothing_kernel(*refs):
    del refs


def after(x, *others):
    if not square():
        return x
    return pl.pallas_call(
        nothing_kernel,
        out_shape=jax.ShapeDtypeStruct(x.shape, x.dtype),
        in_specs=anywhere((x, *others)),
        out_specs=anywhere((x,))[0],
        input_output_aliases={0: 0},
        cost_estimate=pl.CostEstimate(flops=0, bytes_accessed=0, transcendentals=0),
    )(x, *others)


def unit_halves(*weights):
    units = weights[0].shape[0]
    if not square():
        halves = [[w[: units // 2], w[units // 2 :]] for w in weights]
    else:
        place = lax.axis_index("ctx")
        blocks = [w.reshape(4, units // 4, w.shape[1]) for w in weights]

        def half(w, order):
            return jnp.concatenate(
                [lax.dynamic_index_in_dim(w, place ^ r, 0, keepdims=False) for r in order]
            )

        halves = [[half(w, (1, 3)), half(w, (2, 0))] for w in blocks]
    return jnp.concatenate([h[i] for i in range(2) for h in halves])


def lay_heads_kernel(blocks, sizes, place_ref, weight_ref, gain_ref, *refs):
    parts, (qkv_ref, out_ref, gain_attn_ref, gain_ffn_ref) = refs[:-4], refs[-4:]
    q_cols, kv_cols, out_cols, places = sizes
    head_cols = q_cols + 2 * kv_cols
    gain_attn = gain_ffn = 0.0
    for r, block in enumerate(blocks):
        place = place_ref[r]
        rows = jnp.concatenate(
            [parts[i][...] if lead is None else parts[i][lead] for i, lead in block], axis=1
        ).astype(F32)
        first = 0
        for width, start in (
            (q_cols, 0),
            (kv_cols, q_cols * places),
            (kv_cols, (q_cols + kv_cols) * places),
        ):
            columns = pl.ds(pl.multiple_of(start + place * width, 128), width)
            piece = rows[:, first : first + width]
            qkv_ref[:, columns] = piece
            gain_attn += jnp.sum(piece * weight_ref[:, columns].astype(F32), axis=1, keepdims=True)
            first += width
        columns = pl.ds(pl.multiple_of(place * out_cols, 128), out_cols)
        out_ref[:, columns] = rows[:, head_cols : head_cols + out_cols]
        gain_ffn += rows[:, head_cols + out_cols : head_cols + out_cols + 1]
    gain_attn_ref[...] = gain_attn / gain_ref[...]
    gain_ffn_ref[...] = gain_ffn


def lay_heads(parts, blocks, sizes, w_qkv, norm_attn, waits):
    rows, qkv_cols = w_qkv.shape
    q_cols, kv_cols, out_cols, places = sizes
    whole = pl.BlockSpec(memory_space=pltpu.VMEM)
    column = jax.ShapeDtypeStruct((rows, 1), F32)
    return pl.pallas_call(
        functools.partial(lay_heads_kernel, blocks, sizes),
        out_shape=[
            jax.ShapeDtypeStruct((rows, qkv_cols), F32),
            jax.ShapeDtypeStruct((rows, out_cols * places), F32),
            column,
            column,
        ],
        in_specs=[pl.BlockSpec(memory_space=pltpu.SMEM)]
        + [whole] * (2 + len(parts))
        + anywhere(waits),
        out_specs=[whole] * 4,
        compiler_params=kernel_params(),
        cost_estimate=cost(),
    )(block_order(), w_qkv, norm_attn.astype(F32)[:, None], *parts, *waits)


def lay_out_kernel(place_ref, first_own, first_got, second_own, second_got, *refs):
    out_ref = refs[-1]
    step = pl.program_id(0)
    for i, block in enumerate((first_own, first_got, second_own, second_got)):

        @pl.when(step // 2 == i)
        def _(block=block):
            out_ref[...] = block[0].astype(F32)


def lay_out(first_own, first_got, second_own, second_got, waits, us):
    _, height, half = first_own.shape
    places = lax.axis_index("ctx") ^ jnp.array([0, 2, 1, 3, 0, 1, 2, 3], jnp.int32)

    def block_of(i):
        return pl.BlockSpec(
            (1, height, half), lambda g, where: (jnp.clip(g - 2 * i, 0, 1), 0, 0)
        )

    return pl.pallas_call(
        lay_out_kernel,
        out_shape=jax.ShapeDtypeStruct((4 * height, 2 * half), F32),
        grid_spec=pltpu.PrefetchScalarGridSpec(
            num_scalar_prefetch=1,
            grid=(8,),
            in_specs=[block_of(i) for i in range(4)] + anywhere(waits),
            out_specs=pl.BlockSpec((height, half), lambda g, where: (where[g], g // 4)),
        ),
        compiler_params=pltpu.CompilerParams(vmem_limit_bytes=32 * 2**20),
        cost_estimate=cost(us),
    )(places, first_own, first_got, second_own, second_got, *waits)


def sum_low(*terms):
    return sum(t.astype(F32) for t in terms).astype(BF16)


class SumCtx:
    def start_first(self, part):
        self.upper = part
        if not square():
            return
        self.got_first = swap(part[0], 1)
        self.got_third = swap(part[2], 2)

    def start_second(self, part):
        self.lower = part
        if not square():
            blocks = []
            for first, upper, lower in (self.upper, part):
                second = jnp.stack([upper, lower])
                blocks.append(jnp.concatenate([first, second], axis=-1))
            whole = jnp.concatenate(blocks)
            self.whole = lax.psum(whole.reshape(-1, whole.shape[-1]), "ctx").astype(F32)
            return
        self.got_second = swap(part[1], 2)

    def arrived(self, second=False):
        if not square():
            return ()
        return (self.got_second,) if second else (self.got_first, self.got_third)

    def step_2(self, *others):
        if not square():
            return ()
        first = sum_low(self.lower[0][0], self.got_first[1])
        second = sum_low(self.upper[1], self.got_third)
        self.last_first = swap(after(first, *others) if others else first, 2)
        self.last_second = swap(after(second, *others) if others else second, 1)
        return (self.last_first, self.last_second)

    def step_3(self, *others):
        if not square():
            return ()
        self.first = sum_low(self.lower[0][1], self.got_first[0], self.last_first)
        self.second = sum_low(self.lower[2], self.got_second, self.last_second)
        if others:
            self.first = after(self.first, *others)
            self.second = after(self.second, *others)
        self.first_2 = swap(self.first, 2)
        self.second_1 = swap(self.second, 1)
        return (self.first_2, self.second_1)

    def step_4(self, *others):
        if not square():
            return ()
        self.first_02 = jnp.stack([self.first, self.first_2])
        self.second_01 = jnp.stack([self.second, self.second_1])
        if others:
            self.first_02 = after(self.first_02, *others)
            self.second_01 = after(self.second_01, *others)
        self.first_13 = swap(self.first_02, 1)
        self.second_23 = swap(self.second_01, 2)
        return (self.first_13, self.second_23)

    def result(self, waits=(), us=0.3):
        if not square():
            return self.whole
        return lay_out(self.first_02, self.first_13, self.second_01, self.second_23, waits, us)


def local(
    tokens,
    cotangent,
    norm_attn,
    w_qkv,
    w_out,
    norm_ffn,
    w_gate,
    w_up,
    w_down,
    seq_len,
    window,
    global_pos,
):
    places = lax.axis_size("ctx")
    place = lax.axis_index("ctx")
    shards = lax.axis_size("fsdp")
    rows = tokens.shape[1]
    width = tokens.shape[2]
    count = places * rows
    kv_heads = KEY_VALUE_HEADS // places
    q_heads = kv_heads * GROUP
    q_cols = q_heads * HEAD_WIDTH
    kv_cols = kv_heads * HEAD_WIDTH
    q_all = QUERY_HEADS * HEAD_WIDTH
    kv_all = KEY_VALUE_HEADS * HEAD_WIDTH
    out_cols = width // places
    length = seq_len[0]
    window_now = window[0]
    global_here = global_pos[0]
    x_own = tokens[0]
    cot_own = cotangent[0]

    head_cols = q_cols + 2 * kv_cols
    weights_mine = jnp.concatenate(
        [
            lax.dynamic_slice_in_dim(w_qkv, place * q_cols, q_cols, 1),
            lax.dynamic_slice_in_dim(w_qkv, q_all + place * kv_cols, kv_cols, 1),
            lax.dynamic_slice_in_dim(w_qkv, q_all + kv_all + place * kv_cols, kv_cols, 1),
            lax.dynamic_slice_in_dim(w_out, place * out_cols, out_cols, 1),
        ],
        axis=1,
    )
    weights = lax.all_gather(weights_mine, "fsdp", axis=0, tiled=True)
    gains = lax.all_gather(jnp.stack([norm_attn, norm_ffn]), "fsdp", axis=1, tiled=True)
    gain_attn = gains[0].astype(F32)
    gain_ffn = gains[1].astype(F32)
    x_parts, x_blocks = gather_parts(x_own, gains)
    cot_all = lax.all_gather(after(cot_own, *x_parts[-2:]), "fsdp", axis=0, tiled=True)
    gate_up = unit_halves(w_gate, w_up)
    down = unit_halves(w_down)
    w_rows = jnp.concatenate(
        exchange_ctx(weights[:, head_cols:].reshape(places, q_cols, out_cols)), axis=1
    )

    normed_low, packed = norm_project(x_parts, x_blocks, gain_attn[None, :], weights, head_cols)
    order = block_order()
    positions = (order[:, None] * rows + jnp.arange(rows, dtype=jnp.int32)[None, :]).reshape(count)
    cosine, sine = rope_tables(positions)
    is_global = jnp.any(positions[:, None] == global_here[None, :], axis=1)
    allowed = (
        (positions[None, :] <= positions[:, None])
        & (positions[None, :] < length)
        & (
            (positions[:, None] - positions[None, :] < window_now)
            | is_global[:, None]
            | is_global[None, :]
        )
    )
    bias = jnp.where(allowed, 0.0, NEGATIVE_FILLER)
    queries, keys, values, probs, attended_low = attend(packed, cosine, sine, bias, kv_heads)
    branch = scatter_sum_ctx(product_in_parts(attended_low, w_rows, NN, width))

    x_full = x_own.astype(F32)
    middle = x_full + branch
    inv_ffn = lax.rsqrt(jnp.mean(middle * middle, axis=-1, keepdims=True) + NORM_EPS)
    normed_ffn = middle * inv_ffn
    ffn_low = (normed_ffn * gain_ffn[None, :]).astype(BF16)
    ffn_all = lax.all_gather(after(ffn_low, cot_all), "fsdp", axis=0, tiled=True)
    attended_all = jnp.concatenate(
        absolute_order(own_row_order(gather_ctx(attended_low.reshape(places, rows, q_cols)))), axis=-1
    ).reshape(count, q_all)
    sum_down, sum_gate, sum_up = SumCtx(), SumCtx(), SumCtx()
    hidden, d_both, *first_t = hidden_grads(ffn_all, cot_all, gate_up, down, 0, (), (attended_all,))
    down_a = weight_grad(first_t[0], cot_all)
    sum_down.start_first(down_a)
    hidden, d_both, *second_t = hidden_grads(
        ffn_all, cot_all, gate_up, down, 1, (hidden, d_both), down_a
    )
    gate_a = weight_grad(first_t[1], ffn_all, (second_t[0], *sum_down.arrived()))
    sum_gate.start_first(gate_a)
    d_ffn_part = rows_product(d_both, gate_up, gate_a)
    d_ffn = lax.psum_scatter(d_ffn_part, "fsdp", scatter_dimension=0, tiled=True)
    down_b = weight_grad(second_t[0], cot_all, (d_ffn_part, *sum_gate.arrived()))
    sum_down.start_second(down_b)
    down_2 = sum_down.step_2()
    up_a = weight_grad(first_t[2], ffn_all, down_b, 300)
    sum_up.start_first(up_a)
    ffn_part = rows_product(hidden, down, (*up_a, *down_2, *sum_down.arrived(True)), 300)
    gate_b = weight_grad(second_t[1], ffn_all, (ffn_part, *sum_up.arrived()), 300)
    sum_gate.start_second(gate_b)
    gate_2 = sum_gate.step_2()
    down_3 = sum_down.step_3()
    up_b = weight_grad(second_t[2], ffn_all, gate_b, 300)
    sum_up.start_second(up_b)
    d_ffn = after(d_ffn, *down_3, *gate_2)
    ffn_sum = lax.psum_scatter(ffn_part, "fsdp", scatter_dimension=0, tiled=True)
    layer_out = middle + ffn_sum.astype(F32)

    d_ffn = d_ffn.astype(F32)
    scaled = d_ffn * gain_ffn[None, :]
    d_gain_ffn = jnp.sum(d_ffn * normed_ffn, axis=0)
    d_middle = cot_own.astype(F32) + inv_ffn * (
        scaled - normed_ffn * jnp.mean(scaled * normed_ffn, axis=-1, keepdims=True)
    )
    d_branch_own = d_middle.astype(BF16)
    d_branch = gather_ctx(d_branch_own).reshape(count, width)
    d_attended = jnp.einsum("te,fe->tf", d_branch, w_rows, preferred_element_type=F32).astype(BF16)
    up_2 = sum_up.step_2(d_branch)
    gate_3 = sum_gate.step_3(d_branch)
    down_4 = sum_down.step_4(d_branch)
    up_3 = sum_up.step_3()
    d_packed = attend_back(
        queries, keys, values, probs, d_attended, attended_low, cosine, sine
    )
    d_weights = rows_grad(
        [
            (normed_low, d_packed),
            (attended_all, lax.dynamic_slice_in_dim(d_branch, place * out_cols, out_cols, 1)),
        ],
        jnp.broadcast_to(d_gain_ffn.astype(BF16)[:, None], (width, 128)),
    )
    d_weights = after(d_weights, ffn_sum)
    d_attn_parts = product_in_parts(after(d_packed, d_weights, *up_2, *gate_3), weights, NT, width)
    scattered = lax.psum_scatter(d_weights, "fsdp", scatter_dimension=0, tiled=True)
    d_attn = scatter_sum_ctx(d_attn_parts)
    d_attn = after(d_attn, *down_4, *up_3)
    sum_gate.step_4(d_weights)
    sum_up.step_4(d_weights)
    inv_own = lax.rsqrt(jnp.mean(x_full * x_full, axis=-1, keepdims=True) + NORM_EPS)
    normed_attn = x_full * inv_own
    scaled_attn = d_attn * gain_attn[None, :]
    d_tokens = d_middle + inv_own * (
        scaled_attn - normed_attn * jnp.mean(scaled_attn * normed_attn, axis=-1, keepdims=True)
    )

    grad_down = sum_down.result(d_attn_parts, 300)
    parts, blocks = gather_parts(after(scattered, grad_down))
    if not square():
        rows_here = scattered.shape[0]
        parts = [parts[0].reshape(places, rows_here, -1)]
        blocks = [[(0, i)] for i in range(places)]
    grad_up = sum_up.result()
    grad_qkv, grad_out, grad_gain_attn, grad_gain_ffn = lay_heads(
        parts, blocks, (q_cols, kv_cols, out_cols, places), w_qkv, norm_attn, (grad_up,)
    )
    return (
        layer_out.astype(BF16)[None],
        d_tokens[None],
        grad_gain_attn[:, 0],
        grad_qkv,
        grad_out,
        grad_gain_ffn[:, 0],
        sum_gate.result(),
        grad_up,
        grad_down,
    )


def solution(mesh):
    return jax.shard_map(
        local,
        mesh=mesh,
        in_specs=(
            P("fsdp", "ctx", None),
            P("fsdp", "ctx", None),
            P("fsdp"),
            P("fsdp", None),
            P("fsdp", None),
            P("fsdp"),
            P("fsdp", None),
            P("fsdp", None),
            P("fsdp", None),
            P("fsdp"),
            P("fsdp"),
            P("fsdp", None),
        ),
        out_specs=(
            P("fsdp", "ctx", None),
            P("fsdp", "ctx", None),
            P("fsdp"),
            P("fsdp", None),
            P("fsdp", None),
            P("fsdp"),
            P("fsdp", None),
            P("fsdp", None),
            P("fsdp", None),
        ),
        check_vma=False,
    )
```

time: 904 us -> 610 us (0.67)
  waiting for transfers between devices: 510 us -> 189 us
  Pallas kernels: 0 us -> 189 us
  matrix products: 152 us -> 4.98 us
  local copies, waits for them, and re-layouts: 72.5 us -> 32.9 us
  starting transfers between devices: 41.1 us -> 59.7 us
    pallas_call x0 -> x39, Pallas kernels: none -> 189 us  [the longest x6 46.4 us: weight_grad(): pl.pallas_call(weight_grad_kernel, out_shape=[jax.ShapeDtypeStruct((2, he...]
    dot_general x20 -> x0, matrix products: 147 us -> none  [the longest x3 31.5 us: local(): jnp.einsum('tf,td->fd', a, b, preferred_element_type=F32).astype(BF16)]
    psum x1 -> x0, waiting for transfers between devices: 120 us -> none  [local(): lax.psum(jnp.einsum('tf,td->fd', a, b, preferred_element_type=F32).astype...]
    all_gather x4 -> x3, waiting for transfers between devices: 107 us -> 36 us  [the longest x1 21.8 us: local(): lax.all_gather(after(ffn_low, cot_all), 'fsdp', axis=0, tiled=True)]
    reduce_scatter x3 -> x2, waiting for transfers between devices: 66.5 us -> 0.01 us  [the longest x1 0.01 us: local(): lax.psum_scatter(d_ffn_part, 'fsdp', scatter_dimension=0, tiled=True)]
    reduce_scatter x1, waiting for transfers between devices: 60.2 us -> 0.01 us  [local(): lax.psum_scatter(ffn_part, 'fsdp', scatter_dimension=0, tiled=True)]
    ppermute x31 -> x54, starting transfers between devices: 40.6 us -> 59 us  [swap(): return lax.ppermute(x, 'ctx', [(i, i ^ bit) for i in range(4)])]
    sub x1 -> x0, other arithmetic: 11.4 us -> none  [local(): weights = jnp.where(allowed[None, None], jnp.exp(scores - top), 0.0)]
  transfers between devices with their start and end apart: 40 -> 60, of which waited for: 28 -> 26; matrix products, arithmetic and copies ran while one was open for 22% -> 18% of each run, Pallas kernels for 0% -> 25%
where the time goes in v2:
time: 610 us; the launch traced here: 599 us
  waiting for transfers between devices  189 us (31%)
  Pallas kernels  189 us (31%)
  other arithmetic  86.5 us (14%)
  starting transfers between devices  59.7 us (10%)
  local copies, waits for them, and re-layouts  32.9 us (5%)
  between operations  24.4 us (4%)
  blocking collectives  12.1 us (2%)
    ppermute x54, waiting for transfers between devices, swap(): return lax.ppermute(x, 'ctx', [(i, i ^ bit) for i in range(4)])  153 us
    ppermute x54, starting transfers between devices, swap(): return lax.ppermute(x, 'ctx', [(i, i ^ bit) for i in range(4)])  59 us
    pallas_call x6, Pallas kernels, weight_grad(): pl.pallas_call(weight_grad_kernel, out_shape=[jax.ShapeDtypeStruct((2, he...  46.4 us
    pallas_call x2, Pallas kernels, hidden_grads(): pl.pallas_call(hidden_kernel, out_shape=[jax.ShapeDtypeStruct((count, 2 *...  34.4 us
    convert_element_type x16, other arithmetic, sum_low(): return sum((t.astype(F32) for t in terms)).astype(BF16)  31.2 us
    pallas_call x2, Pallas kernels, rows_product(): pl.pallas_call(rows_product_kernel, out_shape=jax.ShapeDtypeStruct((count...  28.9 us
    all_gather x1, waiting for transfers between devices, local(): lax.all_gather(after(ffn_low, cot_all), 'fsdp', axis=0, tiled=True)  21.8 us
    pallas_call x3, Pallas kernels, lay_out(): pl.pallas_call(lay_out_kernel, out_shape=jax.ShapeDtypeStruct((4 * height...  18.8 us
  transfers between devices with their start and end apart: 60, of which 26 were waited for; matrix products, arithmetic and copies ran while one was open for 18% of the time, Pallas kernels for 25%

profile of v2, /device:TPU:0, one launch (start us, length us, event | category | flops | bytes accessed | tf_op | source)
XLA Modules:
  0.0 598.9 jit_solution(11740910342808918396)
XLA Ops:
  15.2 12.1 %all_gather.12.refs_1_ = bf16[2,2048]{1,0:T(2,128)(2,1)} all-gather(bf16[2,256]{1,0:T(2,128)(2,1)S(1)} %pad_maximum_fusion.25), channel_id=1, replica_groups=mesh['ctx'=4,'fsdp'=8] {'fsdp'}, dimensions={1}, use_global_device_ids=true | all-gather | bytes 9216 | tf_op jit(solution)/shard_map/all_gather | solution.py:744
  31.3 17.0 %collective-permute-done.2.refs_3_.refs_1_ = bf16[2,192,1024]{2,1,0:T(8,128)(2,1)S(1)} collective-permute-done((bf16[2,192,1024]{2,1,0:T(8,128)(2,1)}, bf16[2,192,1024]{2,1,0:T(8,128)(2,1)S(1)}, u32[]{:S(2)}, u32[]{:S(2)}) %collective-permute-start.2) | collective-permute-done | bytes 786464 | tf_op jit(solution)/shard_map/ppermute | solution.py:436
  63.8 14.2 %all-gather.4.cloned.1.call-done.refs_6_.rhs_ref = bf16[2048,1536]{1,0:T(8,128)(2,1)} async-done(((bf16[256,1536]{1,0:T(8,128)(2,1)}), bf16[2048,1536]{1,0:T(8,128)(2,1)}) %all-gather.4.cloned.1.call-update) | async-done | bytes 6291472 | tf_op jit(solution)/shard_map/all_gather | solution.py:743
  88.0 9.1 %shard_map.216 = (bf16[768,2048]{1,0:T(8,128)(2,1)}, f32[768,1024]{1,0:T(8,128)}) custom-call(bf16[192,2048]{1,0:T(8,128)(2,1)} %bitcast.189, bf16[192,1024]{1,0:T(8,128)(2,1)} %copy-done.54, bf16[192,1024]{1,0:T(8,128)(2,1)} %copy-done.55, bf16[2,192,1024]{2,1,0:T(8,128)(2,1)} %copy-done.40, bf16[2,192,1024]{2,1,0:T(8,128)(2,1)} %copy-done.41, ...), custom_call_target="tpu_custom_call" | custom-call | flops 300000000 | bytes 1107000 | tf_op jit(solution)/shard_map/pallas_call | solution.py:96
  97.1 11.4 %shard_map.217 = (bf16[768,512]{1,0:T(8,128)(2,1)}, bf16[768,256]{1,0:T(8,128)(2,1)}, bf16[768,256]{1,0:T(8,128)(2,1)}, bf16[4,768,768]{2,1,0:T(8,128)(2,1)}, bf16[768,512]{1,0:T(8,128)(2,1)}) custom-call(f32[768,1024]{1,0:T(8,128)} %get-tuple-element.56.query_in.key_in.value_in, f32[768,1024]{1,0:T(8,128)} %get-tuple-element.56.query_in.key_in.value_in, ...), custom_call_target="tpu_custom_call" | custom-call | flops 300000000 | bytes 1107000 | tf_op jit(solution)/shard_map/pallas_call | solution.py:336
  111.9 5.8 shard_map.218
  120.7 16.4 %collective-permute-done.9 = bf16[2,192,1024]{2,1,0:T(8,128)(2,1)S(1)} collective-permute-done((bf16[2,192,1024]{2,1,0:T(8,128)(2,1)}, bf16[2,192,1024]{2,1,0:T(8,128)(2,1)S(1)}, u32[]{:S(2)}, u32[]{:S(2)}) %collective-permute-start.9) | collective-permute-done | bytes 786464 | tf_op jit(solution)/shard_map/ppermute | solution.py:436
  142.6 5.7 collective-permute-done.10
  165.8 5.4 collective-permute-done.11
  175.8 14.1 %collective-permute-done.12 = bf16[2,4,192,256]{3,2,1,0:T(8,128)(2,1)S(1)} collective-permute-done((bf16[2,4,192,256]{3,2,1,0:T(8,128)(2,1)S(1)}, bf16[2,4,192,256]{3,2,1,0:T(8,128)(2,1)S(1)}, u32[]{:S(2)}, u32[]{:S(2)}) %collective-permute-start.12) | collective-permute-done | bytes 786464 | tf_op jit(solution)/shard_map/ppermute | solution.py:436
  194.0 21.8 %all-gather.8.cloned.1.call-done.x_ref.b_ref = bf16[1536,2048]{1,0:T(8,128)(2,1)} async-done(((bf16[192,2048]{1,0:T(8,128)(2,1)}), bf16[1536,2048]{1,0:T(8,128)(2,1)}) %all-gather.8.cloned.1.call-update) | async-done | bytes 6291472 | tf_op jit(solution)/shard_map/all_gather | solution.py:778
  215.8 17.2 %shard_map.221 = (bf16[1536,1024]{1,0:T(8,128)(2,1)}, bf16[1536,2048]{1,0:T(8,128)(2,1)}, bf16[512,1536]{1,0:T(8,128)(2,1)}, bf16[512,1536]{1,0:T(8,128)(2,1)}, bf16[512,1536]{1,0:T(8,128)(2,1)}) custom-call(bf16[1536,2048]{1,0:T(8,128)(2,1)} %all-gather.8.cloned.1.call-done.x_ref.b_ref, ...), custom_call_target="tpu_custom_call" | custom-call | flops 300000000 | bytes 1107000 | tf_op jit(solution)/shard_map/pallas_call | solution.py:140
  233.0 7.7 %shard_map.222 = (bf16[2,256,1024]{2,1,0:T(8,128)(2,1)}, bf16[256,1024]{1,0:T(8,128)(2,1)}, bf16[256,1024]{1,0:T(8,128)(2,1)}) custom-call(bf16[512,1536]{1,0:T(8,128)(2,1)} %get-tuple-element.64.a_ref, bf16[1536,2048]{1,0:T(8,128)(2,1)} %all-gather.6.cloned.1.call-done.refs_1_.cot_ref.b_ref), custom_call_target="tpu_custom_call" | custom-call | flops 300000000 | bytes 1107000 | tf_op jit(solution)/shard_map/pallas_call | solution.py:210
  243.6 17.2 %shard_map.223 = (bf16[1536,1024]{1,0:T(8,128)(2,1)}, bf16[1536,2048]{1,0:T(8,128)(2,1)}, bf16[512,1536]{1,0:T(8,128)(2,1)}, bf16[512,1536]{1,0:T(8,128)(2,1)}, bf16[512,1536]{1,0:T(8,128)(2,1)}) custom-call(bf16[1536,2048]{1,0:T(8,128)(2,1)} %all-gather.8.cloned.1.call-done.x_ref.b_ref, ...), custom_call_target="tpu_custom_call", output_to_operand_aliasing={{0}: (4, {}), {1}: (5, {})} | custom-call | flops 300000000 | bytes 1107000 | tf_op jit(solution)/shard_map/pallas_call | solution.py:140
  267.2 7.7 %shard_map.224 = (bf16[2,256,1024]{2,1,0:T(8,128)(2,1)}, bf16[256,1024]{1,0:T(8,128)(2,1)}, bf16[256,1024]{1,0:T(8,128)(2,1)}) custom-call(bf16[512,1536]{1,0:T(8,128)(2,1)} %get-tuple-element.72.a_ref, bf16[1536,2048]{1,0:T(8,128)(2,1)} %all-gather.8.cloned.1.call-done.x_ref.b_ref, bf16[512,1536]{1,0:T(8,128)(2,1)} %get-tuple-element.70.refs_0_.a_ref, ...), custom_call_target="tpu_custom_call" | custom-call | flops 300000000 | bytes 1107000 | tf_op jit(solution)/shard_map/pallas_call | solution.py:210
  281.8 18.3 %shard_map.225.refs_0_ = bf16[1536,2048]{1,0:T(8,128)(2,1)} custom-call(bf16[1536,2048]{1,0:T(8,128)(2,1)} %get-tuple-element.71.a_ref, bf16[2048,2048]{1,0:T(8,128)(2,1)} %copy-done.13, bf16[2,256,1024]{2,1,0:T(8,128)(2,1)} %get-tuple-element.73.refs_0_, bf16[256,1024]{1,0:T(8,128)(2,1)} %get-tuple-element.74.refs_1_, ...), custom_call_target="tpu_custom_call" | custom-call | flops 300000000 | bytes 1107000 | tf_op jit(solution)/shard_map/pallas_call | solution.py:176
  304.6 7.6 %shard_map.226 = (bf16[2,256,1024]{2,1,0:T(8,128)(2,1)}, bf16[256,1024]{1,0:T(8,128)(2,1)}, bf16[256,1024]{1,0:T(8,128)(2,1)}) custom-call(bf16[512,1536]{1,0:T(8,128)(2,1)} %get-tuple-element.70.refs_0_.a_ref, bf16[1536,2048]{1,0:T(8,128)(2,1)} %all-gather.6.cloned.1.call-done.refs_1_.cot_ref.b_ref, bf16[1536,2048]{1,0:T(8,128)(2,1)} %shard_map.225.refs_0_, ...), custom_call_target="tpu_custom_call" | custom-call | flops 300000000 | bytes 1107000 | tf_op jit(solution)/shard_map/pallas_call | solution.py:210
  316.3 7.8 %shard_map.227 = (bf16[2,256,1024]{2,1,0:T(8,128)(2,1)}, bf16[256,1024]{1,0:T(8,128)(2,1)}, bf16[256,1024]{1,0:T(8,128)(2,1)}) custom-call(bf16[512,1536]{1,0:T(8,128)(2,1)} %get-tuple-element.69.a_ref, bf16[1536,2048]{1,0:T(8,128)(2,1)} %all-gather.8.cloned.1.call-done.x_ref.b_ref, bf16[2,256,1024]{2,1,0:T(8,128)(2,1)} %get-tuple-element.76.refs_0_, ...), custom_call_target="tpu_custom_call" | custom-call | flops 299999985664 | bytes 1107000064 | tf_op jit(solution)/shard_map/pallas_call | solution.py:210
  333.6 7.1 %collective-permute-done.21.refs_5_ = bf16[256,1024]{1,0:T(8,128)(2,1)} collective-permute-done((bf16[256,1024]{1,0:T(8,128)(2,1)}, bf16[256,1024]{1,0:T(8,128)(2,1)}, u32[]{:S(2)}, u32[]{:S(2)}) %collective-permute-start.21) | collective-permute-done | bytes 524320 | tf_op jit(solution)/shard_map/ppermute | solution.py:436
  343.8 10.7 %shard_map.228.refs_0_ = bf16[1536,2048]{1,0:T(8,128)(2,1)} custom-call(bf16[1536,1024]{1,0:T(8,128)(2,1)} %get-tuple-element.68.a_ref, bf16[1024,2048]{1,0:T(8,128)(2,1)} %pad_maximum_fusion.down_ref.w_ref, bf16[2,256,1024]{2,1,0:T(8,128)(2,1)} %get-tuple-element.79.refs_0_, bf16[256,1024]{1,0:T(8,128)(2,1)} %get-tuple-element.80.refs_1_, ...), custom_call_target="tpu_custom_call" | custom-call | flops 299999985664 | bytes 1107000064 | tf_op jit(solution)/shard_map/pallas_call | solution.py:176
  357.6 7.8 %shard_map.229 = (bf16[2,256,1024]{2,1,0:T(8,128)(2,1)}, bf16[256,1024]{1,0:T(8,128)(2,1)}, bf16[256,1024]{1,0:T(8,128)(2,1)}) custom-call(bf16[512,1536]{1,0:T(8,128)(2,1)} %get-tuple-element.82.a_ref, bf16[1536,2048]{1,0:T(8,128)(2,1)} %all-gather.8.cloned.1.call-done.x_ref.b_ref, bf16[1536,2048]{1,0:T(8,128)(2,1)} %shard_map.228.refs_0_, ...), custom_call_target="tpu_custom_call" | custom-call | flops 299999985664 | bytes 1107000064 | tf_op jit(solution)/shard_map/pallas_call | solution.py:210
  369.5 7.7 %shard_map.234 = (bf16[2,256,1024]{2,1,0:T(8,128)(2,1)}, bf16[256,1024]{1,0:T(8,128)(2,1)}, bf16[256,1024]{1,0:T(8,128)(2,1)}) custom-call(bf16[512,1536]{1,0:T(8,128)(2,1)} %get-tuple-element.89.a_ref, bf16[1536,2048]{1,0:T(8,128)(2,1)} %all-gather.8.cloned.1.call-done.x_ref.b_ref, bf16[2,256,1024]{2,1,0:T(8,128)(2,1)} %get-tuple-element.83.refs_0_, ...), custom_call_target="tpu_custom_call" | custom-call | flops 299999985664 | bytes 1107000064 | tf_op jit(solution)/shard_map/pallas_call | solution.py:210
  377.2 5.4 collective-permute-done.26.refs_3_
  406.0 7.0 %collective-permute-done.30 = bf16[2,192,1024]{2,1,0:T(8,128)(2,1)S(1)} collective-permute-done((bf16[2,192,1024]{2,1,0:T(8,128)(2,1)S(1)}, bf16[2,192,1024]{2,1,0:T(8,128)(2,1)S(1)}, u32[]{:S(2)}, u32[]{:S(2)}) %collective-permute-start.30) | collective-permute-done | bytes 786464 | tf_op jit(solution)/shard_map/ppermute | solution.py:436
  431.6 10.3 %shard_map.231.refs_2_.refs_0_ = bf16[768,1024]{1,0:T(8,128)(2,1)} custom-call(bf16[768,512]{1,0:T(8,128)(2,1)} %get-tuple-element.84.query_ref, bf16[768,256]{1,0:T(8,128)(2,1)} %get-tuple-element.85.key_ref, bf16[768,256]{1,0:T(8,128)(2,1)} %get-tuple-element.86.value_ref, bf16[4,768,768]{2,1,0:T(8,128)(2,1)} %get-tuple-element.87.probs_ref, ...), custom_call_target="tpu_custom_call" | custom-call | flops 300000000 | bytes 1107000 | tf_op jit(solution)/shard_map/pallas_call | solution.py:410
  445.0 10.0 %shard_map.232.refs_0_ = bf16[2048,1664]{1,0:T(8,128)(2,1)} custom-call(bf16[768,2048]{1,0:T(8,128)(2,1)} %get-tuple-element.88.refs_0_, bf16[768,2048]{1,0:T(8,128)(2,1)} %pad_maximum_fusion.1.refs_0_.refs_1_, bf16[768,1024]{1,0:T(8,128)(2,1)} %shard_map.231.refs_2_.refs_0_, bf16[768,512]{1,0:T(8,128)(2,1)} %constant_dynamic-slice_fusion.refs_3_, ...), custom_call_target="tpu_custom_call" | custom-call | flops 300000000 | bytes 1107000 | tf_op jit(solution)/shard_map/pallas_call | solution.py:287
  456.9 8.0 %shard_map.240 = (bf16[2,192,1024]{2,1,0:T(8,128)(2,1)}, bf16[2,192,1024]{2,1,0:T(8,128)(2,1)}, bf16[2,192,1024]{2,1,0:T(8,128)(2,1)}, bf16[2,192,1024]{2,1,0:T(8,128)(2,1)}) custom-call(bf16[768,1024]{1,0:T(8,128)(2,1)} %shard_map.239.lhs_ref, bf16[2048,1536]{1,0:T(8,128)(2,1)} %all-gather.4.cloned.1.call-done.refs_6_.rhs_ref), custom_call_target="tpu_custom_call" | custom-call | flops 300000000 | bytes 1107000 | tf_op jit(solution)/shard_map/pallas_call | solution.py:262
  486.4 17.9 %collective-permute-done.43.refs_3_ = bf16[256,1024]{1,0:T(8,128)(2,1)} collective-permute-done((bf16[256,1024]{1,0:T(8,128)(2,1)}, bf16[256,1024]{1,0:T(8,128)(2,1)}, u32[]{:S(2)}, u32[]{:S(2)}) %collective-permute-start.43) | collective-permute-done | bytes 524320 | tf_op jit(solution)/shard_map/ppermute | solution.py:436
  513.5 5.8 collective-permute-done.45.refs_4_
  526.8 8.5 %shard_map.252 = f32[1024,2048]{1,0:T(8,128)} custom-call(s32[8]{0:T(128)S(1)} %broadcast_xor_fusion.place_ref, bf16[2,256,1024]{2,1,0:T(8,128)(2,1)} %shard_map.250.first_own, bf16[2,256,1024]{2,1,0:T(8,128)(2,1)} %collective-permute-done.52.first_got, bf16[2,256,1024]{2,1,0:T(8,128)(2,1)} %shard_map.251.second_own, ...), custom_call_target="tpu_custom_call" | custom-call | flops 300000000 | bytes 1107000 | tf_op jit(solution)/shard_map/pallas_call | solution.py:618
  535.3 6.9 %collective-permute-done.40 = bf16[192,1024]{1,0:T(8,128)(2,1)} collective-permute-done((bf16[192,1024]{1,0:T(8,128)(2,1)}, bf16[192,1024]{1,0:T(8,128)(2,1)}, u32[]{:S(2)}, u32[]{:S(2)}) %collective-permute-start.40) | collective-permute-done | bytes 393248 | tf_op jit(solution)/shard_map/ppermute | solution.py:436
  582.7 6.0 shard_map.249
  (407 shorter events, 238.8 us)
Async XLA Ops:
  7.2 70.8 %all-gather.4.cloned.1.call-start = ((), (), s32[]{:S(2)}) async-start(), calls=%async_computation.3 | async-start | bytes 7077888 | tf_op jit(solution)/shard_map/all_gather | solution.py:743
  10.3 143.3 %all-gather.6.cloned.1.call-start = ((), (), s32[]{:S(2)}) async-start(), calls=%async_computation.4 | async-start | bytes 7077888 | tf_op jit(solution)/shard_map/all_gather | solution.py:748
  50.4 165.4 %all-gather.8.cloned.1.call-start = ((), (), s32[]{:S(2)}) async-start(), calls=%async_computation.5 | async-start | bytes 7077888 | tf_op jit(solution)/shard_map/all_gather | solution.py:778
  81.0 27.6 %collective-permute-start.4 = (bf16[512,512]{1,0:T(8,128)(2,1)}, bf16[512,512]{1,0:T(8,128)(2,1)S(1)}, u32[]{:S(2)}, u32[]{:S(2)}) collective-permute-start(bf16[512,512]{1,0:T(8,128)(2,1)} %get-tuple-element.119), channel_id=1, source_target_pairs={{0,24},{8,16},{16,8},{24,0},{1,25},{9,17},{17,9},{25,1},{2,26},{10... | collective-permute-start | bytes 1572872 | tf_op jit(solution)/shard_map/ppermute | solution.py:436
  83.3 25.2 %collective-permute-start.5 = (bf16[512,512]{1,0:T(8,128)(2,1)}, bf16[512,512]{1,0:T(8,128)(2,1)}, u32[]{:S(2)}, u32[]{:S(2)}) collective-permute-start(bf16[512,512]{1,0:T(8,128)(2,1)} %get-tuple-element.118), channel_id=1, source_target_pairs={{0,16},{8,24},{16,0},{24,8},{1,17},{9,25},{17,1},{25,9},{2,18},{10... | collective-permute-start | bytes 1572872 | tf_op jit(solution)/shard_map/ppermute | solution.py:436
  153.6 229.0 %reduce-scatter.6.cloned.1.call-start = ((), (), s32[]{:S(2)}) async-start(), calls=%async_computation.7 | async-start | bytes 7077888 | tf_op jit(solution)/shard_map/reduce_scatter | solution.py:792
  240.6 25.5 %collective-permute-start.15 = (bf16[2,256,1024]{2,1,0:T(8,128)(2,1)}, bf16[2,256,1024]{2,1,0:T(8,128)(2,1)S(1)}, u32[]{:S(2)}, u32[]{:S(2)}) collective-permute-start(bf16[2,256,1024]{2,1,0:T(8,128)(2,1)} %get-tuple-element.65.refs_2_), channel_id=1, source_target_pairs={{0,8},{8,0},{16,24},{24,16},{1,9},{9,1},{17,25},{25,17},{2,10},{10... | collective-permute-start | bytes 3145736 | tf_op jit(solution)/shard_map/ppermute | solution.py:436
  274.9 28.7 %collective-permute-start.17 = (bf16[2,256,1024]{2,1,0:T(8,128)(2,1)}, bf16[2,256,1024]{2,1,0:T(8,128)(2,1)S(1)}, u32[]{:S(2)}, u32[]{:S(2)}) collective-permute-start(bf16[2,256,1024]{2,1,0:T(8,128)(2,1)} %get-tuple-element.73.refs_0_), channel_id=1, source_target_pairs={{0,8},{8,0},{16,24},{24,16},{1,9},{9,1},{17,25},{25,17},{2,10},{10... | collective-permute-start | bytes 3145736 | tf_op jit(solution)/shard_map/ppermute | solution.py:436
  281.3 51.2 %collective-permute-start.20 = (bf16[256,1024]{1,0:T(8,128)(2,1)}, bf16[256,1024]{1,0:T(8,128)(2,1)}, u32[]{:S(2)}, u32[]{:S(2)}) collective-permute-start(bf16[256,1024]{1,0:T(8,128)(2,1)} %add_convert_fusion.8), channel_id=1, source_target_pairs={{0,8},{8,0},{16,24},{24,16},{1,9},{9,1},{17,25},{25,17},{2,10},{10... | collective-permute-start | bytes 1572872 | tf_op jit(solution)/shard_map/ppermute | solution.py:436
  300.1 154.9 %reduce-scatter.4.cloned.1.call-start = ((), (), s32[]{:S(2)}) async-start(), calls=%async_computation.6 | async-start | bytes 7077888 | tf_op jit(solution)/shard_map/reduce_scatter | solution.py:806
  302.1 75.0 %collective-permute-start.27 = (bf16[256,1024]{1,0:T(8,128)(2,1)}, bf16[256,1024]{1,0:T(8,128)(2,1)}, u32[]{:S(2)}, u32[]{:S(2)}) collective-permute-start(bf16[256,1024]{1,0:T(8,128)(2,1)} %add_convert_fusion.5), channel_id=1, source_target_pairs={{0,8},{8,0},{16,24},{24,16},{1,9},{9,1},{17,25},{25,17},{2,10},{10... | collective-permute-start | bytes 1572872 | tf_op jit(solution)/shard_map/ppermute | solution.py:436
  315.2 25.5 %collective-permute-start.21 = (bf16[256,1024]{1,0:T(8,128)(2,1)}, bf16[256,1024]{1,0:T(8,128)(2,1)}, u32[]{:S(2)}, u32[]{:S(2)}) collective-permute-start(bf16[256,1024]{1,0:T(8,128)(2,1)} %get-tuple-element.77.refs_1_), channel_id=1, source_target_pairs={{0,16},{8,24},{16,0},{24,8},{1,17},{9,25},{17,1},{25,9},{2,18},{10... | collective-permute-start | bytes 1572872 | tf_op jit(solution)/shard_map/ppermute | solution.py:436
  324.2 33.4 %collective-permute-start.24 = (bf16[2,256,1024]{2,1,0:T(8,128)(2,1)}, bf16[2,256,1024]{2,1,0:T(8,128)(2,1)}, u32[]{:S(2)}, u32[]{:S(2)}) collective-permute-start(bf16[2,256,1024]{2,1,0:T(8,128)(2,1)} %get-tuple-element.79.refs_0_), channel_id=1, source_target_pairs={{0,8},{8,0},{16,24},{24,16},{1,9},{9,1},{17,25},{25,17},{2,10},{10... | collective-permute-start | bytes 3145736 | tf_op jit(solution)/shard_map/ppermute | solution.py:436
  329.4 25.3 %collective-permute-start.25 = (bf16[256,1024]{1,0:T(8,128)(2,1)}, bf16[256,1024]{1,0:T(8,128)(2,1)}, u32[]{:S(2)}, u32[]{:S(2)}) collective-permute-start(bf16[256,1024]{1,0:T(8,128)(2,1)} %get-tuple-element.81.refs_2_), channel_id=1, source_target_pairs={{0,16},{8,24},{16,0},{24,8},{1,17},{9,25},{17,1},{25,9},{2,18},{10... | collective-permute-start | bytes 1572872 | tf_op jit(solution)/shard_map/ppermute | solution.py:436
  332.4 44.8 %collective-permute-start.22 = (bf16[256,1024]{1,0:T(8,128)(2,1)}, bf16[256,1024]{1,0:T(8,128)(2,1)}, u32[]{:S(2)}, u32[]{:S(2)}) collective-permute-start(bf16[256,1024]{1,0:T(8,128)(2,1)} %fusion.22), channel_id=1, source_target_pairs={{0,16},{8,24},{16,0},{24,8},{1,17},{9,25},{17,1},{25,9},{2,18},{10... | collective-permute-start | bytes 1572872 | tf_op jit(solution)/shard_map/ppermute | solution.py:436
  342.9 34.3 %collective-permute-start.23 = (bf16[256,1024]{1,0:T(8,128)(2,1)}, bf16[256,1024]{1,0:T(8,128)(2,1)}, u32[]{:S(2)}, u32[]{:S(2)}) collective-permute-start(bf16[256,1024]{1,0:T(8,128)(2,1)} %add_convert_fusion.7), channel_id=1, source_target_pairs={{0,8},{8,0},{16,24},{24,16},{1,9},{9,1},{17,25},{25,17},{2,10},{10... | collective-permute-start | bytes 1572872 | tf_op jit(solution)/shard_map/ppermute | solution.py:436
  354.5 192.0 %reduce-scatter.8.cloned.1.call-start = ((), (), s32[]{:S(2)}) async-start(), calls=%async_computation.8 | async-start | bytes 7667712 | tf_op jit(solution)/shard_map/reduce_scatter | solution.py:834
  368.0 35.7 %collective-permute-start.35 = (bf16[256,1024]{1,0:T(8,128)(2,1)}, bf16[256,1024]{1,0:T(8,128)(2,1)}, u32[]{:S(2)}, u32[]{:S(2)}) collective-permute-start(bf16[256,1024]{1,0:T(8,128)(2,1)} %get-tuple-element.90.refs_1_), channel_id=1, source_target_pairs={{0,16},{8,24},{16,0},{24,8},{1,17},{9,25},{17,1},{25,9},{2,18},{10... | collective-permute-start | bytes 1572872 | tf_op jit(solution)/shard_map/ppermute | solution.py:436
  416.4 38.7 %collective-permute-start.33 = (bf16[256,1024]{1,0:T(8,128)(2,1)}, bf16[256,1024]{1,0:T(8,128)(2,1)}, u32[]{:S(2)}, u32[]{:S(2)}) collective-permute-start(bf16[256,1024]{1,0:T(8,128)(2,1)} %shard_map.236), channel_id=1, source_target_pairs={{0,8},{8,0},{16,24},{24,16},{1,9},{9,1},{17,25},{25,17},{2,10},{10... | collective-permute-start | bytes 1572872 | tf_op jit(solution)/shard_map/ppermute | solution.py:436
  417.4 39.5 %collective-permute-start.34 = (bf16[256,1024]{1,0:T(8,128)(2,1)}, bf16[256,1024]{1,0:T(8,128)(2,1)}, u32[]{:S(2)}, u32[]{:S(2)}) collective-permute-start(bf16[256,1024]{1,0:T(8,128)(2,1)} %shard_map.237), channel_id=1, source_target_pairs={{0,16},{8,24},{16,0},{24,8},{1,17},{9,25},{17,1},{25,9},{2,18},{10... | collective-permute-start | bytes 1572872 | tf_op jit(solution)/shard_map/ppermute | solution.py:436
  418.6 38.3 %collective-permute-start.36 = (bf16[256,1024]{1,0:T(8,128)(2,1)}, bf16[256,1024]{1,0:T(8,128)(2,1)}, u32[]{:S(2)}, u32[]{:S(2)}) collective-permute-start(bf16[256,1024]{1,0:T(8,128)(2,1)} %shard_map.238), channel_id=1, source_target_pairs={{0,8},{8,0},{16,24},{24,16},{1,9},{9,1},{17,25},{25,17},{2,10},{10... | collective-permute-start | bytes 1572872 | tf_op jit(solution)/shard_map/ppermute | solution.py:436
  420.1 58.9 %collective-permute-start.41 = (bf16[2,256,1024]{2,1,0:T(8,128)(2,1)}, bf16[2,256,1024]{2,1,0:T(8,128)(2,1)S(1)}, u32[]{:S(2)}, u32[]{:S(2)}) collective-permute-start(bf16[2,256,1024]{2,1,0:T(8,128)(2,1)} %shard_map.241.first_own), channel_id=1, source_target_pairs={{0,8},{8,0},{16,24},{24,16},{1,9},{9,1},{17,25},{25,17},{2,10},{10... | collective-permute-start | bytes 3145736 | tf_op jit(solution)/shard_map/ppermute | solution.py:436
  431.3 48.7 %collective-permute-start.42 = (bf16[2,256,1024]{2,1,0:T(8,128)(2,1)S(1)}, bf16[2,256,1024]{2,1,0:T(8,128)(2,1)S(1)}, u32[]{:S(2)}, u32[]{:S(2)}) collective-permute-start(bf16[2,256,1024]{2,1,0:T(8,128)(2,1)S(1)} %copy-done.3), channel_id=1, source_target_pairs={{0,16},{8,24},{16,0},{24,8},{1,17},{9,25},{17,1},{25,9},{2,18},{10... | collective-permute-start | bytes 3145736 | tf_op jit(solution)/shard_map/ppermute | solution.py:436
  464.9 42.2 %collective-permute-start.39 = (bf16[2,192,1024]{2,1,0:T(8,128)(2,1)}, bf16[2,192,1024]{2,1,0:T(8,128)(2,1)}, u32[]{:S(2)}, u32[]{:S(2)}) collective-permute-start(bf16[2,192,1024]{2,1,0:T(8,128)(2,1)} %get-tuple-element.96.refs_2_), channel_id=1, source_target_pairs={{0,16},{8,24},{16,0},{24,8},{1,17},{9,25},{17,1},{25,9},{2,18},{10... | collective-permute-start | bytes 2359304 | tf_op jit(solution)/shard_map/ppermute | solution.py:436
  465.3 45.3 %collective-permute-start.37 = (bf16[2,192,1024]{2,1,0:T(8,128)(2,1)}, bf16[2,192,1024]{2,1,0:T(8,128)(2,1)}, u32[]{:S(2)}, u32[]{:S(2)}) collective-permute-start(bf16[2,192,1024]{2,1,0:T(8,128)(2,1)} %get-tuple-element.94.refs_0_), channel_id=1, source_target_pairs={{0,8},{8,0},{16,24},{24,16},{1,9},{9,1},{17,25},{25,17},{2,10},{10... | collective-permute-start | bytes 2359304 | tf_op jit(solution)/shard_map/ppermute | solution.py:436
  476.2 28.1 %collective-permute-start.43 = (bf16[256,1024]{1,0:T(8,128)(2,1)}, bf16[256,1024]{1,0:T(8,128)(2,1)}, u32[]{:S(2)}, u32[]{:S(2)}) collective-permute-start(bf16[256,1024]{1,0:T(8,128)(2,1)} %fusion.20), channel_id=1, source_target_pairs={{0,16},{8,24},{16,0},{24,8},{1,17},{9,25},{17,1},{25,9},{2,18},{10... | collective-permute-start | bytes 1572872 | tf_op jit(solution)/shard_map/ppermute | solution.py:436
  479.0 42.8 %collective-permute-start.52 = (bf16[2,256,1024]{2,1,0:T(8,128)(2,1)}, bf16[2,256,1024]{2,1,0:T(8,128)(2,1)}, u32[]{:S(2)}, u32[]{:S(2)}) collective-permute-start(bf16[2,256,1024]{2,1,0:T(8,128)(2,1)} %shard_map.250.first_own), channel_id=1, source_target_pairs={{0,8},{8,0},{16,24},{24,16},{1,9},{9,1},{17,25},{25,17},{2,10},{10... | collective-permute-start | bytes 3145736 | tf_op jit(solution)/shard_map/ppermute | solution.py:436
  480.0 46.8 %collective-permute-start.53 = (bf16[2,256,1024]{2,1,0:T(8,128)(2,1)}, bf16[2,256,1024]{2,1,0:T(8,128)(2,1)}, u32[]{:S(2)}, u32[]{:S(2)}) collective-permute-start(bf16[2,256,1024]{2,1,0:T(8,128)(2,1)} %shard_map.251.second_own), channel_id=1, source_target_pairs={{0,16},{8,24},{16,0},{24,8},{1,17},{9,25},{17,1},{25,9},{2,18},{10... | collective-permute-start | bytes 3145736 | tf_op jit(solution)/shard_map/ppermute | solution.py:436
  507.1 60.7 %collective-permute-start.50 = (bf16[2,256,1024]{2,1,0:T(8,128)(2,1)}, bf16[2,256,1024]{2,1,0:T(8,128)(2,1)S(1)}, u32[]{:S(2)}, u32[]{:S(2)}) collective-permute-start(bf16[2,256,1024]{2,1,0:T(8,128)(2,1)} %shard_map.246.first_own), channel_id=1, source_target_pairs={{0,8},{8,0},{16,24},{24,16},{1,9},{9,1},{17,25},{25,17},{2,10},{10... | collective-permute-start | bytes 3145736 | tf_op jit(solution)/shard_map/ppermute | solution.py:436
  510.6 31.6 %collective-permute-start.40 = (bf16[192,1024]{1,0:T(8,128)(2,1)}, bf16[192,1024]{1,0:T(8,128)(2,1)}, u32[]{:S(2)}, u32[]{:S(2)}) collective-permute-start(bf16[192,1024]{1,0:T(8,128)(2,1)} %fusion.34), channel_id=1, source_target_pairs={{0,8},{8,0},{16,24},{24,16},{1,9},{9,1},{17,25},{25,17},{2,10},{10... | collective-permute-start | bytes 1179656 | tf_op jit(solution)/shard_map/ppermute | solution.py:436
  519.4 25.0 %collective-permute-start.38 = (bf16[192,1024]{1,0:T(8,128)(2,1)}, bf16[192,1024]{1,0:T(8,128)(2,1)}, u32[]{:S(2)}, u32[]{:S(2)}) collective-permute-start(bf16[192,1024]{1,0:T(8,128)(2,1)} %fusion.33), channel_id=1, source_target_pairs={{0,16},{8,24},{16,0},{24,8},{1,17},{9,25},{17,1},{25,9},{2,18},{10... | collective-permute-start | bytes 1179656 | tf_op jit(solution)/shard_map/ppermute | solution.py:436
  521.8 46.0 %collective-permute-start.51 = (bf16[2,256,1024]{2,1,0:T(8,128)(2,1)}, bf16[2,256,1024]{2,1,0:T(8,128)(2,1)S(1)}, u32[]{:S(2)}, u32[]{:S(2)}) collective-permute-start(bf16[2,256,1024]{2,1,0:T(8,128)(2,1)} %shard_map.247.second_own), channel_id=1, source_target_pairs={{0,16},{8,24},{16,0},{24,8},{1,17},{9,25},{17,1},{25,9},{2,18},{10... | collective-permute-start | bytes 3145736 | tf_op jit(solution)/shard_map/ppermute | solution.py:436
  (110 other events, 970.6 us)
Sparse Core Ops, SparseCore 0:
  10.5 67.4 all-gather.3
  80.2 63.3 all-gather.5
  153.8 61.9 all-gather.7
  300.2 67.5 reduce-scatter.5
  370.6 68.1 reduce-scatter.3
  455.2 72.4 reduce-scatter.7

commit v3 on v2

--- a/solution.py
+++ b/solution.py
@@ -54,7 +54,15 @@
     return pltpu.CompilerParams(vmem_limit_bytes=VMEM_LIMIT)
 
 
-def cost(us=0.3):
+PLAN = {'c_k0': 0.3, 'c_ha': 0.3, 'c_da': 0.3, 'c_hb': 0.3, 'c_ga': 0.3, 'c_df': 0.3, 'c_db': 0.3, 'c_ua': 300, 'c_ou': 300, 'c_gb': 300, 'c_ub': 300, 'c_op': 0.3, 'c_at': 0.3, 'c_k4': 0.3, 'c_rg': 0.3, 'c_dx': 0.3, 'c_ld': 300, 'c_lg': 0.3, 'c_lu': 0.3, 'c_lh': 0.3, 'w_ga_d1': 1, 'w_ou_g1': 1, 'o_db': 0, 'w_db_d1': 0, 'w_df_d1': 0, 'w_df_g1': 0, 'w_db_g1': 0, 'w_ua_g1': 0, 'w_ou_d2': 1, 'o_c4': 0, 'w_gb_u1': 1, 'w_gb_d2': 0, 'w_ub_u1': 0, 'o_r2u': 0, 'w_nb_d3': 1, 'w_nb_g2': 1, 'w_nb_u1': 0, 'w_ag_d3': 0, 'w_ag_g2': 0, 'o_u2': 1, 'o_g3': 1, 'o_d4': 1, 'o_u3': 0, 'o_c8': 0, 'o_dx': 0, 'w_dx_u2': 1, 'w_dx_g3': 1, 'w_dx_d4': 0, 'o_g4': 0, 'o_u4': 1, 'w_aw_g4': 0, 'w_aw_u4': 0, 'o_dx2': 0, 'o_lg': 0, 'o_lu': 0, 'w_lh': 1, 'o_ga': 1}
+
+
+def on(name, values):
+    return tuple(values) if PLAN[name] else ()
+
+
+def cost(us=300):
+    us = PLAN.get(us, us)
     return pl.CostEstimate(flops=int(us * 1e9), bytes_accessed=int(us * 3.69e6), transcendentals=0)
 
 
@@ -107,7 +115,7 @@
             pl.BlockSpec((count, step), lambda n: (0, n)),
         ],
         compiler_params=kernel_params(),
-        cost_estimate=cost(),
+        cost_estimate=cost('c_k0'),
     )(*parts, gain, weights)
 
 
@@ -159,7 +167,7 @@
         + [transposed] * 3,
         input_output_aliases={4 + i: i for i in range(len(before))},
         compiler_params=kernel_params(),
-        cost_estimate=cost(),
+        cost_estimate=cost('c_ha' if part == 0 else 'c_hb'),
     )(x, cot, gate_up, down, *before, *waits)
 
 
@@ -169,7 +177,7 @@
         out_ref[rows, :] = product(a_ref[rows, :], w_ref[...], NN).astype(BF16)
 
 
-def rows_product(a, w, waits=(), us=0.3):
+def rows_product(a, w, waits=(), us=300):
     count, depth = a.shape
     width = w.shape[1]
     block = 512
@@ -185,6 +193,63 @@
     )(a, w, *waits)
 
 
+def core_product_kernel(core_ref, a_ref, w_ref, *refs):
+    kept_ref, sent_ref = refs[-2:]
+    chips, height, width = kept_ref.shape
+    for chip in range(chips):
+        rows = pl.ds(2 * chip * height, 2 * height)
+        pair = product(a_ref[rows, :], w_ref[...], NN)
+        first, second = pair[:height], pair[height:]
+        own_first = core_ref[0] == 0
+        kept_ref[chip] = jnp.where(own_first, first, second).astype(BF16)
+        sent_ref[chip] = jnp.where(own_first, second, first).astype(BF16)
+
+
+def core_product(a, w, waits=(), us=300):
+    count, depth = a.shape
+    width = w.shape[1]
+    block = 512
+    chips = lax.axis_size("fsdp") // 2
+    height = count // (2 * chips)
+    out = pl.BlockSpec((chips, height, block), lambda n: (0, 0, n))
+    return pl.pallas_call(
+        core_product_kernel,
+        out_shape=[jax.ShapeDtypeStruct((chips, height, width), BF16)] * 2,
+        grid=(width // block,),
+        in_specs=[
+            pl.BlockSpec(memory_space=pltpu.SMEM),
+            resident((count, depth)),
+            pl.BlockSpec((depth, block), lambda n: (0, n)),
+        ]
+        + anywhere(waits),
+        out_specs=[out, out],
+        compiler_params=kernel_params(),
+        cost_estimate=cost(us),
+    )(own_core(), a, w, *waits)
+
+
+def own_core():
+    return (lax.axis_index("fsdp") % 2).astype(jnp.int32)[None]
+
+
+def sum_cores(kept, sent):
+    devices = lax.axis_size("fsdp")
+    got = lax.ppermute(sent, "fsdp", [(i, i ^ 1) for i in range(devices)])
+    return sum_low(kept, got)
+
+
+def scatter_chips(x):
+    devices = lax.axis_size("fsdp")
+    groups = [list(range(core, devices, 2)) for core in range(2)]
+    return lax.psum_scatter(
+        x.reshape(-1, x.shape[-1]),
+        "fsdp",
+        scatter_dimension=0,
+        tiled=True,
+        axis_index_groups=groups,
+    )
+
+
 def weight_grad_kernel(a_ref, b_ref, *refs):
     first_ref, upper_ref, lower_ref = refs[-3:]
     n = pl.program_id(0)
@@ -202,7 +267,7 @@
         lower_ref[...] = result[height:]
 
 
-def weight_grad(a, b, waits=(), us=0.3):
+def weight_grad(a, b, waits=(), us=300):
     units, count = a.shape
     width = b.shape[1]
     height, half, block = units // 2, width // 2, width // 4
@@ -266,36 +331,73 @@
         in_specs=[resident((count, depth)), rhs_spec],
         out_specs=[first, first, second, second],
         compiler_params=kernel_params(),
-        cost_estimate=cost(),
+        cost_estimate=cost('c_op' if dims == NN else 'c_dx'),
     )(lhs, rhs)
 
 
-def rows_grad_kernel(terms, *refs):
-    out_ref = refs[-1]
+def rows_grad_kernel(terms, core_ref, *refs):
+    beside_ref, kept_ref, sent_ref = refs[-3:]
+    height = kept_ref.shape[1]
+    own_first = core_ref[0] == 0
+
+    def store(pair, first_column):
+        columns = pl.ds(first_column, pair.shape[1])
+        first, second = pair[:height], pair[height:]
+        kept_ref[0, :, columns] = jnp.where(own_first, first, second).astype(BF16)
+        sent_ref[0, :, columns] = jnp.where(own_first, second, first).astype(BF16)
+
+    column = 0
+    for i in range(terms):
+        store(product(refs[i][...], refs[terms + i][...], TN), column)
+        column += refs[terms + i].shape[1]
+    store(beside_ref[...], column)
+
+
+def plain_grad_kernel(terms, *refs):
+    beside_ref, out_ref = refs[-2:]
     column = 0
     for i in range(terms):
         columns = pl.ds(column, refs[terms + i].shape[1])
         out_ref[:, columns] = product(refs[i][...], refs[terms + i][...], TN).astype(BF16)
         column += refs[terms + i].shape[1]
-    out_ref[:, column:] = refs[2 * terms][...]
-
-
-def rows_grad(terms, beside, waits=()):
+    out_ref[:, column:] = beside_ref[...].astype(BF16)
+
+
+def plain_grad(terms, beside):
     count, width = terms[0][0].shape
     block = 512
     total = sum(b.shape[1] for _, b in terms) + beside.shape[1]
     return pl.pallas_call(
-        functools.partial(rows_grad_kernel, len(terms)),
+        functools.partial(plain_grad_kernel, len(terms)),
         out_shape=jax.ShapeDtypeStruct((width, total), BF16),
         grid=(width // block,),
         in_specs=[pl.BlockSpec((count, block), lambda m: (0, m))] * len(terms)
         + [resident(b.shape) for _, b in terms]
-        + [pl.BlockSpec((block, beside.shape[1]), lambda m: (m, 0))]
-        + anywhere(waits),
+        + [pl.BlockSpec((block, beside.shape[1]), lambda m: (m, 0))],
         out_specs=pl.BlockSpec((block, total), lambda m: (m, 0)),
         compiler_params=kernel_params(),
-        cost_estimate=cost(),
-    )(*[a for a, _ in terms], *[b for _, b in terms], beside, *waits)
+        cost_estimate=cost('c_rg'),
+    )(*[a for a, _ in terms], *[b for _, b in terms], beside)
+
+
+def rows_grad(terms, beside):
+    count, width = terms[0][0].shape
+    chips = lax.axis_size("fsdp") // 2
+    block = width // chips
+    total = sum(b.shape[1] for _, b in terms) + beside.shape[1]
+    out = pl.BlockSpec((1, block // 2, total), lambda m: (m, 0, 0))
+    return pl.pallas_call(
+        functools.partial(rows_grad_kernel, len(terms)),
+        out_shape=[jax.ShapeDtypeStruct((chips, block // 2, total), BF16)] * 2,
+        grid=(chips,),
+        in_specs=[pl.BlockSpec(memory_space=pltpu.SMEM)]
+        + [pl.BlockSpec((count, block), lambda m: (0, m))] * len(terms)
+        + [resident(b.shape) for _, b in terms]
+        + [pl.BlockSpec((block, beside.shape[1]), lambda m: (m, 0))],
+        out_specs=[out, out],
+        compiler_params=kernel_params(),
+        cost_estimate=cost('c_rg'),
+    )(own_core(), *[a for a, _ in terms], *[b for _, b in terms], beside)
 
 
 def turned(x, cosine, sine):
@@ -359,17 +461,44 @@
             column(wide, 0),
         ],
         compiler_params=kernel_params(),
-        cost_estimate=cost(),
+        cost_estimate=cost('c_at'),
     )(packed, packed, packed, cosine, sine, bias)
 
 
 def attend_back_kernel(
-    query_ref, key_ref, value_ref, probs_ref, d_out_ref, out_ref, cos_ref, sin_ref, *refs
+    blocks,
+    place_ref,
+    query_ref,
+    key_ref,
+    value_ref,
+    probs_ref,
+    out_ref,
+    cos_ref,
+    sin_ref,
+    weight_ref,
+    *refs,
 ):
-    packed_ref = refs[-1]
+    *parts, packed_ref, branch_ref, whole_ref, d_out_ref = refs
     g = pl.program_id(0)
     kv_heads = pl.num_programs(0)
     scale = HEAD_WIDTH ** (-0.5)
+
+    @pl.when(g == 0)
+    def _():
+        first_row = 0
+        for block in blocks:
+            first = 0
+            for i, lead in block:
+                part = parts[i][...] if lead is None else parts[i][lead]
+                height, width = part.shape
+                whole_ref[pl.ds(first_row, height), pl.ds(first, width)] = part
+                first += width
+            first_row += height
+        columns = branch_ref.shape[1]
+        start = pl.multiple_of(place_ref[0] * columns, 128)
+        branch_ref[...] = whole_ref[:, pl.ds(start, columns)]
+
+    d_out_ref[...] = product(whole_ref[...], weight_ref[...], NT).astype(BF16)
     key, value = key_ref[...], value_ref[...]
     d_key = d_value = None
     for h in range(GROUP):
@@ -398,7 +527,7 @@
     packed_ref[:, pl.ds(place, HEAD_WIDTH)] = d_value.astype(BF16)
 
 
-def attend_back(queries, keys, values, probs, d_out, out, cosine, sine, waits=()):
+def attend_back(queries, keys, values, probs, out, cosine, sine, parts, blocks, w_rows, columns):
     count = queries.shape[0]
     kv_heads = keys.shape[1] // HEAD_WIDTH
     wide, narrow = GROUP * HEAD_WIDTH, HEAD_WIDTH
@@ -408,24 +537,43 @@
 
     packed_shape = (count, kv_heads * (GROUP + 2) * HEAD_WIDTH)
     return pl.pallas_call(
-        attend_back_kernel,
-        out_shape=jax.ShapeDtypeStruct(packed_shape, BF16),
+        functools.partial(attend_back_kernel, blocks),
+        out_shape=[
+            jax.ShapeDtypeStruct(packed_shape, BF16),
+            jax.ShapeDtypeStruct((count, columns), BF16),
+        ],
         grid=(kv_heads,),
         in_specs=[
+            pl.BlockSpec(memory_space=pltpu.SMEM),
             column(wide),
             column(narrow),
             column(narrow),
             pl.BlockSpec((GROUP, count, count), lambda g: (g, 0, 0)),
             column(wide),
-            column(wide),
             resident((count, HEAD_WIDTH)),
             resident((count, HEAD_WIDTH)),
+            pl.BlockSpec((wide, w_rows.shape[1]), lambda g: (g, 0)),
         ]
-        + anywhere(waits),
-        out_specs=pl.BlockSpec(packed_shape, lambda g: (0, 0)),
+        + [resident(p.shape) for p in parts],
+        out_specs=[
+            pl.BlockSpec(packed_shape, lambda g: (0, 0)),
+            pl.BlockSpec((count, columns), lambda g: (0, 0)),
+        ],
+        scratch_shapes=[pltpu.VMEM((count, w_rows.shape[1]), BF16), pltpu.VMEM((count, wide), BF16)],
         compiler_params=kernel_params(),
-        cost_estimate=cost(),
-    )(queries, keys, values, probs, d_out, out, cosine, sine, *waits)
+        cost_estimate=cost('c_k4'),
+    )(
+        lax.axis_index("ctx").astype(jnp.int32)[None],
+        queries,
+        keys,
+        values,
+        probs,
+        out,
+        cosine,
+        sine,
+        w_rows,
+        *parts,
+    )
 
 
 def square():
@@ -470,21 +618,29 @@
     )
 
 
-def scatter_sum_ctx(parts):
-    if not square():
-        return lax.psum_scatter(parts, "ctx", scatter_dimension=0, tiled=False).astype(F32)
-    first_sent, first_kept, second_sent, second_kept = parts
-    got_first = swap(first_sent, 1)
-    got_second = swap(second_sent, 2)
-    last_first = swap(sum_low(first_kept[1], got_first[1]), 2)
-    last_second = swap(sum_low(second_kept[1], got_second[1]), 1)
-    return jnp.concatenate(
-        [
-            first_kept[0].astype(F32) + got_first[0].astype(F32) + last_first.astype(F32),
-            second_kept[0].astype(F32) + got_second[0].astype(F32) + last_second.astype(F32),
-        ],
-        axis=-1,
-    )
+class ScatterSumCtx:
+    def __init__(self, parts):
+        self.parts = parts
+        if square():
+            self.got_first = swap(parts[0], 1)
+            self.got_second = swap(parts[2], 2)
+
+    def result(self, *others):
+        if not square():
+            return lax.psum_scatter(self.parts, "ctx", scatter_dimension=0, tiled=False).astype(F32)
+        _, first_kept, _, second_kept = self.parts
+        first = sum_low(first_kept[1], self.got_first[1])
+        second = sum_low(second_kept[1], self.got_second[1])
+        if others:
+            first, second = after(first, *others), after(second, *others)
+        last_first, last_second = swap(first, 2), swap(second, 1)
+        return jnp.concatenate(
+            [
+                sum(t.astype(F32) for t in (first_kept[0], self.got_first[0], last_first)),
+                sum(t.astype(F32) for t in (second_kept[0], self.got_second[0], last_second)),
+            ],
+            axis=-1,
+        )
 
 
 def absolute_order(blocks):
@@ -569,31 +725,31 @@
             first += width
         columns = pl.ds(pl.multiple_of(place * out_cols, 128), out_cols)
         out_ref[:, columns] = rows[:, head_cols : head_cols + out_cols]
-        gain_ffn += rows[:, head_cols + out_cols : head_cols + out_cols + 1]
-    gain_attn_ref[...] = gain_attn / gain_ref[...]
-    gain_ffn_ref[...] = gain_ffn
+        gain_ffn += rows[:, head_cols + out_cols :]
+    gain_ffn_ref[...] = gain_ffn.T[:1]
+    gain_attn = jnp.broadcast_to(gain_attn, (gain_attn.shape[0], 128))
+    gain_attn_ref[...] = gain_attn.T[:1] / gain_ref[...]
 
 
 def lay_heads(parts, blocks, sizes, w_qkv, norm_attn, waits):
     rows, qkv_cols = w_qkv.shape
     q_cols, kv_cols, out_cols, places = sizes
     whole = pl.BlockSpec(memory_space=pltpu.VMEM)
-    column = jax.ShapeDtypeStruct((rows, 1), F32)
     return pl.pallas_call(
         functools.partial(lay_heads_kernel, blocks, sizes),
         out_shape=[
             jax.ShapeDtypeStruct((rows, qkv_cols), F32),
             jax.ShapeDtypeStruct((rows, out_cols * places), F32),
-            column,
-            column,
+            jax.ShapeDtypeStruct((1, rows), F32),
+            jax.ShapeDtypeStruct((1, rows), F32),
         ],
         in_specs=[pl.BlockSpec(memory_space=pltpu.SMEM)]
         + [whole] * (2 + len(parts))
         + anywhere(waits),
         out_specs=[whole] * 4,
         compiler_params=kernel_params(),
-        cost_estimate=cost(),
-    )(block_order(), w_qkv, norm_attn.astype(F32)[:, None], *parts, *waits)
+        cost_estimate=cost('c_lh'),
+    )(block_order(), w_qkv, norm_attn.astype(F32)[None, :], *parts, *waits)
 
 
 def lay_out_kernel(place_ref, first_own, first_got, second_own, second_got, *refs):
@@ -641,7 +797,7 @@
         self.got_first = swap(part[0], 1)
         self.got_third = swap(part[2], 2)
 
-    def start_second(self, part):
+    def start_second(self, part, *others):
         self.lower = part
         if not square():
             blocks = []
@@ -651,7 +807,7 @@
             whole = jnp.concatenate(blocks)
             self.whole = lax.psum(whole.reshape(-1, whole.shape[-1]), "ctx").astype(F32)
             return
-        self.got_second = swap(part[1], 2)
+        self.got_second = swap(after(part[1], *others) if others else part[1], 2)
 
     def arrived(self, second=False):
         if not square():
@@ -691,7 +847,7 @@
         self.second_23 = swap(self.second_01, 2)
         return (self.first_13, self.second_23)
 
-    def result(self, waits=(), us=0.3):
+    def result(self, waits=(), us=300):
         if not square():
             return self.whole
         return lay_out(self.first_02, self.first_13, self.second_01, self.second_23, waits, us)
@@ -768,7 +924,7 @@
     )
     bias = jnp.where(allowed, 0.0, NEGATIVE_FILLER)
     queries, keys, values, probs, attended_low = attend(packed, cosine, sine, bias, kv_heads)
-    branch = scatter_sum_ctx(product_in_parts(attended_low, w_rows, NN, width))
+    branch = ScatterSumCtx(product_in_parts(attended_low, w_rows, NN, width)).result()
 
     x_full = x_own.astype(F32)
     middle = x_full + branch
@@ -781,29 +937,94 @@
     ).reshape(count, q_all)
     sum_down, sum_gate, sum_up = SumCtx(), SumCtx(), SumCtx()
     hidden, d_both, *first_t = hidden_grads(ffn_all, cot_all, gate_up, down, 0, (), (attended_all,))
-    down_a = weight_grad(first_t[0], cot_all)
+    down_a = weight_grad(first_t[0], cot_all, (), "c_da")
     sum_down.start_first(down_a)
     hidden, d_both, *second_t = hidden_grads(
         ffn_all, cot_all, gate_up, down, 1, (hidden, d_both), down_a
     )
-    gate_a = weight_grad(first_t[1], ffn_all, (second_t[0], *sum_down.arrived()))
-    sum_gate.start_first(gate_a)
-    d_ffn_part = rows_product(d_both, gate_up, gate_a)
+    last = (second_t[0],)
+    if PLAN["o_ga"] == 0:
+        gate_a = weight_grad(
+            first_t[1], ffn_all, (*last, *on("w_ga_d1", sum_down.arrived())), "c_ga"
+        )
+        sum_gate.start_first(gate_a)
+        last = gate_a
+    if PLAN["o_db"]:
+        down_b = weight_grad(
+            second_t[0], cot_all, (*last, *on("w_db_d1", sum_down.arrived())), "c_db"
+        )
+        last = down_b
+    d_ffn_part = rows_product(
+        d_both,
+        gate_up,
+        (
+            *last,
+            *on("w_df_d1", sum_down.arrived()),
+            *(on("w_df_g1", sum_gate.arrived()) if PLAN["o_ga"] == 0 else ()),
+        ),
+        "c_df",
+    )
     d_ffn = lax.psum_scatter(d_ffn_part, "fsdp", scatter_dimension=0, tiled=True)
-    down_b = weight_grad(second_t[0], cot_all, (d_ffn_part, *sum_gate.arrived()))
+    last = (d_ffn_part,)
+    if PLAN["o_ga"] == 1:
+        gate_a = weight_grad(
+            first_t[1], ffn_all, (*last, *on("w_ga_d1", sum_down.arrived())), "c_ga"
+        )
+        sum_gate.start_first(gate_a)
+        last = gate_a
+    if not PLAN["o_db"]:
+        down_b = weight_grad(
+            second_t[0], cot_all, (*last, *(on("w_db_g1", sum_gate.arrived()) if PLAN["o_ga"] < 2 else ())), "c_db"
+        )
+        last = down_b
     sum_down.start_second(down_b)
     down_2 = sum_down.step_2()
-    up_a = weight_grad(first_t[2], ffn_all, down_b, 300)
+    if PLAN["o_ga"] == 2:
+        gate_a = weight_grad(
+            first_t[1], ffn_all, (*last, *on("w_ga_d1", sum_down.arrived())), "c_ga"
+        )
+        sum_gate.start_first(gate_a)
+        last = gate_a
+    up_a = weight_grad(first_t[2], ffn_all, (*last, *on("w_ua_g1", sum_gate.arrived())), "c_ua")
     sum_up.start_first(up_a)
-    ffn_part = rows_product(hidden, down, (*up_a, *down_2, *sum_down.arrived(True)), 300)
-    gate_b = weight_grad(second_t[1], ffn_all, (ffn_part, *sum_up.arrived()), 300)
+    waits = (
+        *up_a,
+        *on("w_ou_d2", (*down_2, *sum_down.arrived(True))),
+        *on("w_ou_g1", sum_gate.arrived()),
+    )
+    if PLAN["o_c4"]:
+        ffn_part = sum_cores(*core_product(hidden, down, waits, "c_ou"))
+    else:
+        ffn_part = rows_product(hidden, down, waits, "c_ou")
+    gate_b = weight_grad(
+        second_t[1],
+        ffn_all,
+        (
+            ffn_part,
+            *on("w_gb_u1", sum_up.arrived()),
+            *on("w_gb_d2", (*down_2, *sum_down.arrived(True))),
+        ),
+        "c_gb",
+    )
     sum_gate.start_second(gate_b)
     gate_2 = sum_gate.step_2()
     down_3 = sum_down.step_3()
-    up_b = weight_grad(second_t[2], ffn_all, gate_b, 300)
-    sum_up.start_second(up_b)
-    d_ffn = after(d_ffn, *down_3, *gate_2)
-    ffn_sum = lax.psum_scatter(ffn_part, "fsdp", scatter_dimension=0, tiled=True)
+    up_b = weight_grad(
+        second_t[2], ffn_all, (*gate_b, *on("w_ub_u1", sum_up.arrived())), "c_ub"
+    )
+    if not PLAN["o_r2u"]:
+        sum_up.start_second(up_b)
+    d_ffn = after(
+        d_ffn,
+        *up_b,
+        *on("w_nb_d3", down_3),
+        *on("w_nb_g2", gate_2),
+        *on("w_nb_u1", sum_up.arrived()),
+    )
+    if PLAN["o_c4"]:
+        ffn_sum = scatter_chips(ffn_part)
+    else:
+        ffn_sum = lax.psum_scatter(ffn_part, "fsdp", scatter_dimension=0, tiled=True)
     layer_out = middle + ffn_sum.astype(F32)
 
     d_ffn = d_ffn.astype(F32)
@@ -813,54 +1034,90 @@
         scaled - normed_ffn * jnp.mean(scaled * normed_ffn, axis=-1, keepdims=True)
     )
     d_branch_own = d_middle.astype(BF16)
-    d_branch = gather_ctx(d_branch_own).reshape(count, width)
-    d_attended = jnp.einsum("te,fe->tf", d_branch, w_rows, preferred_element_type=F32).astype(BF16)
-    up_2 = sum_up.step_2(d_branch)
-    gate_3 = sum_gate.step_3(d_branch)
-    down_4 = sum_down.step_4(d_branch)
-    up_3 = sum_up.step_3()
-    d_packed = attend_back(
-        queries, keys, values, probs, d_attended, attended_low, cosine, sine
-    )
-    d_weights = rows_grad(
-        [
-            (normed_low, d_packed),
-            (attended_all, lax.dynamic_slice_in_dim(d_branch, place * out_cols, out_cols, 1)),
-        ],
-        jnp.broadcast_to(d_gain_ffn.astype(BF16)[:, None], (width, 128)),
-    )
+    branch_parts, branch_blocks = gather_parts(
+        d_branch_own, *on("w_ag_d3", down_3), *on("w_ag_g2", gate_2)
+    )
+    arrived = branch_parts[-2:]
+    if PLAN["o_r2u"]:
+        sum_up.start_second(up_b, *arrived)
+    up_2 = sum_up.step_2(*on("o_u2", arrived))
+    gate_3 = sum_gate.step_3(*on("o_g3", arrived))
+    down_4 = sum_down.step_4(*on("o_d4", arrived))
+    d_packed, branch_cols = attend_back(
+        queries,
+        keys,
+        values,
+        probs,
+        attended_low,
+        cosine,
+        sine,
+        branch_parts,
+        branch_blocks,
+        w_rows,
+        out_cols,
+    )
+    up_3 = sum_up.step_3(*on("o_u3", (d_packed,)))
+    gain_cols = jnp.broadcast_to(d_gain_ffn[:, None], (width, 128))
+    terms = [(normed_low, d_packed), (attended_all, branch_cols)]
+    if PLAN["o_c8"]:
+        by_core = rows_grad(terms, gain_cols)
+        d_weights = sum_cores(*by_core)
+    else:
+        by_core = [plain_grad(terms, gain_cols)]
+        d_weights = by_core[0]
     d_weights = after(d_weights, ffn_sum)
-    d_attn_parts = product_in_parts(after(d_packed, d_weights, *up_2, *gate_3), weights, NT, width)
-    scattered = lax.psum_scatter(d_weights, "fsdp", scatter_dimension=0, tiled=True)
-    d_attn = scatter_sum_ctx(d_attn_parts)
-    d_attn = after(d_attn, *down_4, *up_3)
-    sum_gate.step_4(d_weights)
-    sum_up.step_4(d_weights)
+    d_attn_parts = product_in_parts(
+        after(
+            d_packed,
+            d_weights if PLAN["o_dx"] else by_core[0],
+            *on("w_dx_u2", up_2),
+            *on("w_dx_g3", gate_3),
+            *on("w_dx_d4", down_4),
+        ),
+        weights,
+        NT,
+        width,
+    )
+    if PLAN["o_c8"]:
+        scattered = scatter_chips(d_weights)
+    else:
+        scattered = lax.psum_scatter(d_weights, "fsdp", scatter_dimension=0, tiled=True)
+    d_attn_sum = ScatterSumCtx(d_attn_parts)
+    gate_4 = sum_gate.step_4(*on("o_g4", (d_weights,)))
+    up_4 = sum_up.step_4(*on("o_u4", (d_weights,)))
+    grad_down = sum_down.result(d_attn_parts, "c_ld")
+    parts, blocks = gather_parts(
+        after(scattered, grad_down, *on("w_aw_g4", gate_4), *on("w_aw_u4", up_4))
+    )
+    if not square():
+        rows_here = scattered.shape[0]
+        parts = [parts[0].reshape(places, rows_here, -1)]
+        blocks = [[(0, i)] for i in range(places)]
+    d_attn = d_attn_sum.result(*on("o_dx2", parts[1:3]))
     inv_own = lax.rsqrt(jnp.mean(x_full * x_full, axis=-1, keepdims=True) + NORM_EPS)
     normed_attn = x_full * inv_own
     scaled_attn = d_attn * gain_attn[None, :]
     d_tokens = d_middle + inv_own * (
         scaled_attn - normed_attn * jnp.mean(scaled_attn * normed_attn, axis=-1, keepdims=True)
     )
-
-    grad_down = sum_down.result(d_attn_parts, 300)
-    parts, blocks = gather_parts(after(scattered, grad_down))
-    if not square():
-        rows_here = scattered.shape[0]
-        parts = [parts[0].reshape(places, rows_here, -1)]
-        blocks = [[(0, i)] for i in range(places)]
-    grad_up = sum_up.result()
+    grad_gate = sum_gate.result(on("o_lg", parts[1:3]), "c_lg")
+    grad_up = sum_up.result(on("o_lu", parts[1:3]), "c_lu")
     grad_qkv, grad_out, grad_gain_attn, grad_gain_ffn = lay_heads(
-        parts, blocks, (q_cols, kv_cols, out_cols, places), w_qkv, norm_attn, (grad_up,)
+        parts,
+        blocks,
+        (q_cols, kv_cols, out_cols, places),
+        w_qkv,
+        norm_attn,
+        on("w_lh", (grad_up,)),
     )
     return (
         layer_out.astype(BF16)[None],
         d_tokens[None],
-        grad_gain_attn[:, 0],
+        grad_gain_attn[0],
         grad_qkv,
         grad_out,
-        grad_gain_ffn[:, 0],
-        sum_gate.result(),
+        grad_gain_ffn[0],
+        grad_gate,
         grad_up,
         grad_down,
     )

time: 610 us -> 602 us (0.987)
  other arithmetic: 86.5 us -> 70.5 us
  starting transfers between devices: 59.7 us -> 69.4 us
  Pallas kernels: 189 us -> 198 us
    ppermute x54, starting transfers between devices: 59 us -> 68.6 us  [swap(): return lax.ppermute(x, 'ctx', [(i, i ^ bit) for i in range(4)])]
    unnamed x172 -> x180, local copies, waits for them, and re-layouts: 17.6 us -> 20.3 us
  transfers between devices with their start and end apart: 60 -> 60, of which waited for: 26 -> 23; matrix products, arithmetic and copies ran while one was open for 18% -> 14% of each run, Pallas kernels for 25% -> 28%
where the time goes in v3:
time: 602 us; the launch traced here: 591 us
  Pallas kernels  198 us (33%)
  waiting for transfers between devices  186 us (31%)
  other arithmetic  70.5 us (12%)
  starting transfers between devices  69.4 us (12%)
  local copies, waits for them, and re-layouts  30.9 us (5%)
  between operations  24.1 us (4%)
  blocking collectives  12.1 us (2%)
    ppermute x54, waiting for transfers between devices, swap(): return lax.ppermute(x, 'ctx', [(i, i ^ bit) for i in range(4)])  149 us
    ppermute x54, starting transfers between devices, swap(): return lax.ppermute(x, 'ctx', [(i, i ^ bit) for i in range(4)])  68.6 us
    pallas_call x6, Pallas kernels, weight_grad(): pl.pallas_call(weight_grad_kernel, out_shape=[jax.ShapeDtypeStruct((2, he...  46.7 us
    pallas_call x2, Pallas kernels, hidden_grads(): pl.pallas_call(hidden_kernel, out_shape=[jax.ShapeDtypeStruct((count, 2 *...  34.4 us
    pallas_call x2, Pallas kernels, rows_product(): pl.pallas_call(rows_product_kernel, out_shape=jax.ShapeDtypeStruct((count...  28.9 us
    convert_element_type x16, other arithmetic, sum_low(): return sum((t.astype(F32) for t in terms)).astype(BF16)  28.1 us
    all_gather x1, waiting for transfers between devices, local(): lax.all_gather(after(ffn_low, cot_all), 'fsdp', axis=0, tiled=True)  21.9 us
    pallas_call x3, Pallas kernels, lay_out(): pl.pallas_call(lay_out_kernel, out_shape=jax.ShapeDtypeStruct((4 * height...  21.6 us
  transfers between devices with their start and end apart: 60, of which 23 were waited for; matrix products, arithmetic and copies ran while one was open for 14% of the time, Pallas kernels for 28%

profile of v3, /device:TPU:0, one launch (start us, length us, event | category | flops | bytes accessed | tf_op | source)
XLA Modules:
  0.0 591.5 jit_solution(13190693828416105751)
XLA Ops:
  15.2 12.1 %all_gather.12.refs_1_ = bf16[2,2048]{1,0:T(2,128)(2,1)} all-gather(bf16[2,256]{1,0:T(2,128)(2,1)S(1)} %pad_maximum_fusion.23), channel_id=1, replica_groups=mesh['ctx'=4,'fsdp'=8] {'fsdp'}, dimensions={1}, use_global_device_ids=true | all-gather | bytes 9216 | tf_op jit(solution)/shard_map/all_gather | solution.py:900
  31.3 17.0 %collective-permute-done.2.refs_3_.refs_1_ = bf16[2,192,1024]{2,1,0:T(8,128)(2,1)S(1)} collective-permute-done((bf16[2,192,1024]{2,1,0:T(8,128)(2,1)}, bf16[2,192,1024]{2,1,0:T(8,128)(2,1)S(1)}, u32[]{:S(2)}, u32[]{:S(2)}) %collective-permute-start.2) | collective-permute-done | bytes 786464 | tf_op jit(solution)/shard_map/ppermute | solution.py:584
  63.0 15.0 %all-gather.4.cloned.1.call-done.refs_6_.rhs_ref = bf16[2048,1536]{1,0:T(8,128)(2,1)} async-done(((bf16[256,1536]{1,0:T(8,128)(2,1)}), bf16[2048,1536]{1,0:T(8,128)(2,1)}) %all-gather.4.cloned.1.call-update) | async-done | bytes 6291472 | tf_op jit(solution)/shard_map/all_gather | solution.py:899
  87.9 9.1 %shard_map.216 = (bf16[768,2048]{1,0:T(8,128)(2,1)}, f32[768,1024]{1,0:T(8,128)}) custom-call(bf16[192,2048]{1,0:T(8,128)(2,1)} %bitcast.166, bf16[192,1024]{1,0:T(8,128)(2,1)} %copy-done.57, bf16[192,1024]{1,0:T(8,128)(2,1)} %copy-done.58, bf16[2,192,1024]{2,1,0:T(8,128)(2,1)} %copy-done.36, bf16[2,192,1024]{2,1,0:T(8,128)(2,1)} %copy-done.37, ...), custom_call_target="tpu_custom_call" | custom-call | flops 300000000 | bytes 1107000 | tf_op jit(solution)/shard_map/pallas_call | solution.py:104
  97.1 11.4 %shard_map.217 = (bf16[768,512]{1,0:T(8,128)(2,1)}, bf16[768,256]{1,0:T(8,128)(2,1)}, bf16[768,256]{1,0:T(8,128)(2,1)}, bf16[4,768,768]{2,1,0:T(8,128)(2,1)}, bf16[768,512]{1,0:T(8,128)(2,1)}) custom-call(f32[768,1024]{1,0:T(8,128)} %get-tuple-element.58.query_in.key_in.value_in, f32[768,1024]{1,0:T(8,128)} %get-tuple-element.58.query_in.key_in.value_in, ...), custom_call_target="tpu_custom_call" | custom-call | flops 300000000 | bytes 1107000 | tf_op jit(solution)/shard_map/pallas_call | solution.py:438
  111.7 5.8 shard_map.218
  120.5 16.4 %collective-permute-done.9 = bf16[2,192,1024]{2,1,0:T(8,128)(2,1)S(1)} collective-permute-done((bf16[2,192,1024]{2,1,0:T(8,128)(2,1)}, bf16[2,192,1024]{2,1,0:T(8,128)(2,1)S(1)}, u32[]{:S(2)}, u32[]{:S(2)}) %collective-permute-start.9) | collective-permute-done | bytes 786464 | tf_op jit(solution)/shard_map/ppermute | solution.py:584
  142.3 5.7 collective-permute-done.10
  176.1 14.1 %collective-permute-done.12 = bf16[2,4,192,256]{3,2,1,0:T(8,128)(2,1)S(1)} collective-permute-done((bf16[2,4,192,256]{3,2,1,0:T(8,128)(2,1)S(1)}, bf16[2,4,192,256]{3,2,1,0:T(8,128)(2,1)S(1)}, u32[]{:S(2)}, u32[]{:S(2)}) %collective-permute-start.12) | collective-permute-done | bytes 786464 | tf_op jit(solution)/shard_map/ppermute | solution.py:584
  194.2 21.9 %all-gather.8.cloned.1.call-done.x_ref.b_ref = bf16[1536,2048]{1,0:T(8,128)(2,1)} async-done(((bf16[192,2048]{1,0:T(8,128)(2,1)}), bf16[1536,2048]{1,0:T(8,128)(2,1)}) %all-gather.8.cloned.1.call-update) | async-done | bytes 6291472 | tf_op jit(solution)/shard_map/all_gather | solution.py:934
  216.1 17.2 %shard_map.221 = (bf16[1536,1024]{1,0:T(8,128)(2,1)}, bf16[1536,2048]{1,0:T(8,128)(2,1)}, bf16[512,1536]{1,0:T(8,128)(2,1)}, bf16[512,1536]{1,0:T(8,128)(2,1)}, bf16[512,1536]{1,0:T(8,128)(2,1)}) custom-call(bf16[1536,2048]{1,0:T(8,128)(2,1)} %all-gather.8.cloned.1.call-done.x_ref.b_ref, ...), custom_call_target="tpu_custom_call" | custom-call | flops 300000000 | bytes 1107000 | tf_op jit(solution)/shard_map/pallas_call | solution.py:148
  233.3 7.7 %shard_map.222 = (bf16[2,256,1024]{2,1,0:T(8,128)(2,1)}, bf16[256,1024]{1,0:T(8,128)(2,1)}, bf16[256,1024]{1,0:T(8,128)(2,1)}) custom-call(bf16[512,1536]{1,0:T(8,128)(2,1)} %get-tuple-element.66.a_ref, bf16[1536,2048]{1,0:T(8,128)(2,1)} %all-gather.6.cloned.1.call-done.refs_1_.cot_ref.b_ref), custom_call_target="tpu_custom_call" | custom-call | flops 300000000 | bytes 1107000 | tf_op jit(solution)/shard_map/pallas_call | solution.py:275
  244.0 17.2 %shard_map.223 = (bf16[1536,1024]{1,0:T(8,128)(2,1)}, bf16[1536,2048]{1,0:T(8,128)(2,1)}, bf16[512,1536]{1,0:T(8,128)(2,1)}, bf16[512,1536]{1,0:T(8,128)(2,1)}, bf16[512,1536]{1,0:T(8,128)(2,1)}) custom-call(bf16[1536,2048]{1,0:T(8,128)(2,1)} %all-gather.8.cloned.1.call-done.x_ref.b_ref, ...), custom_call_target="tpu_custom_call", output_to_operand_aliasing={{0}: (4, {}), {1}: (5, {})} | custom-call | flops 300000000 | bytes 1107000 | tf_op jit(solution)/shard_map/pallas_call | solution.py:148
  261.2 18.3 %shard_map.224.refs_0_ = bf16[1536,2048]{1,0:T(8,128)(2,1)} custom-call(bf16[1536,2048]{1,0:T(8,128)(2,1)} %get-tuple-element.74.a_ref, bf16[2048,2048]{1,0:T(8,128)(2,1)} %copy-done.9, bf16[512,1536]{1,0:T(8,128)(2,1)} %get-tuple-element.72.refs_0_.a_ref), custom_call_target="tpu_custom_call" | custom-call | flops 300000000 | bytes 1107000 | tf_op jit(solution)/shard_map/pallas_call | solution.py:184
  283.1 7.6 %shard_map.225 = (bf16[2,256,1024]{2,1,0:T(8,128)(2,1)}, bf16[256,1024]{1,0:T(8,128)(2,1)}, bf16[256,1024]{1,0:T(8,128)(2,1)}) custom-call(bf16[512,1536]{1,0:T(8,128)(2,1)} %get-tuple-element.73.a_ref, bf16[1536,2048]{1,0:T(8,128)(2,1)} %all-gather.8.cloned.1.call-done.x_ref.b_ref, bf16[1536,2048]{1,0:T(8,128)(2,1)} %shard_map.224.refs_0_, ...), custom_call_target="tpu_custom_call" | custom-call | flops 300000000 | bytes 1107000 | tf_op jit(solution)/shard_map/pallas_call | solution.py:275
  293.1 7.8 %shard_map.226 = (bf16[2,256,1024]{2,1,0:T(8,128)(2,1)}, bf16[256,1024]{1,0:T(8,128)(2,1)}, bf16[256,1024]{1,0:T(8,128)(2,1)}) custom-call(bf16[512,1536]{1,0:T(8,128)(2,1)} %get-tuple-element.72.refs_0_.a_ref, bf16[1536,2048]{1,0:T(8,128)(2,1)} %all-gather.6.cloned.1.call-done.refs_1_.cot_ref.b_ref, bf16[2,256,1024]{2,1,0:T(8,128)(2,1)} %get-tuple-element.75.refs_0_, ...), custom_call_target="tpu_custom_call" | custom-call | flops 300000000 | bytes 1107000 | tf_op jit(solution)/shard_map/pallas_call | solution.py:275
  305.0 7.8 %shard_map.227 = (bf16[2,256,1024]{2,1,0:T(8,128)(2,1)}, bf16[256,1024]{1,0:T(8,128)(2,1)}, bf16[256,1024]{1,0:T(8,128)(2,1)}) custom-call(bf16[512,1536]{1,0:T(8,128)(2,1)} %get-tuple-element.71.a_ref, bf16[1536,2048]{1,0:T(8,128)(2,1)} %all-gather.8.cloned.1.call-done.x_ref.b_ref, bf16[2,256,1024]{2,1,0:T(8,128)(2,1)} %get-tuple-element.78.refs_0_, ...), custom_call_target="tpu_custom_call" | custom-call | flops 299999985664 | bytes 1107000064 | tf_op jit(solution)/shard_map/pallas_call | solution.py:275
  321.9 7.4 %collective-permute-done.19.refs_5_ = bf16[256,1024]{1,0:T(8,128)(2,1)} collective-permute-done((bf16[256,1024]{1,0:T(8,128)(2,1)}, bf16[256,1024]{1,0:T(8,128)(2,1)}, u32[]{:S(2)}, u32[]{:S(2)}) %collective-permute-start.19) | collective-permute-done | bytes 524320 | tf_op jit(solution)/shard_map/ppermute | solution.py:584
  336.9 10.6 %shard_map.228.refs_0_ = bf16[1536,2048]{1,0:T(8,128)(2,1)} custom-call(bf16[1536,1024]{1,0:T(8,128)(2,1)} %get-tuple-element.70.a_ref, bf16[1024,2048]{1,0:T(8,128)(2,1)} %pad_maximum_fusion.down_ref.w_ref, bf16[2,256,1024]{2,1,0:T(8,128)(2,1)} %get-tuple-element.81.refs_0_, bf16[256,1024]{1,0:T(8,128)(2,1)} %get-tuple-element.82.refs_1_, ...), custom_call_target="tpu_custom_call" | custom-call | flops 299999985664 | bytes 1107000064 | tf_op jit(solution)/shard_map/pallas_call | solution.py:184
  347.5 7.6 %shard_map.229 = (bf16[2,256,1024]{2,1,0:T(8,128)(2,1)}, bf16[256,1024]{1,0:T(8,128)(2,1)}, bf16[256,1024]{1,0:T(8,128)(2,1)}) custom-call(bf16[512,1536]{1,0:T(8,128)(2,1)} %get-tuple-element.85.a_ref, bf16[1536,2048]{1,0:T(8,128)(2,1)} %all-gather.8.cloned.1.call-done.x_ref.b_ref, bf16[1536,2048]{1,0:T(8,128)(2,1)} %shard_map.228.refs_0_, ...), custom_call_target="tpu_custom_call" | custom-call | flops 299999985664 | bytes 1107000064 | tf_op jit(solution)/shard_map/pallas_call | solution.py:275
  358.4 8.0 %shard_map.230 = (bf16[2,256,1024]{2,1,0:T(8,128)(2,1)}, bf16[256,1024]{1,0:T(8,128)(2,1)}, bf16[256,1024]{1,0:T(8,128)(2,1)}) custom-call(bf16[512,1536]{1,0:T(8,128)(2,1)} %get-tuple-element.84.a_ref, bf16[1536,2048]{1,0:T(8,128)(2,1)} %all-gather.8.cloned.1.call-done.x_ref.b_ref, bf16[2,256,1024]{2,1,0:T(8,128)(2,1)} %get-tuple-element.86.refs_0_, ...), custom_call_target="tpu_custom_call" | custom-call | flops 299999985664 | bytes 1107000064 | tf_op jit(solution)/shard_map/pallas_call | solution.py:275
  393.6 7.5 %collective-permute-done.30.refs_3_.refs_1_ = bf16[2,192,1024]{2,1,0:T(8,128)(2,1)S(1)} collective-permute-done((bf16[2,192,1024]{2,1,0:T(8,128)(2,1)S(1)}, bf16[2,192,1024]{2,1,0:T(8,128)(2,1)S(1)}, u32[]{:S(2)}, u32[]{:S(2)}) %collective-permute-start.30) | collective-permute-done | bytes 786464 | tf_op jit(solution)/shard_map/ppermute | solution.py:584
  404.9 7.5 %collective-permute-done.35 = bf16[256,1024]{1,0:T(8,128)(2,1)} collective-permute-done((bf16[256,1024]{1,0:T(8,128)(2,1)}, bf16[256,1024]{1,0:T(8,128)(2,1)}, u32[]{:S(2)}, u32[]{:S(2)}) %collective-permute-start.35) | collective-permute-done | bytes 524320 | tf_op jit(solution)/shard_map/ppermute | solution.py:584
  426.2 16.2 %shard_map.232 = (bf16[768,1024]{1,0:T(8,128)(2,1)}, bf16[768,512]{1,0:T(8,128)(2,1)}) custom-call(s32[1]{0:T(128)} %bitcast.59.place_ref, bf16[768,512]{1,0:T(8,128)(2,1)} %get-tuple-element.92.query_ref, bf16[768,256]{1,0:T(8,128)(2,1)} %get-tuple-element.93.key_ref, bf16[768,256]{1,0:T(8,128)(2,1)} %get-tuple-element.94.value_ref, ...), custom_call_target="tpu_custom_call" | custom-call | flops 300000000 | bytes 1107000 | tf_op jit(solution)/shard_map/pallas_call | solution.py:539
  443.7 10.1 %shard_map.233.refs_1_.refs_0_ = bf16[2048,1664]{1,0:T(8,128)(2,1)} custom-call(bf16[768,2048]{1,0:T(8,128)(2,1)} %get-tuple-element.97.refs_0_, bf16[768,2048]{1,0:T(8,128)(2,1)} %pad_maximum_fusion.1.refs_0_.refs_1_, bf16[768,1024]{1,0:T(8,128)(2,1)} %get-tuple-element.96.refs_2_.refs_0_, bf16[768,512]{1,0:T(8,128)(2,1)} %get-tuple-element.98.refs_3_, ...), custom_call_target="tpu_custom_call" | custom-call | flops 300000000 | bytes 1107000 | tf_op jit(solution)/shard_map/pallas_call | solution.py:370
  456.0 8.0 %shard_map.239 = (bf16[2,192,1024]{2,1,0:T(8,128)(2,1)}, bf16[2,192,1024]{2,1,0:T(8,128)(2,1)}, bf16[2,192,1024]{2,1,0:T(8,128)(2,1)}, bf16[2,192,1024]{2,1,0:T(8,128)(2,1)}) custom-call(bf16[768,1024]{1,0:T(8,128)(2,1)} %shard_map.238.lhs_ref, bf16[2048,1536]{1,0:T(8,128)(2,1)} %all-gather.4.cloned.1.call-done.refs_6_.rhs_ref), custom_call_target="tpu_custom_call" | custom-call | flops 300000000 | bytes 1107000 | tf_op jit(solution)/shard_map/pallas_call | solution.py:327
  474.4 19.6 %collective-permute-done.47 = bf16[256,1024]{1,0:T(8,128)(2,1)} collective-permute-done((bf16[256,1024]{1,0:T(8,128)(2,1)S(1)}, bf16[256,1024]{1,0:T(8,128)(2,1)}, u32[]{:S(2)}, u32[]{:S(2)}) %collective-permute-start.47) | collective-permute-done | bytes 524320 | tf_op jit(solution)/shard_map/ppermute | solution.py:584
  497.9 7.9 %shard_map.243.refs_1_ = f32[1024,2048]{1,0:T(8,128)} custom-call(s32[8]{0:T(128)S(1)} %broadcast_xor_fusion.place_ref, bf16[2,256,1024]{2,1,0:T(8,128)(2,1)S(1)} %copy-done.3, bf16[2,256,1024]{2,1,0:T(8,128)(2,1)} %collective-permute-done.41.first_got, bf16[2,256,1024]{2,1,0:T(8,128)(2,1)S(1)} %copy-done.2, ...), custom_call_target="tpu_custom_call" | custom-call | flops 299999985664 | bytes 1107000064 | tf_op jit(solution)/shard_map/pallas_call | solution.py:774
  515.6 7.2 %collective-permute-done.52.first_got = bf16[2,256,1024]{2,1,0:T(8,128)(2,1)} collective-permute-done((bf16[2,256,1024]{2,1,0:T(8,128)(2,1)}, bf16[2,256,1024]{2,1,0:T(8,128)(2,1)}, u32[]{:S(2)}, u32[]{:S(2)}) %collective-permute-start.52) | collective-permute-done | bytes 1048608 | tf_op jit(solution)/shard_map/ppermute | solution.py:584
  525.6 8.6 %shard_map.249 = f32[1024,2048]{1,0:T(8,128)} custom-call(s32[8]{0:T(128)S(1)} %broadcast_xor_fusion.place_ref, bf16[2,256,1024]{2,1,0:T(8,128)(2,1)} %pad_maximum_fusion.7.first_own, bf16[2,256,1024]{2,1,0:T(8,128)(2,1)} %collective-permute-done.52.first_got, bf16[2,256,1024]{2,1,0:T(8,128)(2,1)} %pad_maximum_fusion.8.second_own, ...), custom_call_target="tpu_custom_call" | custom-call | flops 300000000 | bytes 1107000 | tf_op jit(solution)/shard_map/pallas_call | solution.py:774
  534.1 10.9 %collective-permute-done.40 = bf16[192,1024]{1,0:T(8,128)(2,1)} collective-permute-done((bf16[192,1024]{1,0:T(8,128)(2,1)}, bf16[192,1024]{1,0:T(8,128)(2,1)}, u32[]{:S(2)}, u32[]{:S(2)}) %collective-permute-start.40) | collective-permute-done | bytes 393248 | tf_op jit(solution)/shard_map/ppermute | solution.py:584
  578.4 6.0 %shard_map.248 = (f32[256,4096]{1,0:T(8,128)}, f32[256,2048]{1,0:T(8,128)}, f32[1,256]{1,0:T(1,128)}, f32[1,256]{1,0:T(1,128)}) custom-call(s32[4]{0:T(128)} %copy-done.76, bf16[256,4096]{1,0:T(8,128)(2,1)} %weight_ref.1, f32[1,256]{1,0:T(1,128)} %reshape_convert_fusion.gain_ref, bf16[256,1664]{1,0:T(8,128)(2,1)} %shard_map.244.refs_0_, ...), custom_call_target="tpu_custom_call" | custom-call | flops 300000000 | bytes 1107000 | tf_op jit(solution)/shard_map/pallas_call | solution.py:738
  (400 shorter events, 211.7 us)
Async XLA Ops:
  7.2 70.8 %all-gather.4.cloned.1.call-start = ((), (), s32[]{:S(2)}) async-start(), calls=%async_computation.3 | async-start | bytes 7077888 | tf_op jit(solution)/shard_map/all_gather | solution.py:899
  10.3 143.6 %all-gather.6.cloned.1.call-start = ((), (), s32[]{:S(2)}) async-start(), calls=%async_computation.4 | async-start | bytes 7077888 | tf_op jit(solution)/shard_map/all_gather | solution.py:904
  50.4 165.7 %all-gather.8.cloned.1.call-start = ((), (), s32[]{:S(2)}) async-start(), calls=%async_computation.5 | async-start | bytes 7077888 | tf_op jit(solution)/shard_map/all_gather | solution.py:934
  80.9 27.5 %collective-permute-start.4 = (bf16[512,512]{1,0:T(8,128)(2,1)}, bf16[512,512]{1,0:T(8,128)(2,1)S(1)}, u32[]{:S(2)}, u32[]{:S(2)}) collective-permute-start(bf16[512,512]{1,0:T(8,128)(2,1)} %get-tuple-element.123), channel_id=1, source_target_pairs={{0,24},{8,16},{16,8},{24,0},{1,25},{9,17},{17,9},{25,1},{2,26},{10... | collective-permute-start | bytes 1572872 | tf_op jit(solution)/shard_map/ppermute | solution.py:584
  153.9 213.7 %reduce-scatter.6.cloned.1.call-start = ((), (), s32[]{:S(2)}) async-start(), calls=%async_computation.7 | async-start | bytes 7077888 | tf_op jit(solution)/shard_map/reduce_scatter | solution.py:967
  241.1 41.0 %collective-permute-start.15 = (bf16[2,256,1024]{2,1,0:T(8,128)(2,1)}, bf16[2,256,1024]{2,1,0:T(8,128)(2,1)S(1)}, u32[]{:S(2)}, u32[]{:S(2)}) collective-permute-start(bf16[2,256,1024]{2,1,0:T(8,128)(2,1)} %get-tuple-element.67.refs_2_), channel_id=1, source_target_pairs={{0,8},{8,0},{16,24},{24,16},{1,9},{9,1},{17,25},{25,17},{2,10},{10... | collective-permute-start | bytes 3145736 | tf_op jit(solution)/shard_map/ppermute | solution.py:584
  242.5 37.0 %collective-permute-start.16 = (bf16[256,1024]{1,0:T(8,128)(2,1)}, bf16[256,1024]{1,0:T(8,128)(2,1)S(1)}, u32[]{:S(2)}, u32[]{:S(2)}) collective-permute-start(bf16[256,1024]{1,0:T(8,128)(2,1)} %get-tuple-element.69.refs_4_), channel_id=1, source_target_pairs={{0,16},{8,24},{16,0},{24,8},{1,17},{9,25},{17,1},{25,9},{2,18},{10... | collective-permute-start | bytes 1572872 | tf_op jit(solution)/shard_map/ppermute | solution.py:584
  279.5 192.7 %reduce-scatter.4.cloned.1.call-start = ((), (), s32[]{:S(2)}) async-start(), calls=%async_computation.6 | async-start | bytes 7077888 | tf_op jit(solution)/shard_map/reduce_scatter | solution.py:1027
  281.5 39.3 %collective-permute-start.18 = (bf16[256,1024]{1,0:T(8,128)(2,1)}, bf16[256,1024]{1,0:T(8,128)(2,1)}, u32[]{:S(2)}, u32[]{:S(2)}) collective-permute-start(bf16[256,1024]{1,0:T(8,128)(2,1)} %add_convert_fusion.8), channel_id=1, source_target_pairs={{0,8},{8,0},{16,24},{24,16},{1,9},{9,1},{17,25},{25,17},{2,10},{10... | collective-permute-start | bytes 1572872 | tf_op jit(solution)/shard_map/ppermute | solution.py:584
  290.7 44.7 %collective-permute-start.20 = (bf16[2,256,1024]{2,1,0:T(8,128)(2,1)}, bf16[2,256,1024]{2,1,0:T(8,128)(2,1)}, u32[]{:S(2)}, u32[]{:S(2)}) collective-permute-start(bf16[2,256,1024]{2,1,0:T(8,128)(2,1)} %get-tuple-element.75.refs_0_), channel_id=1, source_target_pairs={{0,8},{8,0},{16,24},{24,16},{1,9},{9,1},{17,25},{25,17},{2,10},{10... | collective-permute-start | bytes 3145736 | tf_op jit(solution)/shard_map/ppermute | solution.py:584
  292.2 40.6 %collective-permute-start.21 = (bf16[256,1024]{1,0:T(8,128)(2,1)}, bf16[256,1024]{1,0:T(8,128)(2,1)}, u32[]{:S(2)}, u32[]{:S(2)}) collective-permute-start(bf16[256,1024]{1,0:T(8,128)(2,1)} %get-tuple-element.77.refs_2_), channel_id=1, source_target_pairs={{0,16},{8,24},{16,0},{24,8},{1,17},{9,25},{17,1},{25,9},{2,18},{10... | collective-permute-start | bytes 1572872 | tf_op jit(solution)/shard_map/ppermute | solution.py:584
  318.1 29.4 %collective-permute-start.22 = (bf16[2,256,1024]{2,1,0:T(8,128)(2,1)}, bf16[2,256,1024]{2,1,0:T(8,128)(2,1)}, u32[]{:S(2)}, u32[]{:S(2)}) collective-permute-start(bf16[2,256,1024]{2,1,0:T(8,128)(2,1)} %get-tuple-element.81.refs_0_), channel_id=1, source_target_pairs={{0,8},{8,0},{16,24},{24,16},{1,9},{9,1},{17,25},{25,17},{2,10},{10... | collective-permute-start | bytes 3145736 | tf_op jit(solution)/shard_map/ppermute | solution.py:584
  320.9 26.7 %collective-permute-start.23 = (bf16[256,1024]{1,0:T(8,128)(2,1)}, bf16[256,1024]{1,0:T(8,128)(2,1)}, u32[]{:S(2)}, u32[]{:S(2)}) collective-permute-start(bf16[256,1024]{1,0:T(8,128)(2,1)} %get-tuple-element.83.refs_2_), channel_id=1, source_target_pairs={{0,16},{8,24},{16,0},{24,8},{1,17},{9,25},{17,1},{25,9},{2,18},{10... | collective-permute-start | bytes 1572872 | tf_op jit(solution)/shard_map/ppermute | solution.py:584
  329.4 37.0 %collective-permute-start.24 = (bf16[256,1024]{1,0:T(8,128)(2,1)}, bf16[256,1024]{1,0:T(8,128)(2,1)}, u32[]{:S(2)}, u32[]{:S(2)}) collective-permute-start(bf16[256,1024]{1,0:T(8,128)(2,1)} %fusion.22), channel_id=1, source_target_pairs={{0,16},{8,24},{16,0},{24,8},{1,17},{9,25},{17,1},{25,9},{2,18},{10... | collective-permute-start | bytes 1572872 | tf_op jit(solution)/shard_map/ppermute | solution.py:584
  332.8 33.6 %collective-permute-start.25 = (bf16[256,1024]{1,0:T(8,128)(2,1)}, bf16[256,1024]{1,0:T(8,128)(2,1)}, u32[]{:S(2)}, u32[]{:S(2)}) collective-permute-start(bf16[256,1024]{1,0:T(8,128)(2,1)} %add_convert_fusion.7), channel_id=1, source_target_pairs={{0,8},{8,0},{16,24},{24,16},{1,9},{9,1},{17,25},{25,17},{2,10},{10... | collective-permute-start | bytes 1572872 | tf_op jit(solution)/shard_map/ppermute | solution.py:584
  335.4 31.0 %collective-permute-start.27 = (bf16[256,1024]{1,0:T(8,128)(2,1)}, bf16[256,1024]{1,0:T(8,128)(2,1)}, u32[]{:S(2)}, u32[]{:S(2)}) collective-permute-start(bf16[256,1024]{1,0:T(8,128)(2,1)} %add_convert_fusion.5), channel_id=1, source_target_pairs={{0,8},{8,0},{16,24},{24,16},{1,9},{9,1},{17,25},{25,17},{2,10},{10... | collective-permute-start | bytes 1572872 | tf_op jit(solution)/shard_map/ppermute | solution.py:584
  358.2 189.1 %reduce-scatter.8.cloned.1.call-start = ((), (), s32[]{:S(2)}) async-start(), calls=%async_computation.8 | async-start | bytes 7667712 | tf_op jit(solution)/shard_map/reduce_scatter | solution.py:1084
  414.7 39.0 %collective-permute-start.33 = (bf16[256,1024]{1,0:T(8,128)(2,1)}, bf16[256,1024]{1,0:T(8,128)(2,1)S(1)}, u32[]{:S(2)}, u32[]{:S(2)}) collective-permute-start(bf16[256,1024]{1,0:T(8,128)(2,1)} %shard_map.235), channel_id=1, source_target_pairs={{0,8},{8,0},{16,24},{24,16},{1,9},{9,1},{17,25},{25,17},{2,10},{10... | collective-permute-start | bytes 1572872 | tf_op jit(solution)/shard_map/ppermute | solution.py:584
  415.8 38.5 %collective-permute-start.34 = (bf16[256,1024]{1,0:T(8,128)(2,1)}, bf16[256,1024]{1,0:T(8,128)(2,1)S(1)}, u32[]{:S(2)}, u32[]{:S(2)}) collective-permute-start(bf16[256,1024]{1,0:T(8,128)(2,1)} %shard_map.236), channel_id=1, source_target_pairs={{0,16},{8,24},{16,0},{24,8},{1,17},{9,25},{17,1},{25,9},{2,18},{10... | collective-permute-start | bytes 1572872 | tf_op jit(solution)/shard_map/ppermute | solution.py:584
  417.5 36.9 %collective-permute-start.36 = (bf16[256,1024]{1,0:T(8,128)(2,1)}, bf16[256,1024]{1,0:T(8,128)(2,1)S(1)}, u32[]{:S(2)}, u32[]{:S(2)}) collective-permute-start(bf16[256,1024]{1,0:T(8,128)(2,1)} %shard_map.237), channel_id=1, source_target_pairs={{0,8},{8,0},{16,24},{24,16},{1,9},{9,1},{17,25},{25,17},{2,10},{10... | collective-permute-start | bytes 1572872 | tf_op jit(solution)/shard_map/ppermute | solution.py:584
  423.4 48.9 %collective-permute-start.41 = (bf16[2,256,1024]{2,1,0:T(8,128)(2,1)}, bf16[2,256,1024]{2,1,0:T(8,128)(2,1)}, u32[]{:S(2)}, u32[]{:S(2)}) collective-permute-start(bf16[2,256,1024]{2,1,0:T(8,128)(2,1)} %shard_map.241.first_own), channel_id=1, source_target_pairs={{0,8},{8,0},{16,24},{24,16},{1,9},{9,1},{17,25},{25,17},{2,10},{10... | collective-permute-start | bytes 3145736 | tf_op jit(solution)/shard_map/ppermute | solution.py:584
  424.0 48.9 %collective-permute-start.42 = (bf16[2,256,1024]{2,1,0:T(8,128)(2,1)}, bf16[2,256,1024]{2,1,0:T(8,128)(2,1)}, u32[]{:S(2)}, u32[]{:S(2)}) collective-permute-start(bf16[2,256,1024]{2,1,0:T(8,128)(2,1)} %shard_map.242.second_own), channel_id=1, source_target_pairs={{0,16},{8,24},{16,0},{24,8},{1,17},{9,25},{17,1},{25,9},{2,18},{10... | collective-permute-start | bytes 3145736 | tf_op jit(solution)/shard_map/ppermute | solution.py:584
  464.0 44.0 %collective-permute-start.39 = (bf16[2,192,1024]{2,1,0:T(8,128)(2,1)}, bf16[2,192,1024]{2,1,0:T(8,128)(2,1)}, u32[]{:S(2)}, u32[]{:S(2)}) collective-permute-start(bf16[2,192,1024]{2,1,0:T(8,128)(2,1)} %get-tuple-element.102.refs_2_), channel_id=1, source_target_pairs={{0,16},{8,24},{16,0},{24,8},{1,17},{9,25},{17,1},{25,9},{2,18},{10... | collective-permute-start | bytes 2359304 | tf_op jit(solution)/shard_map/ppermute | solution.py:584
  466.9 27.1 %collective-permute-start.47 = (bf16[256,1024]{1,0:T(8,128)(2,1)S(1)}, bf16[256,1024]{1,0:T(8,128)(2,1)}, u32[]{:S(2)}, u32[]{:S(2)}) collective-permute-start(bf16[256,1024]{1,0:T(8,128)(2,1)S(1)} %fusion.20), channel_id=1, source_target_pairs={{0,16},{8,24},{16,0},{24,8},{1,17},{9,25},{17,1},{25,9},{2,18},{10... | collective-permute-start | bytes 1572872 | tf_op jit(solution)/shard_map/ppermute | solution.py:584
  469.7 44.4 %collective-permute-start.37 = (bf16[2,192,1024]{2,1,0:T(8,128)(2,1)}, bf16[2,192,1024]{2,1,0:T(8,128)(2,1)}, u32[]{:S(2)}, u32[]{:S(2)}) collective-permute-start(bf16[2,192,1024]{2,1,0:T(8,128)(2,1)} %get-tuple-element.100.refs_0_), channel_id=1, source_target_pairs={{0,8},{8,0},{16,24},{24,16},{1,9},{9,1},{17,25},{25,17},{2,10},{10... | collective-permute-start | bytes 2359304 | tf_op jit(solution)/shard_map/ppermute | solution.py:584
  472.3 38.8 %collective-permute-start.50 = (bf16[256,1024]{1,0:T(8,128)(2,1)}, bf16[256,1024]{1,0:T(8,128)(2,1)}, u32[]{:S(2)}, u32[]{:S(2)}) collective-permute-start(bf16[256,1024]{1,0:T(8,128)(2,1)} %add_convert_fusion.1), channel_id=1, source_target_pairs={{0,8},{8,0},{16,24},{24,16},{1,9},{9,1},{17,25},{25,17},{2,10},{10... | collective-permute-start | bytes 1572872 | tf_op jit(solution)/shard_map/ppermute | solution.py:584
  473.0 49.9 %collective-permute-start.52 = (bf16[2,256,1024]{2,1,0:T(8,128)(2,1)}, bf16[2,256,1024]{2,1,0:T(8,128)(2,1)}, u32[]{:S(2)}, u32[]{:S(2)}) collective-permute-start(bf16[2,256,1024]{2,1,0:T(8,128)(2,1)} %pad_maximum_fusion.7.first_own), channel_id=1, source_target_pairs={{0,8},{8,0},{16,24},{24,16},{1,9},{9,1},{17,25},{25,17},{2,10},{10... | collective-permute-start | bytes 3145736 | tf_op jit(solution)/shard_map/ppermute | solution.py:584
  494.0 31.6 %collective-permute-start.53 = (bf16[2,256,1024]{2,1,0:T(8,128)(2,1)}, bf16[2,256,1024]{2,1,0:T(8,128)(2,1)}, u32[]{:S(2)}, u32[]{:S(2)}) collective-permute-start(bf16[2,256,1024]{2,1,0:T(8,128)(2,1)} %pad_maximum_fusion.8.second_own), channel_id=1, source_target_pairs={{0,16},{8,24},{16,0},{24,8},{1,17},{9,25},{17,1},{25,9},{2,18},{10... | collective-permute-start | bytes 3145736 | tf_op jit(solution)/shard_map/ppermute | solution.py:584
  508.0 58.3 %collective-permute-start.48 = (bf16[2,256,1024]{2,1,0:T(8,128)(2,1)}, bf16[2,256,1024]{2,1,0:T(8,128)(2,1)S(1)}, u32[]{:S(2)}, u32[]{:S(2)}) collective-permute-start(bf16[2,256,1024]{2,1,0:T(8,128)(2,1)} %shard_map.245.first_own), channel_id=1, source_target_pairs={{0,8},{8,0},{16,24},{24,16},{1,9},{9,1},{17,25},{25,17},{2,10},{10... | collective-permute-start | bytes 3145736 | tf_op jit(solution)/shard_map/ppermute | solution.py:584
  511.1 34.0 %collective-permute-start.40 = (bf16[192,1024]{1,0:T(8,128)(2,1)}, bf16[192,1024]{1,0:T(8,128)(2,1)}, u32[]{:S(2)}, u32[]{:S(2)}) collective-permute-start(bf16[192,1024]{1,0:T(8,128)(2,1)} %fusion.34), channel_id=1, source_target_pairs={{0,8},{8,0},{16,24},{24,16},{1,9},{9,1},{17,25},{25,17},{2,10},{10... | collective-permute-start | bytes 1179656 | tf_op jit(solution)/shard_map/ppermute | solution.py:584
  514.1 52.2 %collective-permute-start.51 = (bf16[2,256,1024]{2,1,0:T(8,128)(2,1)}, bf16[2,256,1024]{2,1,0:T(8,128)(2,1)S(1)}, u32[]{:S(2)}, u32[]{:S(2)}) collective-permute-start(bf16[2,256,1024]{2,1,0:T(8,128)(2,1)} %shard_map.246.second_own), channel_id=1, source_target_pairs={{0,16},{8,24},{16,0},{24,8},{1,17},{9,25},{17,1},{25,9},{2,18},{10... | collective-permute-start | bytes 3145736 | tf_op jit(solution)/shard_map/ppermute | solution.py:584
  522.9 30.0 %collective-permute-start.38 = (bf16[192,1024]{1,0:T(8,128)(2,1)S(1)}, bf16[192,1024]{1,0:T(8,128)(2,1)}, u32[]{:S(2)}, u32[]{:S(2)}) collective-permute-start(bf16[192,1024]{1,0:T(8,128)(2,1)S(1)} %fusion.33), channel_id=1, source_target_pairs={{0,16},{8,24},{16,0},{24,8},{1,17},{9,25},{17,1},{25,9},{2,18},{10... | collective-permute-start | bytes 1179656 | tf_op jit(solution)/shard_map/ppermute | solution.py:584
  (114 other events, 1047.3 us)
Sparse Core Ops, SparseCore 0:
  10.5 67.4 all-gather.3
  80.2 63.3 all-gather.5
  154.1 61.9 all-gather.7
  279.7 66.6 reduce-scatter.5
  358.3 67.8 reduce-scatter.3
  472.4 72.1 reduce-scatter.7

commit v4 on v3

--- a/solution.py
+++ b/solution.py
@@ -414,7 +414,7 @@
     value_ref[...] = value
     for h in range(GROUP):
         head = pl.ds(h * HEAD_WIDTH, HEAD_WIDTH)
-        for rows in pieces(query_in.shape[0], 256):
+        for rows in pieces(query_in.shape[0], 384):
             query = turned(query_in[rows, head], cos_ref[rows, :], sin_ref[rows, :]).astype(BF16)
             query_ref[rows, head] = query
             scores = product(query, key, NT) * scale + bias_ref[rows, :]

time: 602 us -> 602 us (level)
  transfers between devices with their start and end apart: 60 -> 60, of which waited for: 23 -> 25; matrix products, arithmetic and copies ran while one was open for 14% -> 14% of each run, Pallas kernels for 28% -> 28%
where the time goes in v4:
time: 602 us; the launch traced here: 591 us
  Pallas kernels  197 us (33%)
  waiting for transfers between devices  191 us (32%)
  other arithmetic  70.5 us (12%)
  starting transfers between devices  65.7 us (11%)
  local copies, waits for them, and re-layouts  31 us (5%)
  between operations  24.1 us (4%)
  blocking collectives  12.1 us (2%)
    ppermute x54, waiting for transfers between devices, swap(): return lax.ppermute(x, 'ctx', [(i, i ^ bit) for i in range(4)])  154 us
    ppermute x54, starting transfers between devices, swap(): return lax.ppermute(x, 'ctx', [(i, i ^ bit) for i in range(4)])  64.9 us
    pallas_call x6, Pallas kernels, weight_grad(): pl.pallas_call(weight_grad_kernel, out_shape=[jax.ShapeDtypeStruct((2, he...  46.7 us
    pallas_call x2, Pallas kernels, hidden_grads(): pl.pallas_call(hidden_kernel, out_shape=[jax.ShapeDtypeStruct((count, 2 *...  34.4 us
    pallas_call x2, Pallas kernels, rows_product(): pl.pallas_call(rows_product_kernel, out_shape=jax.ShapeDtypeStruct((count...  28.9 us
    convert_element_type x16, other arithmetic, sum_low(): return sum((t.astype(F32) for t in terms)).astype(BF16)  28.1 us
    all_gather x1, waiting for transfers between devices, local(): lax.all_gather(after(ffn_low, cot_all), 'fsdp', axis=0, tiled=True)  22 us
    pallas_call x3, Pallas kernels, lay_out(): pl.pallas_call(lay_out_kernel, out_shape=jax.ShapeDtypeStruct((4 * height...  21.6 us
  transfers between devices with their start and end apart: 60, of which 25 were waited for; matrix products, arithmetic and copies ran while one was open for 14% of the time, Pallas kernels for 28%

profile of v4, /device:TPU:0, one launch (start us, length us, event | category | flops | bytes accessed | tf_op | source)
XLA Modules:
  0.0 591.4 jit_solution(15027437124952345565)
XLA Ops:
  15.2 12.1 %all_gather.12.refs_1_ = bf16[2,2048]{1,0:T(2,128)(2,1)} all-gather(bf16[2,256]{1,0:T(2,128)(2,1)S(1)} %pad_maximum_fusion.23), channel_id=1, replica_groups=mesh['ctx'=4,'fsdp'=8] {'fsdp'}, dimensions={1}, use_global_device_ids=true | all-gather | bytes 9216 | tf_op jit(solution)/shard_map/all_gather | solution.py:900
  31.3 17.0 %collective-permute-done.2.refs_3_.refs_1_ = bf16[2,192,1024]{2,1,0:T(8,128)(2,1)S(1)} collective-permute-done((bf16[2,192,1024]{2,1,0:T(8,128)(2,1)}, bf16[2,192,1024]{2,1,0:T(8,128)(2,1)S(1)}, u32[]{:S(2)}, u32[]{:S(2)}) %collective-permute-start.2) | collective-permute-done | bytes 786464 | tf_op jit(solution)/shard_map/ppermute | solution.py:584
  63.0 15.0 %all-gather.4.cloned.1.call-done.refs_6_.rhs_ref = bf16[2048,1536]{1,0:T(8,128)(2,1)} async-done(((bf16[256,1536]{1,0:T(8,128)(2,1)}), bf16[2048,1536]{1,0:T(8,128)(2,1)}) %all-gather.4.cloned.1.call-update) | async-done | bytes 6291472 | tf_op jit(solution)/shard_map/all_gather | solution.py:899
  87.9 9.1 %shard_map.216 = (bf16[768,2048]{1,0:T(8,128)(2,1)}, f32[768,1024]{1,0:T(8,128)}) custom-call(bf16[192,2048]{1,0:T(8,128)(2,1)} %bitcast.166, bf16[192,1024]{1,0:T(8,128)(2,1)} %copy-done.57, bf16[192,1024]{1,0:T(8,128)(2,1)} %copy-done.58, bf16[2,192,1024]{2,1,0:T(8,128)(2,1)} %copy-done.36, bf16[2,192,1024]{2,1,0:T(8,128)(2,1)} %copy-done.37, ...), custom_call_target="tpu_custom_call" | custom-call | flops 300000000 | bytes 1107000 | tf_op jit(solution)/shard_map/pallas_call | solution.py:104
  97.1 9.7 %shard_map.217 = (bf16[768,512]{1,0:T(8,128)(2,1)}, bf16[768,256]{1,0:T(8,128)(2,1)}, bf16[768,256]{1,0:T(8,128)(2,1)}, bf16[4,768,768]{2,1,0:T(8,128)(2,1)}, bf16[768,512]{1,0:T(8,128)(2,1)}) custom-call(f32[768,1024]{1,0:T(8,128)} %get-tuple-element.58.query_in.key_in.value_in, f32[768,1024]{1,0:T(8,128)} %get-tuple-element.58.query_in.key_in.value_in, ...), custom_call_target="tpu_custom_call" | custom-call | flops 300000000 | bytes 1107000 | tf_op jit(solution)/shard_map/pallas_call | solution.py:438
  118.7 17.3 %collective-permute-done.9 = bf16[2,192,1024]{2,1,0:T(8,128)(2,1)S(1)} collective-permute-done((bf16[2,192,1024]{2,1,0:T(8,128)(2,1)}, bf16[2,192,1024]{2,1,0:T(8,128)(2,1)S(1)}, u32[]{:S(2)}, u32[]{:S(2)}) %collective-permute-start.9) | collective-permute-done | bytes 786464 | tf_op jit(solution)/shard_map/ppermute | solution.py:584
  140.6 6.8 %collective-permute-done.10 = bf16[192,1024]{1,0:T(8,128)(2,1)S(1)} collective-permute-done((bf16[192,1024]{1,0:T(8,128)(2,1)S(1)}, bf16[192,1024]{1,0:T(8,128)(2,1)S(1)}, u32[]{:S(2)}, u32[]{:S(2)}) %collective-permute-start.10) | collective-permute-done | bytes 393248 | tf_op jit(solution)/shard_map/ppermute | solution.py:584
  164.6 6.6 %collective-permute-done.11 = bf16[4,192,256]{2,1,0:T(8,128)(2,1)S(1)} collective-permute-done((bf16[4,192,256]{2,1,0:T(8,128)(2,1)S(1)}, bf16[4,192,256]{2,1,0:T(8,128)(2,1)S(1)}, u32[]{:S(2)}, u32[]{:S(2)}) %collective-permute-start.11) | collective-permute-done | bytes 393248 | tf_op jit(solution)/shard_map/ppermute | solution.py:584
  175.7 14.3 %collective-permute-done.12 = bf16[2,4,192,256]{3,2,1,0:T(8,128)(2,1)S(1)} collective-permute-done((bf16[2,4,192,256]{3,2,1,0:T(8,128)(2,1)S(1)}, bf16[2,4,192,256]{3,2,1,0:T(8,128)(2,1)S(1)}, u32[]{:S(2)}, u32[]{:S(2)}) %collective-permute-start.12) | collective-permute-done | bytes 786464 | tf_op jit(solution)/shard_map/ppermute | solution.py:584
  194.0 22.0 %all-gather.8.cloned.1.call-done.x_ref.b_ref = bf16[1536,2048]{1,0:T(8,128)(2,1)} async-done(((bf16[192,2048]{1,0:T(8,128)(2,1)}), bf16[1536,2048]{1,0:T(8,128)(2,1)}) %all-gather.8.cloned.1.call-update) | async-done | bytes 6291472 | tf_op jit(solution)/shard_map/all_gather | solution.py:934
  215.9 17.2 %shard_map.221 = (bf16[1536,1024]{1,0:T(8,128)(2,1)}, bf16[1536,2048]{1,0:T(8,128)(2,1)}, bf16[512,1536]{1,0:T(8,128)(2,1)}, bf16[512,1536]{1,0:T(8,128)(2,1)}, bf16[512,1536]{1,0:T(8,128)(2,1)}) custom-call(bf16[1536,2048]{1,0:T(8,128)(2,1)} %all-gather.8.cloned.1.call-done.x_ref.b_ref, ...), custom_call_target="tpu_custom_call" | custom-call | flops 300000000 | bytes 1107000 | tf_op jit(solution)/shard_map/pallas_call | solution.py:148
  233.2 7.7 %shard_map.222 = (bf16[2,256,1024]{2,1,0:T(8,128)(2,1)}, bf16[256,1024]{1,0:T(8,128)(2,1)}, bf16[256,1024]{1,0:T(8,128)(2,1)}) custom-call(bf16[512,1536]{1,0:T(8,128)(2,1)} %get-tuple-element.66.a_ref, bf16[1536,2048]{1,0:T(8,128)(2,1)} %all-gather.6.cloned.1.call-done.refs_1_.cot_ref.b_ref), custom_call_target="tpu_custom_call" | custom-call | flops 300000000 | bytes 1107000 | tf_op jit(solution)/shard_map/pallas_call | solution.py:275
  243.9 17.2 %shard_map.223 = (bf16[1536,1024]{1,0:T(8,128)(2,1)}, bf16[1536,2048]{1,0:T(8,128)(2,1)}, bf16[512,1536]{1,0:T(8,128)(2,1)}, bf16[512,1536]{1,0:T(8,128)(2,1)}, bf16[512,1536]{1,0:T(8,128)(2,1)}) custom-call(bf16[1536,2048]{1,0:T(8,128)(2,1)} %all-gather.8.cloned.1.call-done.x_ref.b_ref, ...), custom_call_target="tpu_custom_call", output_to_operand_aliasing={{0}: (4, {}), {1}: (5, {})} | custom-call | flops 300000000 | bytes 1107000 | tf_op jit(solution)/shard_map/pallas_call | solution.py:148
  261.0 18.3 %shard_map.224.refs_0_ = bf16[1536,2048]{1,0:T(8,128)(2,1)} custom-call(bf16[1536,2048]{1,0:T(8,128)(2,1)} %get-tuple-element.74.a_ref, bf16[2048,2048]{1,0:T(8,128)(2,1)} %copy-done.9, bf16[512,1536]{1,0:T(8,128)(2,1)} %get-tuple-element.72.refs_0_.a_ref), custom_call_target="tpu_custom_call" | custom-call | flops 300000000 | bytes 1107000 | tf_op jit(solution)/shard_map/pallas_call | solution.py:184
  282.9 7.6 %shard_map.225 = (bf16[2,256,1024]{2,1,0:T(8,128)(2,1)}, bf16[256,1024]{1,0:T(8,128)(2,1)}, bf16[256,1024]{1,0:T(8,128)(2,1)}) custom-call(bf16[512,1536]{1,0:T(8,128)(2,1)} %get-tuple-element.73.a_ref, bf16[1536,2048]{1,0:T(8,128)(2,1)} %all-gather.8.cloned.1.call-done.x_ref.b_ref, bf16[1536,2048]{1,0:T(8,128)(2,1)} %shard_map.224.refs_0_, ...), custom_call_target="tpu_custom_call" | custom-call | flops 300000000 | bytes 1107000 | tf_op jit(solution)/shard_map/pallas_call | solution.py:275
  292.9 7.8 %shard_map.226 = (bf16[2,256,1024]{2,1,0:T(8,128)(2,1)}, bf16[256,1024]{1,0:T(8,128)(2,1)}, bf16[256,1024]{1,0:T(8,128)(2,1)}) custom-call(bf16[512,1536]{1,0:T(8,128)(2,1)} %get-tuple-element.72.refs_0_.a_ref, bf16[1536,2048]{1,0:T(8,128)(2,1)} %all-gather.6.cloned.1.call-done.refs_1_.cot_ref.b_ref, bf16[2,256,1024]{2,1,0:T(8,128)(2,1)} %get-tuple-element.75.refs_0_, ...), custom_call_target="tpu_custom_call" | custom-call | flops 300000000 | bytes 1107000 | tf_op jit(solution)/shard_map/pallas_call | solution.py:275
  304.8 7.8 %shard_map.227 = (bf16[2,256,1024]{2,1,0:T(8,128)(2,1)}, bf16[256,1024]{1,0:T(8,128)(2,1)}, bf16[256,1024]{1,0:T(8,128)(2,1)}) custom-call(bf16[512,1536]{1,0:T(8,128)(2,1)} %get-tuple-element.71.a_ref, bf16[1536,2048]{1,0:T(8,128)(2,1)} %all-gather.8.cloned.1.call-done.x_ref.b_ref, bf16[2,256,1024]{2,1,0:T(8,128)(2,1)} %get-tuple-element.78.refs_0_, ...), custom_call_target="tpu_custom_call" | custom-call | flops 299999985664 | bytes 1107000064 | tf_op jit(solution)/shard_map/pallas_call | solution.py:275
  321.8 7.4 %collective-permute-done.19.refs_5_ = bf16[256,1024]{1,0:T(8,128)(2,1)} collective-permute-done((bf16[256,1024]{1,0:T(8,128)(2,1)}, bf16[256,1024]{1,0:T(8,128)(2,1)}, u32[]{:S(2)}, u32[]{:S(2)}) %collective-permute-start.19) | collective-permute-done | bytes 524320 | tf_op jit(solution)/shard_map/ppermute | solution.py:584
  336.7 10.6 %shard_map.228.refs_0_ = bf16[1536,2048]{1,0:T(8,128)(2,1)} custom-call(bf16[1536,1024]{1,0:T(8,128)(2,1)} %get-tuple-element.70.a_ref, bf16[1024,2048]{1,0:T(8,128)(2,1)} %pad_maximum_fusion.down_ref.w_ref, bf16[2,256,1024]{2,1,0:T(8,128)(2,1)} %get-tuple-element.81.refs_0_, bf16[256,1024]{1,0:T(8,128)(2,1)} %get-tuple-element.82.refs_1_, ...), custom_call_target="tpu_custom_call" | custom-call | flops 299999985664 | bytes 1107000064 | tf_op jit(solution)/shard_map/pallas_call | solution.py:184
  347.3 7.6 %shard_map.229 = (bf16[2,256,1024]{2,1,0:T(8,128)(2,1)}, bf16[256,1024]{1,0:T(8,128)(2,1)}, bf16[256,1024]{1,0:T(8,128)(2,1)}) custom-call(bf16[512,1536]{1,0:T(8,128)(2,1)} %get-tuple-element.85.a_ref, bf16[1536,2048]{1,0:T(8,128)(2,1)} %all-gather.8.cloned.1.call-done.x_ref.b_ref, bf16[1536,2048]{1,0:T(8,128)(2,1)} %shard_map.228.refs_0_, ...), custom_call_target="tpu_custom_call" | custom-call | flops 299999985664 | bytes 1107000064 | tf_op jit(solution)/shard_map/pallas_call | solution.py:275
  358.3 8.0 %shard_map.230 = (bf16[2,256,1024]{2,1,0:T(8,128)(2,1)}, bf16[256,1024]{1,0:T(8,128)(2,1)}, bf16[256,1024]{1,0:T(8,128)(2,1)}) custom-call(bf16[512,1536]{1,0:T(8,128)(2,1)} %get-tuple-element.84.a_ref, bf16[1536,2048]{1,0:T(8,128)(2,1)} %all-gather.8.cloned.1.call-done.x_ref.b_ref, bf16[2,256,1024]{2,1,0:T(8,128)(2,1)} %get-tuple-element.86.refs_0_, ...), custom_call_target="tpu_custom_call" | custom-call | flops 299999985664 | bytes 1107000064 | tf_op jit(solution)/shard_map/pallas_call | solution.py:275
  393.4 7.5 %collective-permute-done.30.refs_3_.refs_1_ = bf16[2,192,1024]{2,1,0:T(8,128)(2,1)S(1)} collective-permute-done((bf16[2,192,1024]{2,1,0:T(8,128)(2,1)S(1)}, bf16[2,192,1024]{2,1,0:T(8,128)(2,1)S(1)}, u32[]{:S(2)}, u32[]{:S(2)}) %collective-permute-start.30) | collective-permute-done | bytes 786464 | tf_op jit(solution)/shard_map/ppermute | solution.py:584
  404.7 7.5 %collective-permute-done.35 = bf16[256,1024]{1,0:T(8,128)(2,1)} collective-permute-done((bf16[256,1024]{1,0:T(8,128)(2,1)}, bf16[256,1024]{1,0:T(8,128)(2,1)}, u32[]{:S(2)}, u32[]{:S(2)}) %collective-permute-start.35) | collective-permute-done | bytes 524320 | tf_op jit(solution)/shard_map/ppermute | solution.py:584
  426.0 16.2 %shard_map.232 = (bf16[768,1024]{1,0:T(8,128)(2,1)}, bf16[768,512]{1,0:T(8,128)(2,1)}) custom-call(s32[1]{0:T(128)} %bitcast.59.place_ref, bf16[768,512]{1,0:T(8,128)(2,1)} %get-tuple-element.92.query_ref, bf16[768,256]{1,0:T(8,128)(2,1)} %get-tuple-element.93.key_ref, bf16[768,256]{1,0:T(8,128)(2,1)} %get-tuple-element.94.value_ref, ...), custom_call_target="tpu_custom_call" | custom-call | flops 300000000 | bytes 1107000 | tf_op jit(solution)/shard_map/pallas_call | solution.py:539
  443.5 10.1 %shard_map.233.refs_1_.refs_0_ = bf16[2048,1664]{1,0:T(8,128)(2,1)} custom-call(bf16[768,2048]{1,0:T(8,128)(2,1)} %get-tuple-element.97.refs_0_, bf16[768,2048]{1,0:T(8,128)(2,1)} %pad_maximum_fusion.1.refs_0_.refs_1_, bf16[768,1024]{1,0:T(8,128)(2,1)} %get-tuple-element.96.refs_2_.refs_0_, bf16[768,512]{1,0:T(8,128)(2,1)} %get-tuple-element.98.refs_3_, ...), custom_call_target="tpu_custom_call" | custom-call | flops 300000000 | bytes 1107000 | tf_op jit(solution)/shard_map/pallas_call | solution.py:370
  455.8 8.0 %shard_map.239 = (bf16[2,192,1024]{2,1,0:T(8,128)(2,1)}, bf16[2,192,1024]{2,1,0:T(8,128)(2,1)}, bf16[2,192,1024]{2,1,0:T(8,128)(2,1)}, bf16[2,192,1024]{2,1,0:T(8,128)(2,1)}) custom-call(bf16[768,1024]{1,0:T(8,128)(2,1)} %shard_map.238.lhs_ref, bf16[2048,1536]{1,0:T(8,128)(2,1)} %all-gather.4.cloned.1.call-done.refs_6_.rhs_ref), custom_call_target="tpu_custom_call" | custom-call | flops 300000000 | bytes 1107000 | tf_op jit(solution)/shard_map/pallas_call | solution.py:327
  474.2 19.6 %collective-permute-done.47 = bf16[256,1024]{1,0:T(8,128)(2,1)} collective-permute-done((bf16[256,1024]{1,0:T(8,128)(2,1)S(1)}, bf16[256,1024]{1,0:T(8,128)(2,1)}, u32[]{:S(2)}, u32[]{:S(2)}) %collective-permute-start.47) | collective-permute-done | bytes 524320 | tf_op jit(solution)/shard_map/ppermute | solution.py:584
  497.8 7.9 %shard_map.243.refs_1_ = f32[1024,2048]{1,0:T(8,128)} custom-call(s32[8]{0:T(128)S(1)} %broadcast_xor_fusion.place_ref, bf16[2,256,1024]{2,1,0:T(8,128)(2,1)S(1)} %copy-done.3, bf16[2,256,1024]{2,1,0:T(8,128)(2,1)} %collective-permute-done.41.first_got, bf16[2,256,1024]{2,1,0:T(8,128)(2,1)S(1)} %copy-done.2, ...), custom_call_target="tpu_custom_call" | custom-call | flops 299999985664 | bytes 1107000064 | tf_op jit(solution)/shard_map/pallas_call | solution.py:774
  515.5 7.2 %collective-permute-done.52.first_got = bf16[2,256,1024]{2,1,0:T(8,128)(2,1)} collective-permute-done((bf16[2,256,1024]{2,1,0:T(8,128)(2,1)}, bf16[2,256,1024]{2,1,0:T(8,128)(2,1)}, u32[]{:S(2)}, u32[]{:S(2)}) %collective-permute-start.52) | collective-permute-done | bytes 1048608 | tf_op jit(solution)/shard_map/ppermute | solution.py:584
  525.4 8.6 %shard_map.249 = f32[1024,2048]{1,0:T(8,128)} custom-call(s32[8]{0:T(128)S(1)} %broadcast_xor_fusion.place_ref, bf16[2,256,1024]{2,1,0:T(8,128)(2,1)} %pad_maximum_fusion.7.first_own, bf16[2,256,1024]{2,1,0:T(8,128)(2,1)} %collective-permute-done.52.first_got, bf16[2,256,1024]{2,1,0:T(8,128)(2,1)} %pad_maximum_fusion.8.second_own, ...), custom_call_target="tpu_custom_call" | custom-call | flops 300000000 | bytes 1107000 | tf_op jit(solution)/shard_map/pallas_call | solution.py:774
  534.0 10.9 %collective-permute-done.40 = bf16[192,1024]{1,0:T(8,128)(2,1)} collective-permute-done((bf16[192,1024]{1,0:T(8,128)(2,1)}, bf16[192,1024]{1,0:T(8,128)(2,1)}, u32[]{:S(2)}, u32[]{:S(2)}) %collective-permute-start.40) | collective-permute-done | bytes 393248 | tf_op jit(solution)/shard_map/ppermute | solution.py:584
  578.3 6.0 %shard_map.248 = (f32[256,4096]{1,0:T(8,128)}, f32[256,2048]{1,0:T(8,128)}, f32[1,256]{1,0:T(1,128)}, f32[1,256]{1,0:T(1,128)}) custom-call(s32[4]{0:T(128)} %copy-done.76, bf16[256,4096]{1,0:T(8,128)(2,1)} %weight_ref.1, f32[1,256]{1,0:T(1,128)} %reshape_convert_fusion.gain_ref, bf16[256,1664]{1,0:T(8,128)(2,1)} %shard_map.244.refs_0_, ...), custom_call_target="tpu_custom_call" | custom-call | flops 300000000 | bytes 1107000 | tf_op jit(solution)/shard_map/pallas_call | solution.py:738
  (400 shorter events, 210.2 us)
Async XLA Ops:
  7.2 70.8 %all-gather.4.cloned.1.call-start = ((), (), s32[]{:S(2)}) async-start(), calls=%async_computation.3 | async-start | bytes 7077888 | tf_op jit(solution)/shard_map/all_gather | solution.py:899
  10.3 143.0 %all-gather.6.cloned.1.call-start = ((), (), s32[]{:S(2)}) async-start(), calls=%async_computation.4 | async-start | bytes 7077888 | tf_op jit(solution)/shard_map/all_gather | solution.py:904
  50.4 165.5 %all-gather.8.cloned.1.call-start = ((), (), s32[]{:S(2)}) async-start(), calls=%async_computation.5 | async-start | bytes 7077888 | tf_op jit(solution)/shard_map/all_gather | solution.py:934
  80.9 25.9 %collective-permute-start.4 = (bf16[512,512]{1,0:T(8,128)(2,1)}, bf16[512,512]{1,0:T(8,128)(2,1)S(1)}, u32[]{:S(2)}, u32[]{:S(2)}) collective-permute-start(bf16[512,512]{1,0:T(8,128)(2,1)} %get-tuple-element.123), channel_id=1, source_target_pairs={{0,24},{8,16},{16,8},{24,0},{1,25},{9,17},{17,9},{25,1},{2,26},{10... | collective-permute-start | bytes 1572872 | tf_op jit(solution)/shard_map/ppermute | solution.py:584
  153.4 214.1 %reduce-scatter.6.cloned.1.call-start = ((), (), s32[]{:S(2)}) async-start(), calls=%async_computation.7 | async-start | bytes 7077888 | tf_op jit(solution)/shard_map/reduce_scatter | solution.py:967
  240.9 41.0 %collective-permute-start.15 = (bf16[2,256,1024]{2,1,0:T(8,128)(2,1)}, bf16[2,256,1024]{2,1,0:T(8,128)(2,1)S(1)}, u32[]{:S(2)}, u32[]{:S(2)}) collective-permute-start(bf16[2,256,1024]{2,1,0:T(8,128)(2,1)} %get-tuple-element.67.refs_2_), channel_id=1, source_target_pairs={{0,8},{8,0},{16,24},{24,16},{1,9},{9,1},{17,25},{25,17},{2,10},{10... | collective-permute-start | bytes 3145736 | tf_op jit(solution)/shard_map/ppermute | solution.py:584
  242.4 37.0 %collective-permute-start.16 = (bf16[256,1024]{1,0:T(8,128)(2,1)}, bf16[256,1024]{1,0:T(8,128)(2,1)S(1)}, u32[]{:S(2)}, u32[]{:S(2)}) collective-permute-start(bf16[256,1024]{1,0:T(8,128)(2,1)} %get-tuple-element.69.refs_4_), channel_id=1, source_target_pairs={{0,16},{8,24},{16,0},{24,8},{1,17},{9,25},{17,1},{25,9},{2,18},{10... | collective-permute-start | bytes 1572872 | tf_op jit(solution)/shard_map/ppermute | solution.py:584
  279.4 192.7 %reduce-scatter.4.cloned.1.call-start = ((), (), s32[]{:S(2)}) async-start(), calls=%async_computation.6 | async-start | bytes 7077888 | tf_op jit(solution)/shard_map/reduce_scatter | solution.py:1027
  281.4 39.3 %collective-permute-start.18 = (bf16[256,1024]{1,0:T(8,128)(2,1)}, bf16[256,1024]{1,0:T(8,128)(2,1)}, u32[]{:S(2)}, u32[]{:S(2)}) collective-permute-start(bf16[256,1024]{1,0:T(8,128)(2,1)} %add_convert_fusion.8), channel_id=1, source_target_pairs={{0,8},{8,0},{16,24},{24,16},{1,9},{9,1},{17,25},{25,17},{2,10},{10... | collective-permute-start | bytes 1572872 | tf_op jit(solution)/shard_map/ppermute | solution.py:584
  290.6 44.7 %collective-permute-start.20 = (bf16[2,256,1024]{2,1,0:T(8,128)(2,1)}, bf16[2,256,1024]{2,1,0:T(8,128)(2,1)}, u32[]{:S(2)}, u32[]{:S(2)}) collective-permute-start(bf16[2,256,1024]{2,1,0:T(8,128)(2,1)} %get-tuple-element.75.refs_0_), channel_id=1, source_target_pairs={{0,8},{8,0},{16,24},{24,16},{1,9},{9,1},{17,25},{25,17},{2,10},{10... | collective-permute-start | bytes 3145736 | tf_op jit(solution)/shard_map/ppermute | solution.py:584
  292.0 40.6 %collective-permute-start.21 = (bf16[256,1024]{1,0:T(8,128)(2,1)}, bf16[256,1024]{1,0:T(8,128)(2,1)}, u32[]{:S(2)}, u32[]{:S(2)}) collective-permute-start(bf16[256,1024]{1,0:T(8,128)(2,1)} %get-tuple-element.77.refs_2_), channel_id=1, source_target_pairs={{0,16},{8,24},{16,0},{24,8},{1,17},{9,25},{17,1},{25,9},{2,18},{10... | collective-permute-start | bytes 1572872 | tf_op jit(solution)/shard_map/ppermute | solution.py:584
  318.0 29.4 %collective-permute-start.22 = (bf16[2,256,1024]{2,1,0:T(8,128)(2,1)}, bf16[2,256,1024]{2,1,0:T(8,128)(2,1)}, u32[]{:S(2)}, u32[]{:S(2)}) collective-permute-start(bf16[2,256,1024]{2,1,0:T(8,128)(2,1)} %get-tuple-element.81.refs_0_), channel_id=1, source_target_pairs={{0,8},{8,0},{16,24},{24,16},{1,9},{9,1},{17,25},{25,17},{2,10},{10... | collective-permute-start | bytes 3145736 | tf_op jit(solution)/shard_map/ppermute | solution.py:584
  320.7 26.6 %collective-permute-start.23 = (bf16[256,1024]{1,0:T(8,128)(2,1)}, bf16[256,1024]{1,0:T(8,128)(2,1)}, u32[]{:S(2)}, u32[]{:S(2)}) collective-permute-start(bf16[256,1024]{1,0:T(8,128)(2,1)} %get-tuple-element.83.refs_2_), channel_id=1, source_target_pairs={{0,16},{8,24},{16,0},{24,8},{1,17},{9,25},{17,1},{25,9},{2,18},{10... | collective-permute-start | bytes 1572872 | tf_op jit(solution)/shard_map/ppermute | solution.py:584
  329.2 37.0 %collective-permute-start.24 = (bf16[256,1024]{1,0:T(8,128)(2,1)}, bf16[256,1024]{1,0:T(8,128)(2,1)}, u32[]{:S(2)}, u32[]{:S(2)}) collective-permute-start(bf16[256,1024]{1,0:T(8,128)(2,1)} %fusion.22), channel_id=1, source_target_pairs={{0,16},{8,24},{16,0},{24,8},{1,17},{9,25},{17,1},{25,9},{2,18},{10... | collective-permute-start | bytes 1572872 | tf_op jit(solution)/shard_map/ppermute | solution.py:584
  332.7 33.6 %collective-permute-start.25 = (bf16[256,1024]{1,0:T(8,128)(2,1)}, bf16[256,1024]{1,0:T(8,128)(2,1)}, u32[]{:S(2)}, u32[]{:S(2)}) collective-permute-start(bf16[256,1024]{1,0:T(8,128)(2,1)} %add_convert_fusion.7), channel_id=1, source_target_pairs={{0,8},{8,0},{16,24},{24,16},{1,9},{9,1},{17,25},{25,17},{2,10},{10... | collective-permute-start | bytes 1572872 | tf_op jit(solution)/shard_map/ppermute | solution.py:584
  335.2 31.0 %collective-permute-start.27 = (bf16[256,1024]{1,0:T(8,128)(2,1)}, bf16[256,1024]{1,0:T(8,128)(2,1)}, u32[]{:S(2)}, u32[]{:S(2)}) collective-permute-start(bf16[256,1024]{1,0:T(8,128)(2,1)} %add_convert_fusion.5), channel_id=1, source_target_pairs={{0,8},{8,0},{16,24},{24,16},{1,9},{9,1},{17,25},{25,17},{2,10},{10... | collective-permute-start | bytes 1572872 | tf_op jit(solution)/shard_map/ppermute | solution.py:584
  358.0 189.0 %reduce-scatter.8.cloned.1.call-start = ((), (), s32[]{:S(2)}) async-start(), calls=%async_computation.8 | async-start | bytes 7667712 | tf_op jit(solution)/shard_map/reduce_scatter | solution.py:1084
  414.6 39.0 %collective-permute-start.33 = (bf16[256,1024]{1,0:T(8,128)(2,1)}, bf16[256,1024]{1,0:T(8,128)(2,1)S(1)}, u32[]{:S(2)}, u32[]{:S(2)}) collective-permute-start(bf16[256,1024]{1,0:T(8,128)(2,1)} %shard_map.235), channel_id=1, source_target_pairs={{0,8},{8,0},{16,24},{24,16},{1,9},{9,1},{17,25},{25,17},{2,10},{10... | collective-permute-start | bytes 1572872 | tf_op jit(solution)/shard_map/ppermute | solution.py:584
  415.7 38.5 %collective-permute-start.34 = (bf16[256,1024]{1,0:T(8,128)(2,1)}, bf16[256,1024]{1,0:T(8,128)(2,1)S(1)}, u32[]{:S(2)}, u32[]{:S(2)}) collective-permute-start(bf16[256,1024]{1,0:T(8,128)(2,1)} %shard_map.236), channel_id=1, source_target_pairs={{0,16},{8,24},{16,0},{24,8},{1,17},{9,25},{17,1},{25,9},{2,18},{10... | collective-permute-start | bytes 1572872 | tf_op jit(solution)/shard_map/ppermute | solution.py:584
  417.3 36.9 %collective-permute-start.36 = (bf16[256,1024]{1,0:T(8,128)(2,1)}, bf16[256,1024]{1,0:T(8,128)(2,1)S(1)}, u32[]{:S(2)}, u32[]{:S(2)}) collective-permute-start(bf16[256,1024]{1,0:T(8,128)(2,1)} %shard_map.237), channel_id=1, source_target_pairs={{0,8},{8,0},{16,24},{24,16},{1,9},{9,1},{17,25},{25,17},{2,10},{10... | collective-permute-start | bytes 1572872 | tf_op jit(solution)/shard_map/ppermute | solution.py:584
  423.2 48.9 %collective-permute-start.41 = (bf16[2,256,1024]{2,1,0:T(8,128)(2,1)}, bf16[2,256,1024]{2,1,0:T(8,128)(2,1)}, u32[]{:S(2)}, u32[]{:S(2)}) collective-permute-start(bf16[2,256,1024]{2,1,0:T(8,128)(2,1)} %shard_map.241.first_own), channel_id=1, source_target_pairs={{0,8},{8,0},{16,24},{24,16},{1,9},{9,1},{17,25},{25,17},{2,10},{10... | collective-permute-start | bytes 3145736 | tf_op jit(solution)/shard_map/ppermute | solution.py:584
  423.9 48.9 %collective-permute-start.42 = (bf16[2,256,1024]{2,1,0:T(8,128)(2,1)}, bf16[2,256,1024]{2,1,0:T(8,128)(2,1)}, u32[]{:S(2)}, u32[]{:S(2)}) collective-permute-start(bf16[2,256,1024]{2,1,0:T(8,128)(2,1)} %shard_map.242.second_own), channel_id=1, source_target_pairs={{0,16},{8,24},{16,0},{24,8},{1,17},{9,25},{17,1},{25,9},{2,18},{10... | collective-permute-start | bytes 3145736 | tf_op jit(solution)/shard_map/ppermute | solution.py:584
  463.9 44.0 %collective-permute-start.39 = (bf16[2,192,1024]{2,1,0:T(8,128)(2,1)}, bf16[2,192,1024]{2,1,0:T(8,128)(2,1)}, u32[]{:S(2)}, u32[]{:S(2)}) collective-permute-start(bf16[2,192,1024]{2,1,0:T(8,128)(2,1)} %get-tuple-element.102.refs_2_), channel_id=1, source_target_pairs={{0,16},{8,24},{16,0},{24,8},{1,17},{9,25},{17,1},{25,9},{2,18},{10... | collective-permute-start | bytes 2359304 | tf_op jit(solution)/shard_map/ppermute | solution.py:584
  466.8 27.1 %collective-permute-start.47 = (bf16[256,1024]{1,0:T(8,128)(2,1)S(1)}, bf16[256,1024]{1,0:T(8,128)(2,1)}, u32[]{:S(2)}, u32[]{:S(2)}) collective-permute-start(bf16[256,1024]{1,0:T(8,128)(2,1)S(1)} %fusion.20), channel_id=1, source_target_pairs={{0,16},{8,24},{16,0},{24,8},{1,17},{9,25},{17,1},{25,9},{2,18},{10... | collective-permute-start | bytes 1572872 | tf_op jit(solution)/shard_map/ppermute | solution.py:584
  469.6 44.4 %collective-permute-start.37 = (bf16[2,192,1024]{2,1,0:T(8,128)(2,1)}, bf16[2,192,1024]{2,1,0:T(8,128)(2,1)}, u32[]{:S(2)}, u32[]{:S(2)}) collective-permute-start(bf16[2,192,1024]{2,1,0:T(8,128)(2,1)} %get-tuple-element.100.refs_0_), channel_id=1, source_target_pairs={{0,8},{8,0},{16,24},{24,16},{1,9},{9,1},{17,25},{25,17},{2,10},{10... | collective-permute-start | bytes 2359304 | tf_op jit(solution)/shard_map/ppermute | solution.py:584
  472.1 38.8 %collective-permute-start.50 = (bf16[256,1024]{1,0:T(8,128)(2,1)}, bf16[256,1024]{1,0:T(8,128)(2,1)}, u32[]{:S(2)}, u32[]{:S(2)}) collective-permute-start(bf16[256,1024]{1,0:T(8,128)(2,1)} %add_convert_fusion.1), channel_id=1, source_target_pairs={{0,8},{8,0},{16,24},{24,16},{1,9},{9,1},{17,25},{25,17},{2,10},{10... | collective-permute-start | bytes 1572872 | tf_op jit(solution)/shard_map/ppermute | solution.py:584
  472.8 49.9 %collective-permute-start.52 = (bf16[2,256,1024]{2,1,0:T(8,128)(2,1)}, bf16[2,256,1024]{2,1,0:T(8,128)(2,1)}, u32[]{:S(2)}, u32[]{:S(2)}) collective-permute-start(bf16[2,256,1024]{2,1,0:T(8,128)(2,1)} %pad_maximum_fusion.7.first_own), channel_id=1, source_target_pairs={{0,8},{8,0},{16,24},{24,16},{1,9},{9,1},{17,25},{25,17},{2,10},{10... | collective-permute-start | bytes 3145736 | tf_op jit(solution)/shard_map/ppermute | solution.py:584
  493.8 31.6 %collective-permute-start.53 = (bf16[2,256,1024]{2,1,0:T(8,128)(2,1)}, bf16[2,256,1024]{2,1,0:T(8,128)(2,1)}, u32[]{:S(2)}, u32[]{:S(2)}) collective-permute-start(bf16[2,256,1024]{2,1,0:T(8,128)(2,1)} %pad_maximum_fusion.8.second_own), channel_id=1, source_target_pairs={{0,16},{8,24},{16,0},{24,8},{1,17},{9,25},{17,1},{25,9},{2,18},{10... | collective-permute-start | bytes 3145736 | tf_op jit(solution)/shard_map/ppermute | solution.py:584
  507.8 58.3 %collective-permute-start.48 = (bf16[2,256,1024]{2,1,0:T(8,128)(2,1)}, bf16[2,256,1024]{2,1,0:T(8,128)(2,1)S(1)}, u32[]{:S(2)}, u32[]{:S(2)}) collective-permute-start(bf16[2,256,1024]{2,1,0:T(8,128)(2,1)} %shard_map.245.first_own), channel_id=1, source_target_pairs={{0,8},{8,0},{16,24},{24,16},{1,9},{9,1},{17,25},{25,17},{2,10},{10... | collective-permute-start | bytes 3145736 | tf_op jit(solution)/shard_map/ppermute | solution.py:584
  510.9 34.0 %collective-permute-start.40 = (bf16[192,1024]{1,0:T(8,128)(2,1)}, bf16[192,1024]{1,0:T(8,128)(2,1)}, u32[]{:S(2)}, u32[]{:S(2)}) collective-permute-start(bf16[192,1024]{1,0:T(8,128)(2,1)} %fusion.34), channel_id=1, source_target_pairs={{0,8},{8,0},{16,24},{24,16},{1,9},{9,1},{17,25},{25,17},{2,10},{10... | collective-permute-start | bytes 1179656 | tf_op jit(solution)/shard_map/ppermute | solution.py:584
  514.0 52.2 %collective-permute-start.51 = (bf16[2,256,1024]{2,1,0:T(8,128)(2,1)}, bf16[2,256,1024]{2,1,0:T(8,128)(2,1)S(1)}, u32[]{:S(2)}, u32[]{:S(2)}) collective-permute-start(bf16[2,256,1024]{2,1,0:T(8,128)(2,1)} %shard_map.246.second_own), channel_id=1, source_target_pairs={{0,16},{8,24},{16,0},{24,8},{1,17},{9,25},{17,1},{25,9},{2,18},{10... | collective-permute-start | bytes 3145736 | tf_op jit(solution)/shard_map/ppermute | solution.py:584
  522.7 30.0 %collective-permute-start.38 = (bf16[192,1024]{1,0:T(8,128)(2,1)S(1)}, bf16[192,1024]{1,0:T(8,128)(2,1)}, u32[]{:S(2)}, u32[]{:S(2)}) collective-permute-start(bf16[192,1024]{1,0:T(8,128)(2,1)S(1)} %fusion.33), channel_id=1, source_target_pairs={{0,16},{8,24},{16,0},{24,8},{1,17},{9,25},{17,1},{25,9},{2,18},{10... | collective-permute-start | bytes 1179656 | tf_op jit(solution)/shard_map/ppermute | solution.py:584
  (114 other events, 1048.6 us)
Sparse Core Ops, SparseCore 0:
  10.5 67.4 all-gather.3
  80.2 63.3 all-gather.5
  153.5 62.4 all-gather.7
  279.5 66.6 reduce-scatter.5
  358.2 67.8 reduce-scatter.3
  472.2 72.1 reduce-scatter.7
